TPU v7x, 256 devices: a whole 4x4x8 slice. The times are simulated.
256 devices in a mesh: row: 32 (over y, z_lo, core), feat: 8 (over z_hi, x).
Axes of the slice: x: 4, y: 4, z: 8 (z_hi: 2, z_lo: 4; z = z_hi * 4 + z_lo), core: 2. Of those that a mesh axis runs over, the one named last changes fastest.
Arguments:
- node_feats: bfloat16 [512, 32768], P('feat', 'row'), may hold values from -6 to 6
- self_weight: float32 [32768], P('row'), may hold values from 0.2 to 1
- hub_ids: int32 [512], P('row'), may hold values from 0 to 1023
- hub_adjacency: bfloat16 [512, 32768], P(None, 'row'), may hold values from -0.25 to 0.25
- send_blocks: int32 [32, 32, 4], P('row'), may hold values from 0 to 7
- recv_counts: int32 [32, 32], P('row'), may hold values from 0 to 4, as said below
- recv_targets: int32 [32, 32, 4], P('row'), may hold values from 0 to 7
- recv_tiles: bfloat16 [32, 32, 4, 128, 128], P('row'), may hold values from -0.125 to 0.125
- weight: bfloat16 [512, 512], replicated, may hold values from -0.25 to 0.25
- grad_out: bfloat16 [512, 32768], P('feat', 'row'), may hold values from -6 to 6
Outputs:
- activation: bfloat16 [512, 32768], P('feat', 'row')
- grad_in: bfloat16 [512, 32768], P('feat', 'row')
Inputs may be any that keep to these rules, and one draw needn't show every extreme that they name: Reader d takes the first recv_counts[d, s] of the 4 slots from source s; some reader takes all 4 slots from every source. `send_blocks`: A block index within the source's nodes. `recv_targets`: A block index within the reader's nodes. `hub_ids`: A row within the owner's nodes; ids may repeat.
All inputs are finite; a program needn't handle non-finite values.
Results may differ from a plain program's by a relative error of at most 0.03.
Values may be sent and summed in bfloat16 or wider, within the bound.
No kernel may reach another device: no remote copies, remote signals or barrier semaphores. Data moves between devices by JAX's collectives and lax.ppermute only.
A program may use at most 64 MiB of HBM per device.

v0:
```python
import jax
import jax.numpy as jnp
from jax import lax
from jax.sharding import PartitionSpec as P

HIGH = lax.Precision.HIGHEST


def gelu_fn(values):
    return jax.nn.gelu(values, approximate=True)


def gelu_back(pre, upstream):
    _, pullback = jax.vjp(gelu_fn, pre)
    return pullback(upstream)[0]


def neighbour_swap(parts):
    return lax.all_to_all(parts, "row", split_axis=0, concat_axis=0, tiled=True)


def shards(
    node_feats,
    self_weight,
    hub_ids,
    hub_adjacency,
    send_blocks,
    recv_counts,
    recv_targets,
    recv_tiles,
    weight,
    grad_out,
):
    group_size, node_count = node_feats.shape
    block_len = recv_tiles.shape[-1]
    slot_count = recv_tiles.shape[2]
    cycle_size = recv_tiles.shape[1]
    num_blocks = node_count // block_len
    feats_wide = node_feats.astype(jnp.float32)
    weight_wide = weight.astype(jnp.float32)
    tiles_wide = recv_tiles[0].astype(jnp.float32)
    hub_feats = jnp.take(node_feats, hub_ids, axis=1)
    adj_rows = hub_adjacency.astype(jnp.float32)
    hub_part = jnp.dot(
        lax.all_gather(hub_feats, "row", axis=1, tiled=True).astype(jnp.float32),
        adj_rows,
        precision=HIGH,
    )
    block_ids = jnp.arange(num_blocks)[None, None, :]
    live_slots = (jnp.arange(slot_count)[None, :] < recv_counts[0][:, None]).astype(jnp.float32)
    place_into = (recv_targets[0][:, :, None] == block_ids).astype(jnp.float32) * live_slots[
        :, :, None
    ]
    block_rows = jnp.transpose(node_feats.reshape(group_size, num_blocks, block_len), (1, 0, 2))
    outgoing = jnp.take(block_rows, send_blocks[0].reshape(-1), axis=0).reshape(
        cycle_size, slot_count, group_size, block_len
    )
    incoming = neighbour_swap(outgoing)
    products = jnp.einsum(
        "skfi,skij->skfj", incoming.astype(jnp.float32), tiles_wide, precision=HIGH
    )
    rem_part = jnp.einsum("skfj,skb->fbj", products, place_into, precision=HIGH).reshape(
        group_size, node_count
    )
    aggregated = (self_weight[None, :] * feats_wide + hub_part + rem_part).astype(jnp.bfloat16)
    feat_group = lax.axis_index("feat")
    w_cols = lax.dynamic_slice_in_dim(weight_wide, feat_group * group_size, group_size, 1)
    w_part = w_cols
    pre = jnp.dot(
        w_part.T,
        lax.all_gather(aggregated, "feat", axis=0, tiled=True).astype(jnp.float32),
        precision=HIGH,
    )
    activation = gelu_fn(pre).astype(jnp.bfloat16)
    grad_pre = gelu_back(pre, grad_out.astype(jnp.float32)).astype(jnp.bfloat16)
    grad_pre_wide = grad_pre.astype(jnp.float32)
    w_part = w_cols
    grad_agg = lax.psum_scatter(
        jnp.dot(w_part, grad_pre_wide, precision=HIGH).astype(jnp.bfloat16),
        "feat",
        scatter_dimension=0,
        tiled=True,
    )
    grad_agg_wide = grad_agg.astype(jnp.float32)
    adj_rows = hub_adjacency.astype(jnp.float32)
    hub_grads = lax.psum_scatter(
        jnp.dot(adj_rows, grad_agg_wide.T, precision=HIGH).astype(jnp.bfloat16),
        "row",
        scatter_dimension=0,
        tiled=True,
    ).astype(jnp.float32)
    hub_pick = (hub_ids[:, None] == jnp.arange(node_count)[None, :]).astype(jnp.float32)
    hub_back = jnp.dot(hub_grads.T, hub_pick, precision=HIGH)
    grad_blocks = jnp.transpose(grad_agg_wide.reshape(group_size, num_blocks, block_len), (1, 0, 2))
    chosen = jnp.take(grad_blocks, recv_targets[0].reshape(-1), axis=0).reshape(
        cycle_size, slot_count, group_size, block_len
    )
    sent_grads = jnp.einsum("skfj,skij->skfi", chosen, tiles_wide, precision=HIGH)
    sent_grads = (sent_grads * live_slots[:, :, None, None]).astype(jnp.bfloat16)
    returned = neighbour_swap(sent_grads)
    place_from = (send_blocks[0][:, :, None] == block_ids).astype(jnp.float32)
    rem_back = jnp.einsum(
        "dkfi,dkb->fbi", returned.astype(jnp.float32), place_from, precision=HIGH
    ).reshape(group_size, node_count)
    grad_in = (self_weight[None, :] * grad_agg_wide + hub_back + rem_back).astype(jnp.bfloat16)
    return (activation, grad_in)


def solution(mesh):
    in_specs = (
        P("feat", "row"),
        P("row"),
        P("row"),
        P(None, "row"),
        P("row", None, None),
        P("row", None),
        P("row", None, None),
        P("row", None, None, None, None),
        P(),
        P("feat", "row"),
    )
    out_specs = (P("feat", "row"), P("feat", "row"))
    return jax.shard_map(shards, mesh=mesh, in_specs=in_specs, out_specs=out_specs, check_vma=False)
```

profile of v0, /device:TPU:2, one launch (start us, length us, event | category | flops | bytes accessed | tf_op | source)
XLA Modules:
  0.0 433.8 jit_solution(17970693772585047728)
XLA Ops:
  7.2 0.9 copy.46
  8.0 0.7 compare_and_fusion.1
  8.7 0.9 bitcast_bitcast_fusion.1
  9.6 0.1 reshape_squeeze.9
  9.8 0.1 copy.44
  9.9 0.9 gather_fusion.1
  10.9 1.6 broadcast_select_fusion
  12.5 8.9 %all-to-all-start = ((bf16[32,4,64,128]{3,2,1,0:T(8,128)(2,1)}), bf16[32,4,64,128]{3,2,1,0:T(8,128)(2,1)S(1)}, u32[]{:S(2)}, u32[]{:S(2)}) async-start(bf16[32,4,64,128]{3,2,1,0:T(8,128)(2,1)} %broadcast_select_fusion), calls=%async_computation | async-start | bytes 4194304 | tf_op jit(solution)/shard_map/all_to_all | solution.py:19
  21.5 0.8 copy.43
  22.3 1.6 gather_fusion
  24.0 76.8 %all_gather.6 = bf16[64,512]{0,1:T(8,128)(2,1)S(1)} all-gather(bf16[64,16]{0,1:T(8,128)(2,1)S(1)} %select_bitcast_fusion), channel_id=1, replica_groups=mesh['row'=32,'feat'=8] {'row'}, dimensions={1}, use_global_device_ids=true | all-gather | bytes 67584 | tf_op jit(solution)/shard_map/all_gather | solution.py:45
  100.8 3.4 fusion.2
  104.3 4.9 %fusion.4 = f32[8,64,128,1]{2,0,3,1:T(8,128)S(1)} fusion(f32[32,4,64,128]{3,2,1,0:T(8,128)S(1)} %fusion.2, f32[32,4]{0,1:T(4,128)S(1)} %fusion.49, s32[32,4]{0,1:T(4,128)S(1)} %bitcast.68), kind=kOutput, calls=%fused_computation.7 | convolution fusion | flops 100665344 | bytes 4457472 | tf_op jit(solution)/shard_map/skfj,skb->fbj/dot_general | solution.py:62
  109.2 1.0 fusion.18
  110.2 0.2 reduce-scatter.5.cloned.1.call-start
  110.4 59.1 %all-gather.2.cloned.1.call-done = bf16[512,1024]{1,0:T(8,128)(2,1)} async-done(((bf16[64,1024]{1,0:T(8,128)(2,1)}), bf16[512,1024]{1,0:T(8,128)(2,1)}) %all-gather.2.cloned.1.call-update) | async-done | bytes 1048592 | tf_op jit(solution)/shard_map/all_gather | solution.py:71
  169.5 2.3 multiply_convert_fusion.1
  171.9 1.5 convolution_convert_fusion
  173.4 0.1 copy.50
  173.6 0.1 reshape_squeeze.10
  173.7 0.1 copy.48
  173.8 82.0 %reduce-scatter.5.cloned.1.call-done = bf16[64,1024]{1,0:T(8,128)(2,1)} async-done(((bf16[512,1024]{1,0:T(8,128)(2,1)}), bf16[64,1024]{1,0:T(8,128)(2,1)}) %reduce-scatter.5.cloned.1.call-update) | async-done | bytes 131088 | tf_op jit(solution)/shard_map/reduce_scatter | solution.py:78
  255.8 0.9 bitcast_bitcast_fusion
  256.7 2.8 gather_fusion.2
  259.5 13.1 %multiply_convert_fusion = bf16[32,4,64,128]{3,2,1,0:T(8,128)(2,1)} fusion(f32[32,4]{1,0:T(8,128)S(1)} %copy.51, bf16[1,32,4,128,128]{4,3,2,1,0:T(8,128)(2,1)} %param.17, f32[32,4,64,128]{3,2,1,0:T(8,128)} %bitcast.64, pred[32,4]{1,0:T(8,128)(4,1)S(1)} %copy.48), kind=kOutput, calls=%fused_computation.9 | convolution fusion | flops 1613758464 | bytes 10486400 | tf_op jit(solution)/shard_map/skfj,skij->skfi/dot_general | solution.py:98
  272.6 5.4 %all-to-all-start.1 = ((bf16[32,4,64,128]{3,2,1,0:T(8,128)(2,1)}), bf16[32,4,64,128]{3,2,1,0:T(8,128)(2,1)S(1)}, u32[]{:S(2)}, u32[]{:S(2)}) async-start(bf16[32,4,64,128]{3,2,1,0:T(8,128)(2,1)} %multiply_convert_fusion), calls=%async_computation.2 | async-start | bytes 4194304 | tf_op jit(solution)/shard_map/all_to_all | solution.py:19
  278.0 0.4 fusion.19
  278.5 0.8 copy.55
  279.3 49.9 %all-to-all-done.1 = bf16[32,4,64,128]{3,2,1,0:T(8,128)(2,1)S(1)} async-done(((bf16[32,4,64,128]{3,2,1,0:T(8,128)(2,1)}), bf16[32,4,64,128]{3,2,1,0:T(8,128)(2,1)S(1)}, u32[]{:S(2)}, u32[]{:S(2)}) %all-to-all-start.1) | async-done | bytes 2097184 | tf_op jit(solution)/shard_map/all_to_all | solution.py:19
  329.1 1.2 fusion.7
  330.4 95.4 %reduce-scatter.7.cloned.1.call-done = bf16[16,64]{1,0:T(8,128)(2,1)} async-done(((bf16[512,64]{1,0:T(8,128)(2,1)}), bf16[16,64]{1,0:T(8,128)(2,1)}) %reduce-scatter.7.cloned.1.call-update) | async-done | bytes 2064
  425.7 1.6 fusion.17
  (37 shorter events, 0.4 us)
Async XLA Ops:
  7.2 102.0 %copy-start = (bf16[512,1024]{1,0:T(8,128)(2,1)S(1)}, bf16[512,1024]{1,0:T(8,128)(2,1)}, u32[]{:S(2)}) copy-start(bf16[512,1024]{1,0:T(8,128)(2,1)} %param.13) | copy-start | bytes 3145732
  10.8 10.6 %copy-start.2 = (bf16[64,1024]{1,0:T(8,128)(2,1)S(1)}, bf16[64,1024]{1,0:T(8,128)(2,1)}, u32[]{:S(2)}) copy-start(bf16[64,1024]{1,0:T(8,128)(2,1)} %param.10) | copy-start | bytes 393220
  10.9 11.5 %copy-start.7 = (s32[16]{0:T(128)S(1)}, s32[16]{0:T(128)}, u32[]{:S(2)}) copy-start(s32[16]{0:T(128)} %param.12) | copy-start | bytes 196
  10.9 89.9 %copy-start.8 = (s32[1,32]{1,0:T(1,128)S(1)}, s32[1,32]{1,0:T(1,128)}, u32[]{:S(2)}) copy-start(s32[1,32]{1,0:T(1,128)} %param.15) | copy-start | bytes 388
  12.5 88.3 %all-to-all-start = ((bf16[32,4,64,128]{3,2,1,0:T(8,128)(2,1)}), bf16[32,4,64,128]{3,2,1,0:T(8,128)(2,1)S(1)}, u32[]{:S(2)}, u32[]{:S(2)}) async-start(bf16[32,4,64,128]{3,2,1,0:T(8,128)(2,1)} %broadcast_select_fusion), calls=%async_computation | async-start | bytes 4194304 | tf_op jit(solution)/shard_map/all_to_all | solution.py:19
  21.4 148.1 %all-gather.2.cloned.1.call-start = ((), (), s32[]{:S(2)}) async-start(), calls=%async_computation.4 | async-start | bytes 1179648 | tf_op jit(solution)/shard_map/all_gather | solution.py:71
  100.8 3.5 copy-start.4
  104.2 4.9 %copy-start.6 = (f32[1024]{0:T(1024)S(1)}, f32[1024]{0:T(1024)}, u32[]{:S(2)}) copy-start(f32[1024]{0:T(1024)} %param.11) | copy-start | bytes 12292
  104.3 65.3 %copy-start.3 = (bf16[512,512]{1,0:T(8,128)(2,1)S(1)}, bf16[512,512]{1,0:T(8,128)(2,1)}, u32[]{:S(2)}) copy-start(bf16[512,512]{1,0:T(8,128)(2,1)} %param.18) | copy-start | bytes 1572868
  104.3 67.6 %copy-start.9 = (bf16[64,1024]{1,0:T(8,128)(2,1)S(1)}, bf16[64,1024]{1,0:T(8,128)(2,1)}, u32[]{:S(2)}) copy-start(bf16[64,1024]{1,0:T(8,128)(2,1)} %param.19) | copy-start | bytes 393220
  110.2 145.6 %reduce-scatter.5.cloned.1.call-start = ((), (), s32[]{:S(2)}) async-start(), calls=%async_computation.5 | async-start | bytes 1179648 | tf_op jit(solution)/shard_map/reduce_scatter | solution.py:78
  272.6 5.5 %copy-start.1 = (bf16[64,1024]{1,0:T(8,128)(2,1)S(1)}, bf16[64,1024]{1,0:T(8,128)(2,1)}, u32[]{:S(2)}) copy-start(bf16[64,1024]{1,0:T(8,128)(2,1)} %reduce-scatter.5.cloned.1.call-done) | copy-start | bytes 393220
  272.6 56.6 %copy-start.5 = (s32[1,32,4]{1,2,0:T(4,128)S(1)}, s32[1,32,4]{1,2,0:T(4,128)}, u32[]{:S(2)}) copy-start(s32[1,32,4]{1,2,0:T(4,128)} %param.14) | copy-start | bytes 1540
  272.6 56.6 %all-to-all-start.1 = ((bf16[32,4,64,128]{3,2,1,0:T(8,128)(2,1)}), bf16[32,4,64,128]{3,2,1,0:T(8,128)(2,1)S(1)}, u32[]{:S(2)}, u32[]{:S(2)}) async-start(bf16[32,4,64,128]{3,2,1,0:T(8,128)(2,1)} %multiply_convert_fusion), calls=%async_computation.2 | async-start | bytes 4194304 | tf_op jit(solution)/shard_map/all_to_all | solution.py:19
  278.0 147.7 %reduce-scatter.7.cloned.1.call-start = ((), (), s32[]{:S(2)}) async-start(), calls=%async_computation.6 | async-start | bytes 135168
Sparse Core Ops, SparseCore 0:
  110.3 59.1 all-gather.1
  173.5 82.2 reduce-scatter.4
  282.0 143.6 reduce-scatter.6
where the time goes:
time: 434 us
  waiting for transfers between devices  286 us (66%)
  blocking collectives  76.8 us (18%)
  matrix products  29.4 us (7%)
  starting transfers between devices  14.6 us (3%)
  between operations  13.9 us (3%)
  local copies, waits for them, and re-layouts  9.31 us (2%)
    unnamed x4, waiting for transfers between devices  95.4 us
    reduce_scatter x1, waiting for transfers between devices, shards(): lax.psum_scatter(jnp.dot(w_part, grad_pre_wide, precision=HIGH).astype(jn...  82 us
    all_gather x1, blocking collectives, shards(): lax.all_gather(hub_feats, 'row', axis=1, tiled=True).astype(jnp.float32)  76.8 us
    all_gather x1, waiting for transfers between devices, shards(): lax.all_gather(aggregated, 'feat', axis=0, tiled=True).astype(jnp.float32)  59.1 us
    all_to_all x2, waiting for transfers between devices, neighbour_swap(): return lax.all_to_all(parts, 'row', split_axis=0, concat_axis=0, tiled=True)  49.9 us
    all_to_all x2, starting transfers between devices, neighbour_swap(): return lax.all_to_all(parts, 'row', split_axis=0, concat_axis=0, tiled=True)  14.3 us
    dot_general x1, matrix products, shards(): jnp.einsum('skfj,skij->skfi', chosen, tiles_wide, precision=HIGH)  13.1 us
  transfers between devices with their start and end apart: 5, of which 4 were waited for; matrix products, arithmetic and copies ran while one was open for 1% of the time, Pallas kernels for 0%

commit v1 on v0

v1 whole, which is shorter than its diff:
```python
import functools

import jax
import jax.numpy as jnp
from jax import lax
from jax.experimental import pallas as pl
from jax.experimental.pallas import tpu as pltpu
from jax.sharding import PartitionSpec as P

BF = jnp.bfloat16
F32 = jnp.float32
VM = pl.BlockSpec(memory_space=pltpu.VMEM)
SM = pl.BlockSpec(memory_space=pltpu.SMEM)
MIB = 1 << 20
STEPS = (0, 1, 3, 2)
BACK = (0, 2, 1, 3)
NY, NZ, NC = 4, 4, 2
LIVE = 33


def row_perm(dy, dz, dc):
    pairs = []
    for y in range(NY):
        for z in range(NZ):
            for c in range(NC):
                to = (((y + dy) % NY) * NZ + (z + dz) % NZ) * NC + (c + dc) % NC
                pairs.append(((y * NZ + z) * NC + c, to))
    return pairs


def feat_perm(dh, dx):
    return [(h * 4 + x, ((h + dh) % 2) * 4 + (x + dx) % 4) for h in range(2) for x in range(4)]


def row_send(value, dy, dz, dc):
    return lax.ppermute(value, "row", row_perm(dy, dz, dc))


def feat_gather(value):
    across = lax.ppermute(value, "feat", feat_perm(1, 0))
    near = [lax.ppermute(value, "feat", feat_perm(0, k)) for k in STEPS[1:]]
    far = [lax.ppermute(across, "feat", feat_perm(0, k)) for k in STEPS[1:]]
    return [value, *near, across, *far]


def dot(a, b):
    return jnp.dot(a, b, preferred_element_type=F32)


def dot_nt(a, b):
    return lax.dot_general(a, b, (((1,), (1,)), ((), ())), preferred_element_type=F32)


def prep_kernel(me_ref, x_ref, ids_ref, sb_ref, out_ref):
    me = me_ref[0]
    window = lax.rem(me, 8)
    other = window + 1 - 2 * lax.rem(me, 2)
    for b in range(8):
        out_ref[b] = x_ref[:, b * 128 : (b + 1) * 128]
    rows = lax.broadcasted_iota(jnp.int32, (1024, 16), 0)
    pick = (rows == ids_ref[...]).astype(F32).astype(BF)
    hubs = dot(x_ref[...], pick).astype(BF)
    lane = lax.broadcasted_iota(jnp.int32, (16, 128), 1)
    which = lax.broadcasted_iota(jnp.int32, (16, 128), 0)
    place = (lane == window * 16 + which).astype(F32).astype(BF)
    extra = dot(hubs, place)
    lanes = lax.broadcasted_iota(jnp.int32, (32, 128), 1)
    ids = jnp.zeros((32, 128), F32)
    sb = sb_ref[...].astype(F32)
    for k in range(4):
        ids = ids + jnp.where(lanes == other * 16 + k, sb[:, k : k + 1], 0.0)
    out_ref[8, 0:32, :] = (extra[0:32] + ids).astype(BF)
    out_ref[8, 32:64, :] = extra[32:64].astype(BF)


def stack_kernel(p0, p1, p2, p3, out_ref):
    extra = jnp.zeros((64, 128), F32)
    for i, p in enumerate((p0, p1, p2, p3)):
        out_ref[i * 8 : (i + 1) * 8] = p[0:8]
        extra = extra + p[8].astype(F32)
    out_ref[32] = extra.astype(BF)


def place_of(me):
    return lax.div(me, 8), lax.rem(lax.div(me, 2), 4), lax.rem(me, 2)


def agg_kernel(
    me_ref, cnt_ref, tgt_ref, *rest
):
    srcs = rest[:8]
    tiles_ref, adj_ref, x_ref, self_ref, out_ref, sb_ref, acc, ids_v, ids_s, sem = rest[8:]
    me = me_ref[0]
    y, z, c = place_of(me)
    row = lax.broadcasted_iota(jnp.int32, (64, 128), 0)
    for a in range(8):
        here = jnp.where(row == me, srcs[a][32].astype(F32), 0.0)
        ids_v[a : a + 1, :] = jnp.sum(here, axis=0, keepdims=True).astype(jnp.int32)
    copy = pltpu.make_async_copy(ids_v, ids_s, sem)
    copy.start()
    acc[...] = jnp.zeros_like(acc)
    lane = lax.broadcasted_iota(jnp.int32, (64, 128), 1)
    parity = lax.rem(lax.div(lane, 16), 2)
    hub = jnp.zeros((64, 1024), F32)
    for j in range(4):
        sy = lax.rem(y - STEPS[j] + 4, 4)
        both = jnp.where(parity == c, srcs[j][32].astype(F32), srcs[4 + j][32].astype(F32)).astype(BF)
        hub = hub + dot(both, adj_ref[pl.ds(pl.multiple_of(sy * 128, 128), 128), :])
    copy.wait()
    for a in range(8):
        for i in range(8):
            sb_ref[a, i] = 0
    for a in range(8):
        j = a % 4
        cc = c if a < 4 else 1 - c
        sy = lax.rem(y - STEPS[j] + 4, 4)
        src = srcs[a]
        for i in range(4):
            sz = lax.rem(z - STEPS[i] + 4, 4)
            s = (sy * 4 + sz) * 2 + cc
            count = cnt_ref[s]
            parts = []
            for k in range(4):
                b = ids_s[a, (sz * 2 + 1 - cc) * 16 + k]
                sb_ref[s // 4, lax.rem(s, 4) * 4 + k] = b
                parts.append(dot(src[i * 8 + b], tiles_ref[s, k]))
            for k in range(4):
                t = jnp.where(k < count, tgt_ref[s, k], 8)
                acc[t] += parts[k]
    for b in range(8):
        cols = slice(b * 128, (b + 1) * 128)
        total = x_ref[:, cols].astype(F32) * self_ref[:, cols] + hub[:, cols] + acc[b]
        out_ref[:, cols] = total.astype(BF)


def mid_kernel(group_ref, *rest):
    aggs = rest[:8]
    ups = rest[8:16]
    wt_ref, w_ref, act_ref, ga_ref, full, pre, down = rest[16:]
    group = group_ref[0]
    h, x = lax.div(group, 4), lax.rem(group, 4)
    first = []
    for j in range(8):
        hh = h if j < 4 else 1 - h
        xx = lax.rem(x - STEPS[j % 4] + 4, 4)
        first.append(pl.multiple_of((hh * 4 + xx) * 64, 64))
    for j in range(8):
        full[pl.ds(first[j], 64), :] = aggs[j][...]
    own = w_ref[pl.ds(first[0], 64), :]
    for n in range(4):
        cols = slice(n * 256, (n + 1) * 256)
        pre[...] = dot(wt_ref[...], full[:, cols])
        for j in range(8):
            v = pre[pl.ds(first[j], 64), :]
            sq = v * v
            t = jnp.tanh(v * (0.7978845608 + (0.7978845608 * 0.044715) * sq))
            half = 0.5 + 0.5 * t
            if j == 0:
                act_ref[:, cols] = (v * half).astype(BF)
            slope = half + (0.5 * v) * (1.0 - t * t) * (
                0.7978845608 + (0.7978845608 * 3 * 0.044715) * sq
            )
            down[pl.ds(first[j], 64), :] = (ups[j][:, cols].astype(F32) * slope).astype(BF)
        grads = dot(own, down[...]).astype(BF)
        ga_ref[2 * n] = grads[:, :128]
        ga_ref[2 * n + 1] = grads[:, 128:]


def back_kernel(swap, me_ref, cnt_ref, tgt_ref, sb_ref, ga_ref, tiles_ref, adj_ref, o0, o1, o2, o3, acc):
    me = me_ref[0]
    y, z, c = place_of(me)
    cc = 1 - c if swap else c
    for j, out in enumerate((o0, o1, o2, o3)):
        sy = lax.rem(y + STEPS[j], 4)
        for i in range(4):
            sz = lax.rem(z + STEPS[i], 4)
            s = (sy * 4 + sz) * 2 + cc
            count = cnt_ref[s]
            acc[0:8] = jnp.zeros((8, 64, 128), F32)
            parts = [dot_nt(ga_ref[tgt_ref[s, k]], tiles_ref[s, k]) for k in range(4)]
            for k in range(4):
                b = jnp.where(k < count, sb_ref[s // 4, lax.rem(s, 4) * 4 + k], 8)
                acc[b] += parts[k]
            out[i * 8 : (i + 1) * 8] = acc[0:8].astype(BF)
        hubs = jnp.zeros((64, 128), F32)
        at = pl.ds(pl.multiple_of(sy * 128, 128), 128)
        for b in range(8):
            hubs = hubs + dot_nt(ga_ref[b], adj_ref[at, b * 128 : (b + 1) * 128])
        out[32] = hubs.astype(BF)


def sum_kernel(p0, p1, p2, p3, z0, z1, z2, z3):
    for i, out in enumerate((z0, z1, z2, z3)):
        for b in range(8):
            r = i * 8 + b
            out[b] = (p0[r].astype(F32) + p1[r].astype(F32) + p2[r].astype(F32) + p3[r].astype(F32)).astype(BF)
    extra = (p0[32].astype(F32) + p1[32].astype(F32) + p2[32].astype(F32) + p3[32].astype(F32)).astype(BF)
    for out in (z0, z1, z2, z3):
        out[8] = extra


def last_kernel(me_ref, z0, z1, z2, z3, ga_ref, self_ref, ids_ref, out_ref):
    window = lax.rem(me_ref[0], 8)

    def total(b):
        return z0[b].astype(F32) + z1[b].astype(F32) + z2[b].astype(F32) + z3[b].astype(F32)

    def halves(v):
        high = v.astype(BF)
        return high, (v - high.astype(F32)).astype(BF)

    lane = lax.broadcasted_iota(jnp.int32, (128, 16), 0)
    which = lax.broadcasted_iota(jnp.int32, (128, 16), 1)
    take = (lane == window * 16 + which).astype(F32).astype(BF)
    high, low = halves(total(8))
    high, low = halves(dot(high, take) + dot(low, take))
    node = lax.broadcasted_iota(jnp.int32, (16, 1024), 1)
    spread = (node == ids_ref[...]).astype(F32).astype(BF)
    hubs = dot(high, spread) + dot(low, spread)
    for b in range(8):
        cols = slice(b * 128, (b + 1) * 128)
        out_ref[:, cols] = (ga_ref[b].astype(F32) * self_ref[:, cols] + hubs[:, cols] + total(b)).astype(BF)


def call(kernel, name, outs, in_specs, args, scratch=(), limit=32, out_specs=None, flops=0, size=0):
    shapes = [jax.ShapeDtypeStruct(s, d) for s, d in outs]
    return pl.pallas_call(
        kernel,
        out_shape=shapes,
        in_specs=in_specs,
        out_specs=out_specs or [VM] * len(shapes),
        scratch_shapes=list(scratch),
        compiler_params=pltpu.CompilerParams(vmem_limit_bytes=limit * MIB),
        cost_estimate=pl.CostEstimate(flops=flops, bytes_accessed=size, transcendentals=0),
        name=name,
    )(*args)


def shards(
    node_feats,
    self_weight,
    hub_ids,
    hub_adjacency,
    send_blocks,
    recv_counts,
    recv_targets,
    recv_tiles,
    weight,
    grad_out,
):
    me = lax.axis_index("row").astype(jnp.int32).reshape(1)
    group = lax.axis_index("feat").astype(jnp.int32).reshape(1)
    counts = recv_counts.reshape(32)
    targets = recv_targets.reshape(32, 4)
    tiles = recv_tiles.reshape(32, 4, 128, 128)
    self_row = self_weight.reshape(1, 1024)
    part = ((9, 64, 128), BF)
    wide = ((LIVE, 64, 128), BF)

    (p0,) = call(
        prep_kernel, "prep", [part], [SM, VM, VM, VM],
        (me, node_feats, hub_ids.reshape(1, 16), send_blocks.reshape(32, 4)),
    )
    ps = [p0] + [row_send(p0, 0, k, 0) for k in STEPS[1:]]
    (a0,) = call(stack_kernel, "stack", [wide], [VM] * 4, ps)
    a0, grad_late = lax.optimization_barrier((a0, grad_out))
    own = [a0] + [row_send(a0, k, 0, 0) for k in STEPS[1:]]
    ups = feat_gather(grad_late)
    sibling = [row_send(a, 0, 0, 1) for a in own]
    agg, sb = call(
        agg_kernel, "aggregate",
        [((64, 1024), BF), ((8, 16), jnp.int32)],
        [SM] * 3 + [VM] * 12,
        (me, counts, targets, *own, *sibling, tiles, hub_adjacency, node_feats, self_row),
        scratch=[
            pltpu.VMEM((9, 64, 128), F32),
            pltpu.VMEM((8, 128), jnp.int32),
            pltpu.SMEM((8, 128), jnp.int32),
            pltpu.SemaphoreType.DMA,
        ],
        out_specs=[VM, SM],
    )
    aggs = feat_gather(agg)
    act, ga = call(
        mid_kernel, "middle",
        [((64, 1024), BF), ((8, 64, 128), BF)],
        [SM] + [VM] * 18,
        (group, *aggs, *ups, weight.T, weight),
        scratch=[
            pltpu.VMEM((512, 1024), BF),
            pltpu.VMEM((512, 256), F32),
            pltpu.VMEM((512, 256), BF),
        ],
    )
    back_args = (me, counts, targets, sb, ga, tiles, hub_adjacency)
    outs = []
    for swap in (True, False):
        outs.append(
            call(
                functools.partial(back_kernel, swap), "back_swap" if swap else "back_own",
                [wide] * 4, [SM] * 4 + [VM] * 3, back_args,
                scratch=[pltpu.VMEM((9, 64, 128), F32)],
            )
        )
    came = [row_send(v, 0, 0, 1) for v in outs[0]]
    both = [(a.astype(F32) + b.astype(F32)).astype(BF) for a, b in zip(outs[1], came)]
    ys = [both[0]] + [row_send(both[j], STEPS[j], 0, 0) for j in (1, 2, 3)]
    zs = call(sum_kernel, "sum_y", [part] * 4, [VM] * 4, ys)
    zs = [zs[0]] + [row_send(zs[i], 0, STEPS[i], 0) for i in (1, 2, 3)]
    (grad_in,) = call(
        last_kernel, "last", [((64, 1024), BF)], [SM] + [VM] * 7,
        (me, *zs, ga, self_row, hub_ids.reshape(16, 1)),
    )
    return (act, grad_in)


def solution(mesh):
    in_specs = (
        P("feat", "row"),
        P("row"),
        P("row"),
        P(None, "row"),
        P("row", None, None),
        P("row", None),
        P("row", None, None),
        P("row", None, None, None, None),
        P(),
        P("feat", "row"),
    )
    out_specs = (P("feat", "row"), P("feat", "row"))
    return jax.shard_map(shards, mesh=mesh, in_specs=in_specs, out_specs=out_specs, check_vma=False)
```

time: 434 us -> 161 us (0.37)
  waiting for transfers between devices: 286 us -> 82.8 us
  blocking collectives: 76.8 us -> 0 us
  matrix products: 29.4 us -> 0 us
  starting transfers between devices: 14.6 us -> 43.6 us
  Pallas kernels: 0 us -> 17.6 us
  between operations: 13.9 us -> 0.86 us
  local copies, waits for them, and re-layouts: 9.31 us -> 13.7 us
    unnamed x4 -> x0, waiting for transfers between devices: 95.4 us -> none
    ppermute x0 -> x34, waiting for transfers between devices: none -> 82.8 us  [the longest x20 69 us: row_send(): return lax.ppermute(value, 'row', row_perm(dy, dz, dc))]
    reduce_scatter x1 -> x0, waiting for transfers between devices: 82 us -> none  [shards(): lax.psum_scatter(jnp.dot(w_part, grad_pre_wide, precision=HIGH).astype(jn...]
    all_gather x1 -> x0, blocking collectives: 76.8 us -> none  [shards(): lax.all_gather(hub_feats, 'row', axis=1, tiled=True).astype(jnp.float32)]
    all_gather x1 -> x0, waiting for transfers between devices: 59.1 us -> none  [shards(): lax.all_gather(aggregated, 'feat', axis=0, tiled=True).astype(jnp.float32)]
    all_to_all x2 -> x0, waiting for transfers between devices: 49.9 us -> none  [neighbour_swap(): return lax.all_to_all(parts, 'row', split_axis=0, concat_axis=0, tiled=True)]
    ppermute x0 -> x34, starting transfers between devices: none -> 43.6 us  [the longest x20 19.4 us: row_send(): return lax.ppermute(value, 'row', row_perm(dy, dz, dc))]
    dot_general x9 -> x0, matrix products: 29.4 us -> none  [the longest x1 13.1 us: shards(): jnp.einsum('skfj,skij->skfi', chosen, tiles_wide, precision=HIGH)]
  transfers between devices with their start and end apart: 5 -> 34, of which waited for: 4 -> 14; matrix products, arithmetic and copies ran while one was open for 1% -> 1% of each run, Pallas kernels for 0% -> 5%
where the time goes in v1:
time: 161 us; the launch traced here: 159 us
  waiting for transfers between devices  82.8 us (51%)
  starting transfers between devices  43.6 us (27%)
  Pallas kernels  17.6 us (11%)
  local copies, waits for them, and re-layouts  13.7 us (9%)
    ppermute x20, waiting for transfers between devices, row_send(): return lax.ppermute(value, 'row', row_perm(dy, dz, dc))  69 us
    ppermute x20, starting transfers between devices, row_send(): return lax.ppermute(value, 'row', row_perm(dy, dz, dc))  19.4 us
    pallas_call x8, Pallas kernels, call(): pl.pallas_call(kernel, out_shape=shapes, in_specs=in_specs, out_specs=out...  17.6 us
    unnamed x45, local copies, waits for them, and re-layouts  12.7 us
    ppermute x6, starting transfers between devices, feat_gather(): far = [lax.ppermute(across, 'feat', feat_perm(0, k)) for k in STEPS[1:]]  8.51 us
    ppermute x6, starting transfers between devices, feat_gather(): near = [lax.ppermute(value, 'feat', feat_perm(0, k)) for k in STEPS[1:]]  8.22 us
    ppermute x2, waiting for transfers between devices, feat_gather(): across = lax.ppermute(value, 'feat', feat_perm(1, 0))  7.9 us
    ppermute x2, starting transfers between devices, feat_gather(): across = lax.ppermute(value, 'feat', feat_perm(1, 0))  7.47 us
  transfers between devices with their start and end apart: 34, of which 14 were waited for; matrix products, arithmetic and copies ran while one was open for 1% of the time, Pallas kernels for 5%

profile of v1, /device:TPU:2, one launch (start us, length us, event | category | flops | bytes accessed | tf_op | source)
XLA Modules:
  0.0 159.4 jit_solution(12550690769294812223)
XLA Ops:
  3.4 1.9 %collective-permute-start = (bf16[9,64,128]{2,1,0:T(8,128)(2,1)S(1)}, bf16[9,64,128]{2,1,0:T(8,128)(2,1)S(1)}, u32[]{:S(2)}, u32[]{:S(2)}) collective-permute-start(bf16[9,64,128]{2,1,0:T(8,128)(2,1)S(1)} %prep.1.p0), channel_id=1, source_target_pairs={{0,16},{8,24},{16,32},{24,40},{32,48},{40,56},{48,0},{56,8},{64,80... | collective-permute-start | bytes 442376 | tf_op jit(solution)/shard_map/ppermute | solution.py:36
  5.3 2.8 %collective-permute-start.1 = (bf16[9,64,128]{2,1,0:T(8,128)(2,1)S(1)}, bf16[9,64,128]{2,1,0:T(8,128)(2,1)S(1)}, u32[]{:S(2)}, u32[]{:S(2)}) collective-permute-start(bf16[9,64,128]{2,1,0:T(8,128)(2,1)S(1)} %prep.1.p0), channel_id=1, source_target_pairs={{0,48},{8,56},{16,0},{24,8},{32,16},{40,24},{48,32},{56,40},{64,11... | collective-permute-start | bytes 442376 | tf_op jit(solution)/shard_map/ppermute | solution.py:36
  8.7 4.0 %collective-permute-done.p1 = bf16[9,64,128]{2,1,0:T(8,128)(2,1)S(1)} collective-permute-done((bf16[9,64,128]{2,1,0:T(8,128)(2,1)S(1)}, bf16[9,64,128]{2,1,0:T(8,128)(2,1)S(1)}, u32[]{:S(2)}, u32[]{:S(2)}) %collective-permute-start) | collective-permute-done | bytes 147488 | tf_op jit(solution)/shard_map/ppermute | solution.py:36
  14.0 7.4 %collective-permute-done.2.p3 = bf16[9,64,128]{2,1,0:T(8,128)(2,1)S(1)} collective-permute-done((bf16[9,64,128]{2,1,0:T(8,128)(2,1)S(1)}, bf16[9,64,128]{2,1,0:T(8,128)(2,1)S(1)}, u32[]{:S(2)}, u32[]{:S(2)}) %collective-permute-start.2) | collective-permute-done | bytes 147488 | tf_op jit(solution)/shard_map/ppermute | solution.py:36
  21.4 1.7 %collective-permute-start.3 = (bf16[33,64,128]{2,1,0:T(8,128)(2,1)S(1)}, bf16[33,64,128]{2,1,0:T(8,128)(2,1)S(1)}, u32[]{:S(2)}, u32[]{:S(2)}) collective-permute-start(bf16[33,64,128]{2,1,0:T(8,128)(2,1)S(1)} %stack.1.rest_0_), channel_id=1, source_target_pairs={{0,64},{8,72},{16,80},{24,88},{32,96},{40,104},{48,112},{56,120},{... | collective-permute-start | bytes 1622024 | tf_op jit(solution)/shard_map/ppermute | solution.py:36
  23.1 1.7 %collective-permute-start.4 = (bf16[33,64,128]{2,1,0:T(8,128)(2,1)S(1)}, bf16[33,64,128]{2,1,0:T(8,128)(2,1)S(1)}, u32[]{:S(2)}, u32[]{:S(2)}) collective-permute-start(bf16[33,64,128]{2,1,0:T(8,128)(2,1)S(1)} %stack.1.rest_0_), channel_id=1, source_target_pairs={{0,192},{8,200},{16,208},{24,216},{32,224},{40,232},{48,240},{56,2... | collective-permute-start | bytes 1622024 | tf_op jit(solution)/shard_map/ppermute | solution.py:36
  24.7 2.0 %collective-permute-start.5 = (bf16[33,64,128]{2,1,0:T(8,128)(2,1)S(1)}, bf16[33,64,128]{2,1,0:T(8,128)(2,1)}, u32[]{:S(2)}, u32[]{:S(2)}) collective-permute-start(bf16[33,64,128]{2,1,0:T(8,128)(2,1)S(1)} %stack.1.rest_0_), channel_id=1, source_target_pairs={{0,128},{8,136},{16,144},{24,152},{32,160},{40,168},{48,176},{56,1... | collective-permute-start | bytes 1622024 | tf_op jit(solution)/shard_map/ppermute | solution.py:36
  26.7 10.2 %collective-permute-done.3.rest_1_ = bf16[33,64,128]{2,1,0:T(8,128)(2,1)S(1)} collective-permute-done((bf16[33,64,128]{2,1,0:T(8,128)(2,1)S(1)}, bf16[33,64,128]{2,1,0:T(8,128)(2,1)S(1)}, u32[]{:S(2)}, u32[]{:S(2)}) %collective-permute-start.3) | collective-permute-done | bytes 540704 | tf_op jit(solution)/shard_map/ppermute | solution.py:36
  37.0 11.0 %collective-permute-done.4.rest_2_ = bf16[33,64,128]{2,1,0:T(8,128)(2,1)S(1)} collective-permute-done((bf16[33,64,128]{2,1,0:T(8,128)(2,1)S(1)}, bf16[33,64,128]{2,1,0:T(8,128)(2,1)S(1)}, u32[]{:S(2)}, u32[]{:S(2)}) %collective-permute-start.4) | collective-permute-done | bytes 540704 | tf_op jit(solution)/shard_map/ppermute | solution.py:36
  47.9 1.9 %collective-permute-done.5.rest_3_ = bf16[33,64,128]{2,1,0:T(8,128)(2,1)} collective-permute-done((bf16[33,64,128]{2,1,0:T(8,128)(2,1)S(1)}, bf16[33,64,128]{2,1,0:T(8,128)(2,1)}, u32[]{:S(2)}, u32[]{:S(2)}) %collective-permute-start.5) | collective-permute-done | bytes 540704 | tf_op jit(solution)/shard_map/ppermute | solution.py:36
  49.8 4.8 %collective-permute-start.20 = (bf16[64,1024]{1,0:T(8,128)(2,1)S(1)}, bf16[64,1024]{1,0:T(8,128)(2,1)}, u32[]{:S(2)}, u32[]{:S(2)}) collective-permute-start(bf16[64,1024]{1,0:T(8,128)(2,1)S(1)} %copy-done.10), channel_id=1, source_target_pairs={{0,4},{1,5},{2,6},{3,7},{4,0},{5,1},{6,2},{7,3},{8,12},{9,13},{10,... | collective-permute-start | bytes 393224 | tf_op jit(solution)/shard_map/ppermute | solution.py:40
  54.7 7.9 %collective-permute-done.20.rest_12_ = bf16[64,1024]{1,0:T(8,128)(2,1)} collective-permute-done((bf16[64,1024]{1,0:T(8,128)(2,1)S(1)}, bf16[64,1024]{1,0:T(8,128)(2,1)}, u32[]{:S(2)}, u32[]{:S(2)}) %collective-permute-start.20) | collective-permute-done | bytes 131104 | tf_op jit(solution)/shard_map/ppermute | solution.py:40
  62.6 1.5 collective-permute-start.17
  66.2 2.1 %collective-permute-start.19 = (bf16[64,1024]{1,0:T(8,128)(2,1)S(1)}, bf16[64,1024]{1,0:T(8,128)(2,1)}, u32[]{:S(2)}, u32[]{:S(2)}) collective-permute-start(bf16[64,1024]{1,0:T(8,128)(2,1)S(1)} %copy-done.10), channel_id=1, source_target_pairs={{0,2},{1,3},{2,0},{3,1},{4,6},{5,7},{6,4},{7,5},{8,10},{9,11},{10,... | collective-permute-start | bytes 393224 | tf_op jit(solution)/shard_map/ppermute | solution.py:41
  70.5 2.2 %copy-done = bf16[1,32,4,128,128]{4,3,2,1,0:T(8,128)(2,1)S(1)} copy-done((bf16[1,32,4,128,128]{4,3,2,1,0:T(8,128)(2,1)S(1)}, bf16[1,32,4,128,128]{4,3,2,1,0:T(8,128)(2,1)}, u32[]{:S(2)}) %copy-start) | copy-done | bytes 4194328
  74.8 4.5 %aggregate.1 = (bf16[64,1024]{1,0:T(8,128)(2,1)}, s32[8,16]{1,0:T(8,128)S(1)}) custom-call(s32[1]{0:T(128)} %bitcast.1.me_ref, s32[32]{0:T(128)S(1)} %bitcast.16, s32[32,4]{1,0:T(8,128)S(1)} %copy.13.tgt_ref, bf16[33,64,128]{2,1,0:T(8,128)(2,1)S(1)} %stack.1.rest_0_, bf16[33,64,128]{2,1,0:T(8,128)(2,1)S(1)} %collective-permute-done.3.rest_1_, ...), custom_call_target="tpu_custom_call" | custom-call | tf_op jit(solution)/shard_map/aggregate/pallas_call | solution.py:227
  79.3 2.6 %collective-permute-start.13 = (bf16[64,1024]{1,0:T(8,128)(2,1)}, bf16[64,1024]{1,0:T(8,128)(2,1)S(1)}, u32[]{:S(2)}, u32[]{:S(2)}) collective-permute-start(bf16[64,1024]{1,0:T(8,128)(2,1)} %get-tuple-element.21.rest_0_), channel_id=1, source_target_pairs={{0,4},{1,5},{2,6},{3,7},{4,0},{5,1},{6,2},{7,3},{8,12},{9,13},{10,... | collective-permute-start | bytes 393224 | tf_op jit(solution)/shard_map/ppermute | solution.py:40
  82.0 1.5 collective-permute-start.23
  83.5 2.6 %collective-permute-start.10 = (bf16[64,1024]{1,0:T(8,128)(2,1)}, bf16[64,1024]{1,0:T(8,128)(2,1)S(1)}, u32[]{:S(2)}, u32[]{:S(2)}) collective-permute-start(bf16[64,1024]{1,0:T(8,128)(2,1)} %get-tuple-element.21.rest_0_), channel_id=1, source_target_pairs={{0,1},{1,2},{2,3},{3,0},{4,5},{5,6},{6,7},{7,4},{8,9},{9,10},{10,1... | collective-permute-start | bytes 393224 | tf_op jit(solution)/shard_map/ppermute | solution.py:41
  88.9 2.3 %collective-permute-start.14 = (bf16[64,1024]{1,0:T(8,128)(2,1)S(1)}, bf16[64,1024]{1,0:T(8,128)(2,1)S(1)}, u32[]{:S(2)}, u32[]{:S(2)}) collective-permute-start(bf16[64,1024]{1,0:T(8,128)(2,1)S(1)} %collective-permute-done.13.rest_4_), channel_id=1, source_target_pairs={{0,1},{1,2},{2,3},{3,0},{4,5},{5,6},{6,7},{7,4},{8,9},{9,10},{10,1... | collective-permute-start | bytes 393224 | tf_op jit(solution)/shard_map/ppermute | solution.py:42
  91.7 2.1 %collective-permute-start.16 = (bf16[64,1024]{1,0:T(8,128)(2,1)S(1)}, bf16[64,1024]{1,0:T(8,128)(2,1)}, u32[]{:S(2)}, u32[]{:S(2)}) collective-permute-start(bf16[64,1024]{1,0:T(8,128)(2,1)S(1)} %collective-permute-done.13.rest_4_), channel_id=1, source_target_pairs={{0,2},{1,3},{2,0},{3,1},{4,6},{5,7},{6,4},{7,5},{8,10},{9,11},{10,... | collective-permute-start | bytes 393224 | tf_op jit(solution)/shard_map/ppermute | solution.py:42
  94.1 1.8 %collective-permute-done.11.rest_2_ = bf16[64,1024]{1,0:T(8,128)(2,1)S(1)} collective-permute-done((bf16[64,1024]{1,0:T(8,128)(2,1)}, bf16[64,1024]{1,0:T(8,128)(2,1)S(1)}, u32[]{:S(2)}, u32[]{:S(2)}) %collective-permute-start.11) | collective-permute-done | bytes 131104 | tf_op jit(solution)/shard_map/ppermute | solution.py:41
  97.0 2.9 %collective-permute-done.15.rest_6_ = bf16[64,1024]{1,0:T(8,128)(2,1)S(1)} collective-permute-done((bf16[64,1024]{1,0:T(8,128)(2,1)S(1)}, bf16[64,1024]{1,0:T(8,128)(2,1)S(1)}, u32[]{:S(2)}, u32[]{:S(2)}) %collective-permute-start.15) | collective-permute-done | bytes 131104 | tf_op jit(solution)/shard_map/ppermute | solution.py:42
  101.5 5.3 %middle.1 = (bf16[64,1024]{1,0:T(8,128)(2,1)}, bf16[8,64,128]{2,1,0:T(8,128)(2,1)S(1)}) custom-call(s32[1]{0:T(128)} %bitcast.group_ref, bf16[64,1024]{1,0:T(8,128)(2,1)} %get-tuple-element.21.rest_0_, bf16[64,1024]{1,0:T(8,128)(2,1)S(1)} %collective-permute-done.10.rest_1_, bf16[64,1024]{1,0:T(8,128)(2,1)S(1)} %collective-permute-done.11.rest_2_, ...), custom_call_target="tpu_custom_call" | custom-call | tf_op jit(solution)/shard_map/middle/pallas_call | solution.py:227
  106.8 2.2 %copy-done.1 = bf16[1,32,4,128,128]{4,3,2,1,0:T(8,128)(2,1)S(1)} copy-done((bf16[1,32,4,128,128]{4,3,2,1,0:T(8,128)(2,1)S(1)}, bf16[1,32,4,128,128]{4,3,2,1,0:T(8,128)(2,1)}, u32[]{:S(2)}) %copy-start.1) | copy-done | bytes 4194328
  109.0 3.1 %back_swap.1 = (bf16[33,64,128]{2,1,0:T(8,128)(2,1)S(1)}, bf16[33,64,128]{2,1,0:T(8,128)(2,1)S(1)}, bf16[33,64,128]{2,1,0:T(8,128)(2,1)S(1)}, bf16[33,64,128]{2,1,0:T(8,128)(2,1)S(1)}) custom-call(s32[1]{0:T(128)} %bitcast.1.me_ref, s32[32]{0:T(128)S(1)} %bitcast.17, s32[32,4]{1,0:T(8,128)S(1)} %copy.13.tgt_ref, s32[8,16]{1,0:T(8,128)S(1)} %get-tuple-element.24.sb_ref, ...), custom_call_target="tpu_custom_call" | custom-call | tf_op jit(solution)/shard_map/back_swap/pallas_call | solution.py:227
  113.0 3.1 %back_own.1 = (bf16[33,64,128]{2,1,0:T(8,128)(2,1)S(1)}, bf16[33,64,128]{2,1,0:T(8,128)(2,1)S(1)}, bf16[33,64,128]{2,1,0:T(8,128)(2,1)S(1)}, bf16[33,64,128]{2,1,0:T(8,128)(2,1)S(1)}) custom-call(s32[1]{0:T(128)} %bitcast.1.me_ref, s32[32]{0:T(128)S(1)} %bitcast.18, s32[32,4]{1,0:T(8,128)S(1)} %copy.13.tgt_ref, s32[8,16]{1,0:T(8,128)S(1)} %get-tuple-element.24.sb_ref, ...), custom_call_target="tpu_custom_call" | custom-call | tf_op jit(solution)/shard_map/back_own/pallas_call | solution.py:227
  118.2 2.2 %collective-permute-start.28 = (bf16[33,64,128]{2,1,0:T(8,128)(2,1)S(1)}, bf16[33,64,128]{2,1,0:T(8,128)(2,1)S(1)}, u32[]{:S(2)}, u32[]{:S(2)}) collective-permute-start(bf16[33,64,128]{2,1,0:T(8,128)(2,1)S(1)} %add_convert_fusion.1), channel_id=1, source_target_pairs={{0,192},{8,200},{16,208},{24,216},{32,224},{40,232},{48,240},{56,2... | collective-permute-start | bytes 1622024 | tf_op jit(solution)/shard_map/ppermute | solution.py:36
  120.9 23.0 %collective-permute-done.26.p1 = bf16[33,64,128]{2,1,0:T(8,128)(2,1)S(1)} collective-permute-done((bf16[33,64,128]{2,1,0:T(8,128)(2,1)S(1)}, bf16[33,64,128]{2,1,0:T(8,128)(2,1)S(1)}, u32[]{:S(2)}, u32[]{:S(2)}) %collective-permute-start.26) | collective-permute-done | bytes 540704 | tf_op jit(solution)/shard_map/ppermute | solution.py:36
  144.3 3.8 %collective-permute-start.32 = (bf16[9,64,128]{2,1,0:T(8,128)(2,1)S(1)}, bf16[9,64,128]{2,1,0:T(8,128)(2,1)S(1)}, u32[]{:S(2)}, u32[]{:S(2)}) collective-permute-start(bf16[9,64,128]{2,1,0:T(8,128)(2,1)S(1)} %get-tuple-element.36), channel_id=1, source_target_pairs={{0,48},{8,56},{16,0},{24,8},{32,16},{40,24},{48,32},{56,40},{64,11... | collective-permute-start | bytes 442376 | tf_op jit(solution)/shard_map/ppermute | solution.py:36
  148.2 4.7 %collective-permute-done.31.z1 = bf16[9,64,128]{2,1,0:T(8,128)(2,1)S(1)} collective-permute-done((bf16[9,64,128]{2,1,0:T(8,128)(2,1)S(1)}, bf16[9,64,128]{2,1,0:T(8,128)(2,1)S(1)}, u32[]{:S(2)}, u32[]{:S(2)}) %collective-permute-start.31) | collective-permute-done | bytes 147488 | tf_op jit(solution)/shard_map/ppermute | solution.py:36
  153.6 4.8 %collective-permute-done.33.z3 = bf16[9,64,128]{2,1,0:T(8,128)(2,1)S(1)} collective-permute-done((bf16[9,64,128]{2,1,0:T(8,128)(2,1)S(1)}, bf16[9,64,128]{2,1,0:T(8,128)(2,1)S(1)}, u32[]{:S(2)}, u32[]{:S(2)}) %collective-permute-start.33) | collective-permute-done | bytes 147488 | tf_op jit(solution)/shard_map/ppermute | solution.py:36
  (96 shorter events, 22.9 us)
Async XLA Ops:
  3.4 9.4 %collective-permute-start = (bf16[9,64,128]{2,1,0:T(8,128)(2,1)S(1)}, bf16[9,64,128]{2,1,0:T(8,128)(2,1)S(1)}, u32[]{:S(2)}, u32[]{:S(2)}) collective-permute-start(bf16[9,64,128]{2,1,0:T(8,128)(2,1)S(1)} %prep.1.p0), channel_id=1, source_target_pairs={{0,16},{8,24},{16,32},{24,40},{32,48},{40,56},{48,0},{56,8},{64,80... | collective-permute-start | bytes 442376 | tf_op jit(solution)/shard_map/ppermute | solution.py:36
  5.3 8.6 %collective-permute-start.1 = (bf16[9,64,128]{2,1,0:T(8,128)(2,1)S(1)}, bf16[9,64,128]{2,1,0:T(8,128)(2,1)S(1)}, u32[]{:S(2)}, u32[]{:S(2)}) collective-permute-start(bf16[9,64,128]{2,1,0:T(8,128)(2,1)S(1)} %prep.1.p0), channel_id=1, source_target_pairs={{0,48},{8,56},{16,0},{24,8},{32,16},{40,24},{48,32},{56,40},{64,11... | collective-permute-start | bytes 442376 | tf_op jit(solution)/shard_map/ppermute | solution.py:36
  8.1 13.2 %collective-permute-start.2 = (bf16[9,64,128]{2,1,0:T(8,128)(2,1)S(1)}, bf16[9,64,128]{2,1,0:T(8,128)(2,1)S(1)}, u32[]{:S(2)}, u32[]{:S(2)}) collective-permute-start(bf16[9,64,128]{2,1,0:T(8,128)(2,1)S(1)} %prep.1.p0), channel_id=1, source_target_pairs={{0,32},{8,40},{16,48},{24,56},{32,0},{40,8},{48,16},{56,24},{64,96... | collective-permute-start | bytes 442376 | tf_op jit(solution)/shard_map/ppermute | solution.py:36
  21.4 15.5 %collective-permute-start.3 = (bf16[33,64,128]{2,1,0:T(8,128)(2,1)S(1)}, bf16[33,64,128]{2,1,0:T(8,128)(2,1)S(1)}, u32[]{:S(2)}, u32[]{:S(2)}) collective-permute-start(bf16[33,64,128]{2,1,0:T(8,128)(2,1)S(1)} %stack.1.rest_0_), channel_id=1, source_target_pairs={{0,64},{8,72},{16,80},{24,88},{32,96},{40,104},{48,112},{56,120},{... | collective-permute-start | bytes 1622024 | tf_op jit(solution)/shard_map/ppermute | solution.py:36
  23.1 24.9 %collective-permute-start.4 = (bf16[33,64,128]{2,1,0:T(8,128)(2,1)S(1)}, bf16[33,64,128]{2,1,0:T(8,128)(2,1)S(1)}, u32[]{:S(2)}, u32[]{:S(2)}) collective-permute-start(bf16[33,64,128]{2,1,0:T(8,128)(2,1)S(1)} %stack.1.rest_0_), channel_id=1, source_target_pairs={{0,192},{8,200},{16,208},{24,216},{32,224},{40,232},{48,240},{56,2... | collective-permute-start | bytes 1622024 | tf_op jit(solution)/shard_map/ppermute | solution.py:36
  24.7 25.1 %collective-permute-start.5 = (bf16[33,64,128]{2,1,0:T(8,128)(2,1)S(1)}, bf16[33,64,128]{2,1,0:T(8,128)(2,1)}, u32[]{:S(2)}, u32[]{:S(2)}) collective-permute-start(bf16[33,64,128]{2,1,0:T(8,128)(2,1)S(1)} %stack.1.rest_0_), channel_id=1, source_target_pairs={{0,128},{8,136},{16,144},{24,152},{32,160},{40,168},{48,176},{56,1... | collective-permute-start | bytes 1622024 | tf_op jit(solution)/shard_map/ppermute | solution.py:36
  26.7 37.4 %collective-permute-start.6 = (bf16[33,64,128]{2,1,0:T(8,128)(2,1)S(1)}, bf16[33,64,128]{2,1,0:T(8,128)(2,1)S(1)}, u32[]{:S(2)}, u32[]{:S(2)}) collective-permute-start(bf16[33,64,128]{2,1,0:T(8,128)(2,1)S(1)} %stack.1.rest_0_), channel_id=1, source_target_pairs={{0,8},{8,0},{16,24},{24,16},{32,40},{40,32},{48,56},{56,48},{64,72... | collective-permute-start | bytes 1622024 | tf_op jit(solution)/shard_map/ppermute | solution.py:36
  37.0 28.5 %collective-permute-start.7 = (bf16[33,64,128]{2,1,0:T(8,128)(2,1)S(1)}, bf16[33,64,128]{2,1,0:T(8,128)(2,1)S(1)}, u32[]{:S(2)}, u32[]{:S(2)}) collective-permute-start(bf16[33,64,128]{2,1,0:T(8,128)(2,1)S(1)} %collective-permute-done.3.rest_1_), channel_id=1, source_target_pairs={{0,8},{8,0},{16,24},{24,16},{32,40},{40,32},{48,56},{56,48},{64,72... | collective-permute-start | bytes 1622024 | tf_op jit(solution)/shard_map/ppermute | solution.py:36
  47.9 20.5 %collective-permute-start.8 = (bf16[33,64,128]{2,1,0:T(8,128)(2,1)S(1)}, bf16[33,64,128]{2,1,0:T(8,128)(2,1)}, u32[]{:S(2)}, u32[]{:S(2)}) collective-permute-start(bf16[33,64,128]{2,1,0:T(8,128)(2,1)S(1)} %collective-permute-done.4.rest_2_), channel_id=1, source_target_pairs={{0,8},{8,0},{16,24},{24,16},{32,40},{40,32},{48,56},{56,48},{64,72... | collective-permute-start | bytes 1622024 | tf_op jit(solution)/shard_map/ppermute | solution.py:36
  49.8 19.7 %collective-permute-start.9 = (bf16[33,64,128]{2,1,0:T(8,128)(2,1)}, bf16[33,64,128]{2,1,0:T(8,128)(2,1)}, u32[]{:S(2)}, u32[]{:S(2)}) collective-permute-start(bf16[33,64,128]{2,1,0:T(8,128)(2,1)} %collective-permute-done.5.rest_3_), channel_id=1, source_target_pairs={{0,8},{8,0},{16,24},{24,16},{32,40},{40,32},{48,56},{56,48},{64,72... | collective-permute-start | bytes 1622024 | tf_op jit(solution)/shard_map/ppermute | solution.py:36
  49.8 12.7 %collective-permute-start.20 = (bf16[64,1024]{1,0:T(8,128)(2,1)S(1)}, bf16[64,1024]{1,0:T(8,128)(2,1)}, u32[]{:S(2)}, u32[]{:S(2)}) collective-permute-start(bf16[64,1024]{1,0:T(8,128)(2,1)S(1)} %copy-done.10), channel_id=1, source_target_pairs={{0,4},{1,5},{2,6},{3,7},{4,0},{5,1},{6,2},{7,3},{8,12},{9,13},{10,... | collective-permute-start | bytes 393224 | tf_op jit(solution)/shard_map/ppermute | solution.py:40
  62.6 16.7 %collective-permute-start.17 = (bf16[64,1024]{1,0:T(8,128)(2,1)S(1)}, bf16[64,1024]{1,0:T(8,128)(2,1)}, u32[]{:S(2)}, u32[]{:S(2)}) collective-permute-start(bf16[64,1024]{1,0:T(8,128)(2,1)S(1)} %copy-done.10), channel_id=1, source_target_pairs={{0,1},{1,2},{2,3},{3,0},{4,5},{5,6},{6,7},{7,4},{8,9},{9,10},{10,1... | collective-permute-start | bytes 393224 | tf_op jit(solution)/shard_map/ppermute | solution.py:41
  64.9 17.1 %collective-permute-start.18 = (bf16[64,1024]{1,0:T(8,128)(2,1)S(1)}, bf16[64,1024]{1,0:T(8,128)(2,1)}, u32[]{:S(2)}, u32[]{:S(2)}) collective-permute-start(bf16[64,1024]{1,0:T(8,128)(2,1)S(1)} %copy-done.10), channel_id=1, source_target_pairs={{0,3},{1,0},{2,1},{3,2},{4,7},{5,4},{6,5},{7,6},{8,11},{9,8},{10,9... | collective-permute-start | bytes 393224 | tf_op jit(solution)/shard_map/ppermute | solution.py:41
  66.2 17.3 %collective-permute-start.19 = (bf16[64,1024]{1,0:T(8,128)(2,1)S(1)}, bf16[64,1024]{1,0:T(8,128)(2,1)}, u32[]{:S(2)}, u32[]{:S(2)}) collective-permute-start(bf16[64,1024]{1,0:T(8,128)(2,1)S(1)} %copy-done.10), channel_id=1, source_target_pairs={{0,2},{1,3},{2,0},{3,1},{4,6},{5,7},{6,4},{7,5},{8,10},{9,11},{10,... | collective-permute-start | bytes 393224 | tf_op jit(solution)/shard_map/ppermute | solution.py:41
  68.4 17.7 %collective-permute-start.21 = (bf16[64,1024]{1,0:T(8,128)(2,1)}, bf16[64,1024]{1,0:T(8,128)(2,1)S(1)}, u32[]{:S(2)}, u32[]{:S(2)}) collective-permute-start(bf16[64,1024]{1,0:T(8,128)(2,1)} %collective-permute-done.20.rest_12_), channel_id=1, source_target_pairs={{0,1},{1,2},{2,3},{3,0},{4,5},{5,6},{6,7},{7,4},{8,9},{9,10},{10,1... | collective-permute-start | bytes 393224 | tf_op jit(solution)/shard_map/ppermute | solution.py:42
  69.5 17.2 %collective-permute-start.22 = (bf16[64,1024]{1,0:T(8,128)(2,1)}, bf16[64,1024]{1,0:T(8,128)(2,1)S(1)}, u32[]{:S(2)}, u32[]{:S(2)}) collective-permute-start(bf16[64,1024]{1,0:T(8,128)(2,1)} %collective-permute-done.20.rest_12_), channel_id=1, source_target_pairs={{0,3},{1,0},{2,1},{3,2},{4,7},{5,4},{6,5},{7,6},{8,11},{9,8},{10,9... | collective-permute-start | bytes 393224 | tf_op jit(solution)/shard_map/ppermute | solution.py:42
  79.3 9.5 %collective-permute-start.13 = (bf16[64,1024]{1,0:T(8,128)(2,1)}, bf16[64,1024]{1,0:T(8,128)(2,1)S(1)}, u32[]{:S(2)}, u32[]{:S(2)}) collective-permute-start(bf16[64,1024]{1,0:T(8,128)(2,1)} %get-tuple-element.21.rest_0_), channel_id=1, source_target_pairs={{0,4},{1,5},{2,6},{3,7},{4,0},{5,1},{6,2},{7,3},{8,12},{9,13},{10,... | collective-permute-start | bytes 393224 | tf_op jit(solution)/shard_map/ppermute | solution.py:40
  82.0 9.2 %collective-permute-start.23 = (bf16[64,1024]{1,0:T(8,128)(2,1)}, bf16[64,1024]{1,0:T(8,128)(2,1)S(1)}, u32[]{:S(2)}, u32[]{:S(2)}) collective-permute-start(bf16[64,1024]{1,0:T(8,128)(2,1)} %collective-permute-done.20.rest_12_), channel_id=1, source_target_pairs={{0,2},{1,3},{2,0},{3,1},{4,6},{5,7},{6,4},{7,5},{8,10},{9,11},{10,... | collective-permute-start | bytes 393224 | tf_op jit(solution)/shard_map/ppermute | solution.py:42
  83.5 8.2 %collective-permute-start.10 = (bf16[64,1024]{1,0:T(8,128)(2,1)}, bf16[64,1024]{1,0:T(8,128)(2,1)S(1)}, u32[]{:S(2)}, u32[]{:S(2)}) collective-permute-start(bf16[64,1024]{1,0:T(8,128)(2,1)} %get-tuple-element.21.rest_0_), channel_id=1, source_target_pairs={{0,1},{1,2},{2,3},{3,0},{4,5},{5,6},{6,7},{7,4},{8,9},{9,10},{10,1... | collective-permute-start | bytes 393224 | tf_op jit(solution)/shard_map/ppermute | solution.py:41
  86.7 9.2 %collective-permute-start.11 = (bf16[64,1024]{1,0:T(8,128)(2,1)}, bf16[64,1024]{1,0:T(8,128)(2,1)S(1)}, u32[]{:S(2)}, u32[]{:S(2)}) collective-permute-start(bf16[64,1024]{1,0:T(8,128)(2,1)} %get-tuple-element.21.rest_0_), channel_id=1, source_target_pairs={{0,3},{1,0},{2,1},{3,2},{4,7},{5,4},{6,5},{7,6},{8,11},{9,8},{10,9... | collective-permute-start | bytes 393224 | tf_op jit(solution)/shard_map/ppermute | solution.py:41
  87.4 8.5 %collective-permute-start.12 = (bf16[64,1024]{1,0:T(8,128)(2,1)}, bf16[64,1024]{1,0:T(8,128)(2,1)S(1)}, u32[]{:S(2)}, u32[]{:S(2)}) collective-permute-start(bf16[64,1024]{1,0:T(8,128)(2,1)} %get-tuple-element.21.rest_0_), channel_id=1, source_target_pairs={{0,2},{1,3},{2,0},{3,1},{4,6},{5,7},{6,4},{7,5},{8,10},{9,11},{10,... | collective-permute-start | bytes 393224 | tf_op jit(solution)/shard_map/ppermute | solution.py:41
  88.9 8.2 %collective-permute-start.14 = (bf16[64,1024]{1,0:T(8,128)(2,1)S(1)}, bf16[64,1024]{1,0:T(8,128)(2,1)S(1)}, u32[]{:S(2)}, u32[]{:S(2)}) collective-permute-start(bf16[64,1024]{1,0:T(8,128)(2,1)S(1)} %collective-permute-done.13.rest_4_), channel_id=1, source_target_pairs={{0,1},{1,2},{2,3},{3,0},{4,5},{5,6},{6,7},{7,4},{8,9},{9,10},{10,1... | collective-permute-start | bytes 393224 | tf_op jit(solution)/shard_map/ppermute | solution.py:42
  91.1 8.8 %collective-permute-start.15 = (bf16[64,1024]{1,0:T(8,128)(2,1)S(1)}, bf16[64,1024]{1,0:T(8,128)(2,1)S(1)}, u32[]{:S(2)}, u32[]{:S(2)}) collective-permute-start(bf16[64,1024]{1,0:T(8,128)(2,1)S(1)} %collective-permute-done.13.rest_4_), channel_id=1, source_target_pairs={{0,3},{1,0},{2,1},{3,2},{4,7},{5,4},{6,5},{7,6},{8,11},{9,8},{10,9... | collective-permute-start | bytes 393224 | tf_op jit(solution)/shard_map/ppermute | solution.py:42
  91.7 8.9 %collective-permute-start.16 = (bf16[64,1024]{1,0:T(8,128)(2,1)S(1)}, bf16[64,1024]{1,0:T(8,128)(2,1)}, u32[]{:S(2)}, u32[]{:S(2)}) collective-permute-start(bf16[64,1024]{1,0:T(8,128)(2,1)S(1)} %collective-permute-done.13.rest_4_), channel_id=1, source_target_pairs={{0,2},{1,3},{2,0},{3,1},{4,6},{5,7},{6,4},{7,5},{8,10},{9,11},{10,... | collective-permute-start | bytes 393224 | tf_op jit(solution)/shard_map/ppermute | solution.py:42
  112.4 5.6 %collective-permute-start.27 = (bf16[33,64,128]{2,1,0:T(8,128)(2,1)S(1)}, bf16[33,64,128]{2,1,0:T(8,128)(2,1)S(1)}, u32[]{:S(2)}, u32[]{:S(2)}) collective-permute-start(bf16[33,64,128]{2,1,0:T(8,128)(2,1)S(1)} %get-tuple-element.31), channel_id=1, source_target_pairs={{0,8},{8,0},{16,24},{24,16},{32,40},{40,32},{48,56},{56,48},{64,72... | collective-permute-start | bytes 1622024 | tf_op jit(solution)/shard_map/ppermute | solution.py:36
  112.9 7.5 %collective-permute-start.29 = (bf16[33,64,128]{2,1,0:T(8,128)(2,1)S(1)}, bf16[33,64,128]{2,1,0:T(8,128)(2,1)S(1)}, u32[]{:S(2)}, u32[]{:S(2)}) collective-permute-start(bf16[33,64,128]{2,1,0:T(8,128)(2,1)S(1)} %get-tuple-element.33), channel_id=1, source_target_pairs={{0,8},{8,0},{16,24},{24,16},{32,40},{40,32},{48,56},{56,48},{64,72... | collective-permute-start | bytes 1622024 | tf_op jit(solution)/shard_map/ppermute | solution.py:36
  116.8 27.1 %collective-permute-start.26 = (bf16[33,64,128]{2,1,0:T(8,128)(2,1)S(1)}, bf16[33,64,128]{2,1,0:T(8,128)(2,1)S(1)}, u32[]{:S(2)}, u32[]{:S(2)}) collective-permute-start(bf16[33,64,128]{2,1,0:T(8,128)(2,1)S(1)} %add_convert_fusion.2), channel_id=1, source_target_pairs={{0,64},{8,72},{16,80},{24,88},{32,96},{40,104},{48,112},{56,120},{... | collective-permute-start | bytes 1622024 | tf_op jit(solution)/shard_map/ppermute | solution.py:36
  118.2 25.7 %collective-permute-start.28 = (bf16[33,64,128]{2,1,0:T(8,128)(2,1)S(1)}, bf16[33,64,128]{2,1,0:T(8,128)(2,1)S(1)}, u32[]{:S(2)}, u32[]{:S(2)}) collective-permute-start(bf16[33,64,128]{2,1,0:T(8,128)(2,1)S(1)} %add_convert_fusion.1), channel_id=1, source_target_pairs={{0,192},{8,200},{16,208},{24,216},{32,224},{40,232},{48,240},{56,2... | collective-permute-start | bytes 1622024 | tf_op jit(solution)/shard_map/ppermute | solution.py:36
  120.6 23.4 %collective-permute-start.30 = (bf16[33,64,128]{2,1,0:T(8,128)(2,1)S(1)}, bf16[33,64,128]{2,1,0:T(8,128)(2,1)S(1)}, u32[]{:S(2)}, u32[]{:S(2)}) collective-permute-start(bf16[33,64,128]{2,1,0:T(8,128)(2,1)S(1)} %add_convert_fusion), channel_id=1, source_target_pairs={{0,128},{8,136},{16,144},{24,152},{32,160},{40,168},{48,176},{56,1... | collective-permute-start | bytes 1622024 | tf_op jit(solution)/shard_map/ppermute | solution.py:36
  144.2 8.7 %collective-permute-start.31 = (bf16[9,64,128]{2,1,0:T(8,128)(2,1)S(1)}, bf16[9,64,128]{2,1,0:T(8,128)(2,1)S(1)}, u32[]{:S(2)}, u32[]{:S(2)}) collective-permute-start(bf16[9,64,128]{2,1,0:T(8,128)(2,1)S(1)} %get-tuple-element.35), channel_id=1, source_target_pairs={{0,16},{8,24},{16,32},{24,40},{32,48},{40,56},{48,0},{56,8},{64,80... | collective-permute-start | bytes 442376 | tf_op jit(solution)/shard_map/ppermute | solution.py:36
  144.3 9.3 %collective-permute-start.32 = (bf16[9,64,128]{2,1,0:T(8,128)(2,1)S(1)}, bf16[9,64,128]{2,1,0:T(8,128)(2,1)S(1)}, u32[]{:S(2)}, u32[]{:S(2)}) collective-permute-start(bf16[9,64,128]{2,1,0:T(8,128)(2,1)S(1)} %get-tuple-element.36), channel_id=1, source_target_pairs={{0,48},{8,56},{16,0},{24,8},{32,16},{40,24},{48,32},{56,40},{64,11... | collective-permute-start | bytes 442376 | tf_op jit(solution)/shard_map/ppermute | solution.py:36
  148.1 10.2 %collective-permute-start.33 = (bf16[9,64,128]{2,1,0:T(8,128)(2,1)S(1)}, bf16[9,64,128]{2,1,0:T(8,128)(2,1)S(1)}, u32[]{:S(2)}, u32[]{:S(2)}) collective-permute-start(bf16[9,64,128]{2,1,0:T(8,128)(2,1)S(1)} %get-tuple-element.37), channel_id=1, source_target_pairs={{0,32},{8,40},{16,48},{24,56},{32,0},{40,8},{48,16},{56,24},{64,96... | collective-permute-start | bytes 442376 | tf_op jit(solution)/shard_map/ppermute | solution.py:36
  (24 other events, 477.6 us)

commit v2 on v1

v2 whole, which is shorter than its diff:
```python
import functools

import jax
import jax.numpy as jnp
from jax import lax
from jax.experimental import pallas as pl
from jax.experimental.pallas import tpu as pltpu
from jax.sharding import PartitionSpec as P

BF = jnp.bfloat16
F32 = jnp.float32
VM = pl.BlockSpec(memory_space=pltpu.VMEM)
HB = pl.BlockSpec(memory_space=pltpu.HBM)
ANY = pl.BlockSpec(memory_space=pl.ANY)
SM = pl.BlockSpec(memory_space=pltpu.SMEM)
MIB = 1 << 20
STEPS = (0, 1, 3, 2)
BACK = (0, 2, 1, 3)
NY, NZ, NC = 4, 4, 2
LIVE = 33
NA = 6
NB = 8 - NA
WIDE_A, WIDE_B = 4 * NA + 1, 4 * NB


def row_perm(dy, dz, dc):
    pairs = []
    for y in range(NY):
        for z in range(NZ):
            for c in range(NC):
                to = (((y + dy) % NY) * NZ + (z + dz) % NZ) * NC + (c + dc) % NC
                pairs.append(((y * NZ + z) * NC + c, to))
    return pairs


def feat_perm(dh, dx):
    return [(h * 4 + x, ((h + dh) % 2) * 4 + (x + dx) % 4) for h in range(2) for x in range(4)]


def row_send(value, dy, dz, dc):
    return lax.ppermute(value, "row", row_perm(dy, dz, dc))


def feat_gather(value):
    across = lax.ppermute(value, "feat", feat_perm(1, 0))
    near = [lax.ppermute(value, "feat", feat_perm(0, k)) for k in STEPS[1:]]
    far = [lax.ppermute(across, "feat", feat_perm(0, k)) for k in STEPS[1:]]
    return [value, *near, across, *far]


def dot(a, b):
    return jnp.dot(a, b, preferred_element_type=F32)


def dot_nt(a, b):
    return lax.dot_general(a, b, (((1,), (1,)), ((), ())), preferred_element_type=F32)


def dot_tn(a, b):
    return lax.dot_general(a, b, (((0,), (0,)), ((), ())), preferred_element_type=F32)


def here():
    me = lax.axis_index("row")
    return lax.div(me, 8), lax.rem(lax.div(me, 2), 4), lax.rem(me, 2)


def ahead(at, step):
    return lax.rem(at + step, 4)


def behind(at, step):
    return lax.rem(at + 4 - step, 4)


def prep_kernel(x_ref, ints_ref, out_ref):
    _, z, c = here()
    window = (z * 2 + c) * 16
    other = (z * 2 + 1 - c) * 16
    for b in range(8):
        out_ref[b] = x_ref[:, b * 128 : (b + 1) * 128]
    rows = lax.broadcasted_iota(jnp.int32, (1024, 16), 0)
    pick = (rows == ints_ref[9:10, 0:16]).astype(F32).astype(BF)
    hubs = dot(x_ref[...], pick).astype(BF)
    lane = lax.broadcasted_iota(jnp.int32, (16, 128), 1)
    which = lax.broadcasted_iota(jnp.int32, (16, 128), 0)
    extra = dot(hubs, (lane == window + which).astype(F32).astype(BF))
    lane = lax.broadcasted_iota(jnp.int32, (4, 128), 1)
    which = lax.broadcasted_iota(jnp.int32, (4, 128), 0)
    place = (lane == other + which).astype(F32)
    ids = dot_tn(ints_ref[0:4, :].astype(F32), place)
    out_ref[8, 0:32, :] = (extra[0:32] + ids).astype(BF)
    out_ref[8, 32:64, :] = extra[32:64].astype(BF)


def stack_kernel(p0, p1, p2, p3, out_ref):
    extra = jnp.zeros((64, 128), F32)
    for i, p in enumerate((p0, p1, p2, p3)):
        out_ref[i * 8 : (i + 1) * 8] = p[0:8]
        extra = extra + p[8].astype(F32)
    out_ref[32] = extra.astype(BF)


def pair_kernel(up_ref, far_ref, w_ref, tiles_ref, _, pair_ref, wt_ref, own_ref):
    pair_ref[0:64, :] = up_ref[...]
    pair_ref[64:128, :] = far_ref[...]
    wt_ref[...] = w_ref[...].T
    own_ref[...] = w_ref[pl.ds(pl.multiple_of(lax.axis_index("feat") * 64, 64), 64), :]


def slot_sums(swap, ints_ref, srcs, tiles_ref, sb_ref, acc, ids_v, ids_s, sem):
    y, z, c = here()
    me = (y * 4 + z) * 2 + c
    cc = 1 - c if swap else c
    row = lax.broadcasted_iota(jnp.int32, (64, 128), 0)
    ids_v[...] = jnp.zeros_like(ids_v)
    for j in range(4):
        mine = jnp.where(row == me, srcs[j][32].astype(F32), 0.0)
        ids_v[j : j + 1, :] = jnp.sum(mine, axis=0, keepdims=True).astype(jnp.int32)
    copy = pltpu.make_async_copy(ids_v, ids_s, sem)
    copy.start()
    copy.wait()
    for j in range(4):
        sy = behind(y, STEPS[j])
        for i in range(4):
            sz = behind(z, STEPS[i])
            s = (sy * 4 + sz) * 2 + cc
            count = ints_ref[8, s]
            parts = []
            for k in range(4):
                b = ids_s[j, (sz * 2 + 1 - cc) * 16 + k]
                sb_ref[sy, sz * 4 + k] = b
                parts.append(dot(srcs[j][i * 8 + b], tiles_ref[s, k]))
            for k in range(4):
                t = jnp.where(k < count, ints_ref[4 + k, s], 8)
                acc[t] += parts[k]


def agg_own_kernel(ints_ref, *rest):
    srcs = rest[:4]
    tiles_ref, out_ref, sb_ref, acc, *scratch = rest[4:]
    acc[...] = jnp.zeros_like(acc)
    slot_sums(False, ints_ref, srcs, tiles_ref, sb_ref, acc, *scratch)
    out_ref[...] = acc[0:8]


def agg_swap_kernel(ints_ref, *rest):
    srcs, owns = rest[:4], rest[4:8]
    tiles_ref, adj_ref, x_ref, self_ref, sum_ref, out_ref, sb_ref, acc, *scratch = rest[8:]
    y, _, c = here()
    acc[0:8] = sum_ref[...]
    acc[8] = jnp.zeros((64, 128), F32)
    slot_sums(True, ints_ref, srcs, tiles_ref, sb_ref, acc, *scratch)
    side = lax.rem(lax.div(lax.broadcasted_iota(jnp.int32, (64, 128), 1), 16), 2)
    hub = jnp.zeros((64, 1024), F32)
    for j in range(4):
        sy = behind(y, STEPS[j])
        both = jnp.where(side == c, owns[j][32].astype(F32), srcs[j][32].astype(F32)).astype(BF)
        hub = hub + dot(both, adj_ref[pl.ds(pl.multiple_of(sy * 128, 128), 128), :])
    for b in range(8):
        cols = slice(b * 128, (b + 1) * 128)
        total = x_ref[:, cols].astype(F32) * self_ref[:, cols] + hub[:, cols] + acc[b]
        out_ref[:, cols] = total.astype(BF)


def mid_kernel(*rest):
    aggs = rest[:8]
    ups = rest[8:12]
    wt_ref, own_ref, act_ref, ga_ref, full, pre, down = rest[12:]
    group = lax.axis_index("feat")
    h, x = lax.div(group, 4), lax.rem(group, 4)
    first = []
    for j in range(8):
        hh = h if j < 4 else 1 - h
        first.append(pl.multiple_of((hh * 4 + behind(x, STEPS[j % 4])) * 64, 64))
    for j in range(8):
        full[pl.ds(first[j], 64), :] = aggs[j][...]
    own = own_ref[...]
    for n in range(4):
        cols = slice(n * 256, (n + 1) * 256)
        pre[...] = dot(wt_ref[...], full[:, cols])
        for j in range(8):
            v = pre[pl.ds(first[j], 64), :]
            sq = v * v
            t = jnp.tanh(v * (0.7978845608 + (0.7978845608 * 0.044715) * sq))
            half = 0.5 + 0.5 * t
            if j == 0:
                act_ref[:, cols] = (v * half).astype(BF)
            slope = half + (0.5 * v) * (1.0 - t * t) * (
                0.7978845608 + (0.7978845608 * 3 * 0.044715) * sq
            )
            up = ups[j % 4][(j // 4) * 64 : (j // 4 + 1) * 64, cols]
            down[pl.ds(first[j], 64), :] = (up.astype(F32) * slope).astype(BF)
        grads = dot(own, down[...]).astype(BF)
        ga_ref[2 * n] = grads[:, :128]
        ga_ref[2 * n + 1] = grads[:, 128:]


def back_kernel(swap, ints_ref, sb_ref, ga_ref, tiles_ref, adj_ref, out, acc):
    y, z, c = here()
    cc = 1 - c if swap else c
    for j in range(4):
        sy = ahead(y, STEPS[j])
        hubs = jnp.zeros((64, 128), F32)
        at = pl.ds(pl.multiple_of(sy * 128, 128), 128)
        for b in range(8):
            hubs = hubs + dot_nt(ga_ref[b], adj_ref[at, b * 128 : (b + 1) * 128])
        out[128 + j] = hubs.astype(BF)
        for i in range(4):
            sz = ahead(z, STEPS[i])
            s = (sy * 4 + sz) * 2 + cc
            count = ints_ref[8, s]
            acc[0:8] = jnp.zeros((8, 64, 128), F32)
            parts = [dot_nt(ga_ref[ints_ref[4 + k, s]], tiles_ref[s, k]) for k in range(4)]
            for k in range(4):
                b = jnp.where(k < count, sb_ref[sy, sz * 4 + k], 8)
                acc[b] += parts[k]
            n = (j * 4 + i) * 8
            out[n : n + 8] = acc[0:8].astype(BF)


def add_kernel(a, b, *outs):
    def both(n):
        return (a[n].astype(F32) + b[n].astype(F32)).astype(BF)

    for j in range(4):
        for i in range(4):
            for r in range(8):
                total = both((j * 4 + i) * 8 + r)
                if r < NA:
                    outs[j][i * NA + r] = total
                else:
                    outs[4 + i][j * NB + r - NA] = total
        outs[j][4 * NA] = both(128 + j)


def four(refs, r):
    return (refs[0][r].astype(F32) + refs[1][r].astype(F32)) + (refs[2][r].astype(F32) + refs[3][r].astype(F32))


def sum_a_kernel(*refs):
    hubs = four(refs[:4], 4 * NA).astype(BF)
    for i in range(4):
        for b in range(NA):
            refs[4 + i][b] = four(refs[:4], i * NA + b).astype(BF)
        refs[4 + i][NA] = hubs


def sum_b_kernel(*refs):
    for j in range(4):
        for b in range(NB):
            refs[4 + j][b] = four(refs[:4], j * NB + b).astype(BF)


def last_kernel(*rest):
    pas, pbs = rest[:4], rest[4:8]
    ga_ref, self_ref, ids_ref, out_ref = rest[8:]
    _, z, c = here()

    def halves(v):
        high = v.astype(BF)
        return high, (v - high.astype(F32)).astype(BF)

    lane = lax.broadcasted_iota(jnp.int32, (128, 16), 0)
    which = lax.broadcasted_iota(jnp.int32, (128, 16), 1)
    take = (lane == (z * 2 + c) * 16 + which).astype(F32).astype(BF)
    high, low = halves(four(pas, NA))
    high, low = halves(dot(high, take) + dot(low, take))
    node = lax.broadcasted_iota(jnp.int32, (1024, 16), 0)
    spread = (node == ids_ref[...]).astype(F32).astype(BF)
    hubs = dot_nt(high, spread) + dot_nt(low, spread)
    for b in range(8):
        cols = slice(b * 128, (b + 1) * 128)
        total = four(pas, b) if b < NA else four(pbs, b - NA)
        out_ref[:, cols] = (ga_ref[b].astype(F32) * self_ref[:, cols] + hubs[:, cols] + total).astype(BF)


def call(kernel, name, outs, args, scalars=0, scratch=(), limit=8, out_specs=None, size=MIB, hbm=0, loose=0):
    shapes = [jax.ShapeDtypeStruct(s, d) for s, d in outs]
    return pl.pallas_call(
        kernel,
        out_shape=shapes,
        in_specs=[HB] * hbm + [SM] * scalars + [VM] * (len(args) - scalars - hbm - loose) + [ANY] * loose,
        out_specs=out_specs or [VM] * len(shapes),
        scratch_shapes=list(scratch),
        compiler_params=pltpu.CompilerParams(vmem_limit_bytes=limit * MIB),
        cost_estimate=pl.CostEstimate(flops=0, bytes_accessed=size, transcendentals=0),
        name=name,
    )(*args)


def shards(
    node_feats,
    self_weight,
    hub_ids,
    hub_adjacency,
    send_blocks,
    recv_counts,
    recv_targets,
    recv_tiles,
    weight,
    grad_out,
):
    ids = hub_ids.reshape(1, 16)
    ints = jnp.concatenate(
        [
            jnp.transpose(send_blocks, (0, 2, 1)).reshape(4, 32),
            jnp.transpose(recv_targets, (0, 2, 1)).reshape(4, 32),
            recv_counts,
            jnp.concatenate([ids, ids], axis=1),
        ],
        axis=0,
    )
    tiles = recv_tiles.reshape(32, 4, 128, 128)
    self_row = self_weight.reshape(1, 1024)

    def shape(n):
        return ((n, 64, 128), BF)

    (p0,) = call(prep_kernel, "prep", [shape(9)], (node_feats, ints))
    ps = [p0] + [row_send(p0, 0, k, 0) for k in STEPS[1:]]
    (s0,) = call(stack_kernel, "stack", [shape(LIVE)], ps)
    owns = [s0] + [row_send(s0, k, 0, 0) for k in STEPS[1:]]
    up, _ = lax.optimization_barrier((grad_out, p0))
    up_far = lax.ppermute(up, "feat", feat_perm(1, 0))
    pair, wt, own = call(
        pair_kernel, "pair", [((128, 1024), BF), ((512, 512), BF), ((64, 512), BF)],
        (grad_out, up_far, weight, tiles, s0), 0, (), 12, loose=1,
    )
    ups = [pair] + [lax.ppermute(pair, "feat", feat_perm(0, k)) for k in STEPS[1:]]
    late = lax.optimization_barrier((owns[3], *ups))
    owns[3], ups = late[0], late[1:]
    swaps = [row_send(v, 0, 0, 1) for v in owns]
    slots = [
        pltpu.VMEM((9, 64, 128), F32),
        pltpu.VMEM((8, 128), jnp.int32),
        pltpu.SMEM((8, 128), jnp.int32),
        pltpu.SemaphoreType.DMA,
    ]
    listed = ((4, 16), jnp.int32)
    part, sb_own = call(
        agg_own_kernel, "agg_own", [((8, 64, 128), F32), listed],
        (ints, *owns, tiles), 1, slots, 16, [VM, SM], 8 * MIB,
    )
    agg, sb_swap = call(
        agg_swap_kernel, "agg_swap", [((64, 1024), BF), listed],
        (ints, *swaps, *owns, tiles, hub_adjacency, node_feats, self_row, part),
        1, slots, 16, [VM, SM], 8 * MIB,
    )
    aggs = feat_gather(agg)
    act, ga = call(
        mid_kernel, "middle", [((64, 1024), BF), shape(8)], (*aggs, *ups, wt, own), 0,
        [
            pltpu.VMEM((512, 1024), BF),
            pltpu.VMEM((512, 256), F32),
            pltpu.VMEM((512, 256), BF),
        ],
        16, None, 16 * MIB,
    )
    outs = []
    for swap in (True, False):
        (out,) = call(
            functools.partial(back_kernel, swap), "back_swap" if swap else "back_own",
            [shape(132)], (ints, sb_swap if swap else sb_own, ga, tiles, hub_adjacency), 2,
            [pltpu.VMEM((9, 64, 128), F32)], 16, None, 8 * MIB,
        )
        outs.append(out)
    came = row_send(outs[0], 0, 0, 1)
    both = call(add_kernel, "add", [shape(WIDE_A)] * 4 + [shape(WIDE_B)] * 4, (outs[1], came), 0, (), 16)
    ras = [both[0]] + [row_send(both[j], STEPS[j], 0, 0) for j in (1, 2, 3)]
    rbs = [both[4]] + [row_send(both[4 + i], 0, STEPS[i], 0) for i in (1, 2, 3)]
    zas = call(sum_a_kernel, "sum_a", [shape(NA + 1)] * 4, ras)
    ybs = call(sum_b_kernel, "sum_b", [shape(NB)] * 4, rbs)
    zas = [zas[0]] + [row_send(zas[i], 0, STEPS[i], 0) for i in (1, 2, 3)]
    ybs = [ybs[0]] + [row_send(ybs[j], STEPS[j], 0, 0) for j in (1, 2, 3)]
    (grad_in,) = call(last_kernel, "last", [((64, 1024), BF)], (*zas, *ybs, ga, self_row, ids))
    return (act, grad_in)


def solution(mesh):
    in_specs = (
        P("feat", "row"),
        P("row"),
        P("row"),
        P(None, "row"),
        P("row", None, None),
        P("row", None),
        P("row", None, None),
        P("row", None, None, None, None),
        P(),
        P("feat", "row"),
    )
    out_specs = (P("feat", "row"), P("feat", "row"))
    return jax.shard_map(shards, mesh=mesh, in_specs=in_specs, out_specs=out_specs, check_vma=False)
```

time: 161 us -> 132 us (0.82)
  waiting for transfers between devices: 82.8 us -> 57.4 us
  local copies, waits for them, and re-layouts: 13.7 us -> 5.07 us
  starting transfers between devices: 43.6 us -> 50.7 us
    ppermute x20 -> x23, waiting for transfers between devices: 69 us -> 37.2 us  [row_send(): return lax.ppermute(value, 'row', row_perm(dy, dz, dc))]
    ppermute x0 -> x4, waiting for transfers between devices: none -> 11.2 us  [the longest x3 11.2 us: shards(): lax.ppermute(pair, 'feat', feat_perm(0, k))]
    ppermute x0 -> x4, starting transfers between devices: none -> 9.95 us  [the longest x1 5.72 us: shards(): up_far = lax.ppermute(up, 'feat', feat_perm(1, 0))]
    ppermute x20 -> x23, starting transfers between devices: 19.4 us -> 27.5 us  [row_send(): return lax.ppermute(value, 'row', row_perm(dy, dz, dc))]
    unnamed x45 -> x18, local copies, waits for them, and re-layouts: 12.7 us -> 5.07 us
    ppermute x2 -> x1, waiting for transfers between devices: 7.9 us -> 3.48 us  [feat_gather(): across = lax.ppermute(value, 'feat', feat_perm(1, 0))]
    ppermute x6 -> x3, starting transfers between devices: 8.51 us -> 4.15 us  [feat_gather(): far = [lax.ppermute(across, 'feat', feat_perm(0, k)) for k in STEPS[1:]]]
    ppermute x6 -> x3, starting transfers between devices: 8.22 us -> 4.15 us  [feat_gather(): near = [lax.ppermute(value, 'feat', feat_perm(0, k)) for k in STEPS[1:]]]
  transfers between devices with their start and end apart: 34 -> 34, of which waited for: 14 -> 15; matrix products, arithmetic and copies ran while one was open for 1% -> 0% of each run, Pallas kernels for 5% -> 4%
where the time goes in v2:
time: 132 us
  waiting for transfers between devices  57.4 us (43%)
  starting transfers between devices  50.7 us (38%)
  Pallas kernels  17 us (13%)
  local copies, waits for them, and re-layouts  5.07 us (4%)
    ppermute x23, waiting for transfers between devices, row_send(): return lax.ppermute(value, 'row', row_perm(dy, dz, dc))  37.2 us
    ppermute x23, starting transfers between devices, row_send(): return lax.ppermute(value, 'row', row_perm(dy, dz, dc))  27.5 us
    pallas_call x12, Pallas kernels, call(): pl.pallas_call(kernel, out_shape=shapes, in_specs=[HB] * hbm + [SM] * sca...  17 us
    ppermute x3, waiting for transfers between devices, shards(): lax.ppermute(pair, 'feat', feat_perm(0, k))  11.2 us
    ppermute x1, starting transfers between devices, shards(): up_far = lax.ppermute(up, 'feat', feat_perm(1, 0))  5.72 us
    ppermute x3, waiting for transfers between devices, feat_gather(): far = [lax.ppermute(across, 'feat', feat_perm(0, k)) for k in STEPS[1:]]  5.44 us
    unnamed x18, local copies, waits for them, and re-layouts  5.07 us
    ppermute x1, starting transfers between devices, feat_gather(): across = lax.ppermute(value, 'feat', feat_perm(1, 0))  4.94 us
  transfers between devices with their start and end apart: 34, of which 15 were waited for; matrix products, arithmetic and copies ran while one was open for 0% of the time, Pallas kernels for 4%

profile of v2, /device:TPU:2, one launch (start us, length us, event | category | flops | bytes accessed | tf_op | source)
XLA Modules:
  0.0 131.9 jit_solution(14069037261063904184)
XLA Ops:
  2.6 2.0 %collective-permute-start = (bf16[9,64,128]{2,1,0:T(8,128)(2,1)S(1)}, bf16[9,64,128]{2,1,0:T(8,128)(2,1)S(1)}, u32[]{:S(2)}, u32[]{:S(2)}) collective-permute-start(bf16[9,64,128]{2,1,0:T(8,128)(2,1)S(1)} %prep.1.p0), channel_id=1, source_target_pairs={{0,16},{8,24},{16,32},{24,40},{32,48},{40,56},{48,0},{56,8},{64,80... | collective-permute-start | bytes 442376 | tf_op jit(solution)/shard_map/ppermute | solution.py:41
  4.6 2.8 %collective-permute-start.1 = (bf16[9,64,128]{2,1,0:T(8,128)(2,1)S(1)}, bf16[9,64,128]{2,1,0:T(8,128)(2,1)S(1)}, u32[]{:S(2)}, u32[]{:S(2)}) collective-permute-start(bf16[9,64,128]{2,1,0:T(8,128)(2,1)S(1)} %prep.1.p0), channel_id=1, source_target_pairs={{0,48},{8,56},{16,0},{24,8},{32,16},{40,24},{48,32},{56,40},{64,11... | collective-permute-start | bytes 442376 | tf_op jit(solution)/shard_map/ppermute | solution.py:41
  8.0 5.7 %collective-permute-start.9 = (bf16[64,1024]{1,0:T(8,128)(2,1)}, bf16[64,1024]{1,0:T(8,128)(2,1)S(1)}, u32[]{:S(2)}, u32[]{:S(2)}) collective-permute-start(bf16[64,1024]{1,0:T(8,128)(2,1)} %up_ref.1), channel_id=1, source_target_pairs={{0,4},{1,5},{2,6},{3,7},{4,0},{5,1},{6,2},{7,3},{8,12},{9,13},{10,... | collective-permute-start | bytes 393224 | tf_op jit(solution)/shard_map/ppermute | solution.py:325
  13.7 12.5 %collective-permute-done.2.p3 = bf16[9,64,128]{2,1,0:T(8,128)(2,1)S(1)} collective-permute-done((bf16[9,64,128]{2,1,0:T(8,128)(2,1)S(1)}, bf16[9,64,128]{2,1,0:T(8,128)(2,1)S(1)}, u32[]{:S(2)}, u32[]{:S(2)}) %collective-permute-start.2) | collective-permute-done | bytes 147488 | tf_op jit(solution)/shard_map/ppermute | solution.py:41
  26.3 3.3 %collective-permute-start.8 = (bf16[33,64,128]{2,1,0:T(8,128)(2,1)S(1)}, bf16[33,64,128]{2,1,0:T(8,128)(2,1)S(1)}, u32[]{:S(2)}, u32[]{:S(2)}) collective-permute-start(bf16[33,64,128]{2,1,0:T(8,128)(2,1)S(1)} %stack.1._.rest_0_.rest_4_), channel_id=1, source_target_pairs={{0,128},{8,136},{16,144},{24,152},{32,160},{40,168},{48,176},{56,1... | collective-permute-start | bytes 1622024 | tf_op jit(solution)/shard_map/ppermute | solution.py:41
  30.3 2.6 %collective-permute-start.6 = (bf16[33,64,128]{2,1,0:T(8,128)(2,1)S(1)}, bf16[33,64,128]{2,1,0:T(8,128)(2,1)S(1)}, u32[]{:S(2)}, u32[]{:S(2)}) collective-permute-start(bf16[33,64,128]{2,1,0:T(8,128)(2,1)S(1)} %stack.1._.rest_0_.rest_4_), channel_id=1, source_target_pairs={{0,192},{8,200},{16,208},{24,216},{32,224},{40,232},{48,240},{56,2... | collective-permute-start | bytes 1622024 | tf_op jit(solution)/shard_map/ppermute | solution.py:41
  32.8 2.2 %copy-done = bf16[1,32,4,128,128]{4,3,2,1,0:T(8,128)(2,1)S(1)} copy-done((bf16[1,32,4,128,128]{4,3,2,1,0:T(8,128)(2,1)S(1)}, bf16[1,32,4,128,128]{4,3,2,1,0:T(8,128)(2,1)}, u32[]{:S(2)}) %copy-start) | copy-done | bytes 4194328
  37.2 1.6 %collective-permute-start.10 = (bf16[128,1024]{1,0:T(8,128)(2,1)S(1)}, bf16[128,1024]{1,0:T(8,128)(2,1)S(1)}, u32[]{:S(2)}, u32[]{:S(2)}) collective-permute-start(bf16[128,1024]{1,0:T(8,128)(2,1)S(1)} %get-tuple-element.38.rest_8_), channel_id=1, source_target_pairs={{0,1},{1,2},{2,3},{3,0},{4,5},{5,6},{6,7},{7,4},{8,9},{9,10},{10,1... | collective-permute-start | bytes 786440 | tf_op jit(solution)/shard_map/ppermute | solution.py:330
  39.3 5.4 %collective-permute-done.10.rest_9_ = bf16[128,1024]{1,0:T(8,128)(2,1)S(1)} collective-permute-done((bf16[128,1024]{1,0:T(8,128)(2,1)S(1)}, bf16[128,1024]{1,0:T(8,128)(2,1)S(1)}, u32[]{:S(2)}, u32[]{:S(2)}) %collective-permute-start.10) | collective-permute-done | bytes 262176 | tf_op jit(solution)/shard_map/ppermute | solution.py:330
  44.7 2.1 %collective-permute-start.12 = (bf16[128,1024]{1,0:T(8,128)(2,1)S(1)}, bf16[128,1024]{1,0:T(8,128)(2,1)S(1)}, u32[]{:S(2)}, u32[]{:S(2)}) collective-permute-start(bf16[128,1024]{1,0:T(8,128)(2,1)S(1)} %get-tuple-element.38.rest_8_), channel_id=1, source_target_pairs={{0,2},{1,3},{2,0},{3,1},{4,6},{5,7},{6,4},{7,5},{8,10},{9,11},{10,... | collective-permute-start | bytes 786440 | tf_op jit(solution)/shard_map/ppermute | solution.py:330
  46.8 5.8 %collective-permute-done.12.rest_11_ = bf16[128,1024]{1,0:T(8,128)(2,1)S(1)} collective-permute-done((bf16[128,1024]{1,0:T(8,128)(2,1)S(1)}, bf16[128,1024]{1,0:T(8,128)(2,1)S(1)}, u32[]{:S(2)}, u32[]{:S(2)}) %collective-permute-start.12) | collective-permute-done | bytes 262176 | tf_op jit(solution)/shard_map/ppermute | solution.py:330
  54.2 2.5 %agg_own.1 = (f32[8,64,128]{2,1,0:T(8,128)S(1)}, s32[4,16]{1,0:T(4,128)S(1)}) custom-call(s32[10,32]{1,0:T(8,128)S(1)} %add_add_fusion.ints_ref, bf16[33,64,128]{2,1,0:T(8,128)(2,1)S(1)} %stack.1._.rest_0_.rest_4_, bf16[33,64,128]{2,1,0:T(8,128)(2,1)S(1)} %collective-permute-done.4.rest_1_.rest_5_, ...), custom_call_target="tpu_custom_call" | custom-call | bytes 8388608 | tf_op jit(solution)/shard_map/agg_own/pallas_call | solution.py:280
  56.8 2.7 %agg_swap.1 = (bf16[64,1024]{1,0:T(8,128)(2,1)S(1)}, s32[4,16]{1,0:T(4,128)S(1)}) custom-call(s32[10,32]{1,0:T(8,128)S(1)} %add_add_fusion.ints_ref, bf16[33,64,128]{2,1,0:T(8,128)(2,1)S(1)} %collective-permute-done.3.rest_0_, bf16[33,64,128]{2,1,0:T(8,128)(2,1)S(1)} %collective-permute-done.5.rest_1_, ...), custom_call_target="tpu_custom_call" | custom-call | bytes 8388608 | tf_op jit(solution)/shard_map/agg_swap/pallas_call | solution.py:280
  59.5 4.9 %collective-permute-start.17 = (bf16[64,1024]{1,0:T(8,128)(2,1)S(1)}, bf16[64,1024]{1,0:T(8,128)(2,1)S(1)}, u32[]{:S(2)}, u32[]{:S(2)}) collective-permute-start(bf16[64,1024]{1,0:T(8,128)(2,1)S(1)} %get-tuple-element.37.rest_0_), channel_id=1, source_target_pairs={{0,4},{1,5},{2,6},{3,7},{4,0},{5,1},{6,2},{7,3},{8,12},{9,13},{10,... | collective-permute-start | bytes 393224 | tf_op jit(solution)/shard_map/ppermute | solution.py:45
  66.5 2.1 %collective-permute-start.16 = (bf16[64,1024]{1,0:T(8,128)(2,1)S(1)}, bf16[64,1024]{1,0:T(8,128)(2,1)S(1)}, u32[]{:S(2)}, u32[]{:S(2)}) collective-permute-start(bf16[64,1024]{1,0:T(8,128)(2,1)S(1)} %get-tuple-element.37.rest_0_), channel_id=1, source_target_pairs={{0,2},{1,3},{2,0},{3,1},{4,6},{5,7},{6,4},{7,5},{8,10},{9,11},{10,... | collective-permute-start | bytes 393224 | tf_op jit(solution)/shard_map/ppermute | solution.py:46
  68.6 3.5 %collective-permute-done.17.rest_4_ = bf16[64,1024]{1,0:T(8,128)(2,1)S(1)} collective-permute-done((bf16[64,1024]{1,0:T(8,128)(2,1)S(1)}, bf16[64,1024]{1,0:T(8,128)(2,1)S(1)}, u32[]{:S(2)}, u32[]{:S(2)}) %collective-permute-start.17) | collective-permute-done | bytes 131104 | tf_op jit(solution)/shard_map/ppermute | solution.py:45
  74.1 2.1 %collective-permute-start.20 = (bf16[64,1024]{1,0:T(8,128)(2,1)S(1)}, bf16[64,1024]{1,0:T(8,128)(2,1)S(1)}, u32[]{:S(2)}, u32[]{:S(2)}) collective-permute-start(bf16[64,1024]{1,0:T(8,128)(2,1)S(1)} %collective-permute-done.17.rest_4_), channel_id=1, source_target_pairs={{0,2},{1,3},{2,0},{3,1},{4,6},{5,7},{6,4},{7,5},{8,10},{9,11},{10,... | collective-permute-start | bytes 393224 | tf_op jit(solution)/shard_map/ppermute | solution.py:47
  77.0 2.9 %collective-permute-done.19.rest_6_ = bf16[64,1024]{1,0:T(8,128)(2,1)S(1)} collective-permute-done((bf16[64,1024]{1,0:T(8,128)(2,1)S(1)}, bf16[64,1024]{1,0:T(8,128)(2,1)S(1)}, u32[]{:S(2)}, u32[]{:S(2)}) %collective-permute-start.19) | collective-permute-done | bytes 131104 | tf_op jit(solution)/shard_map/ppermute | solution.py:47
  79.9 1.7 %collective-permute-done.20.rest_7_ = bf16[64,1024]{1,0:T(8,128)(2,1)S(1)} collective-permute-done((bf16[64,1024]{1,0:T(8,128)(2,1)S(1)}, bf16[64,1024]{1,0:T(8,128)(2,1)S(1)}, u32[]{:S(2)}, u32[]{:S(2)}) %collective-permute-start.20) | collective-permute-done | bytes 131104 | tf_op jit(solution)/shard_map/ppermute | solution.py:47
  81.7 4.1 %middle.1 = (bf16[64,1024]{1,0:T(8,128)(2,1)}, bf16[8,64,128]{2,1,0:T(8,128)(2,1)S(1)}) custom-call(bf16[64,1024]{1,0:T(8,128)(2,1)S(1)} %get-tuple-element.37.rest_0_, bf16[64,1024]{1,0:T(8,128)(2,1)S(1)} %collective-permute-done.14.rest_1_, bf16[64,1024]{1,0:T(8,128)(2,1)S(1)} %collective-permute-done.15.rest_2_, ...), custom_call_target="tpu_custom_call" | custom-call | bytes 16777216 | tf_op jit(solution)/shard_map/middle/pallas_call | solution.py:280
  85.8 2.7 %back_swap.1 = bf16[132,64,128]{2,1,0:T(8,128)(2,1)S(1)} custom-call(s32[10,32]{1,0:T(8,128)S(1)} %add_add_fusion.ints_ref, s32[4,16]{1,0:T(4,128)S(1)} %get-tuple-element.47.sb_ref, bf16[8,64,128]{2,1,0:T(8,128)(2,1)S(1)} %get-tuple-element.46.ga_ref.rest_8_, bf16[32,4,128,128]{3,2,1,0:T(8,128)(2,1)S(1)} %bitcast.12, bf16[512,1024]{1,0:T(8,128)(2,1)S(1)} %copy-done.2), custom_call_target="tpu_custom_call" | custom-call | bytes 8388608 | tf_op jit(solution)/shard_map/back_swap/pallas_call | solution.py:280
  88.6 2.7 %back_own.1.a = bf16[132,64,128]{2,1,0:T(8,128)(2,1)S(1)} custom-call(s32[10,32]{1,0:T(8,128)S(1)} %add_add_fusion.ints_ref, s32[4,16]{1,0:T(4,128)S(1)} %get-tuple-element.45.sb_ref, bf16[8,64,128]{2,1,0:T(8,128)(2,1)S(1)} %get-tuple-element.46.ga_ref.rest_8_, bf16[32,4,128,128]{3,2,1,0:T(8,128)(2,1)S(1)} %bitcast.13, bf16[512,1024]{1,0:T(8,128)(2,1)S(1)} %copy-done.2), custom_call_target="tpu_custom_call" | custom-call | bytes 8388608 | tf_op jit(solution)/shard_map/back_own/pallas_call | solution.py:280
  91.3 1.5 %collective-permute-done.21.b = bf16[132,64,128]{2,1,0:T(8,128)(2,1)S(1)} collective-permute-done((bf16[132,64,128]{2,1,0:T(8,128)(2,1)S(1)}, bf16[132,64,128]{2,1,0:T(8,128)(2,1)S(1)}, u32[]{:S(2)}, u32[]{:S(2)}) %collective-permute-start.21) | collective-permute-done | bytes 2162720 | tf_op jit(solution)/shard_map/ppermute | solution.py:41
  94.4 2.2 %collective-permute-start.23 = (bf16[25,64,128]{2,1,0:T(8,128)(2,1)S(1)}, bf16[25,64,128]{2,1,0:T(8,128)(2,1)S(1)}, u32[]{:S(2)}, u32[]{:S(2)}) collective-permute-start(bf16[25,64,128]{2,1,0:T(8,128)(2,1)S(1)} %get-tuple-element.50), channel_id=1, source_target_pairs={{0,192},{8,200},{16,208},{24,216},{32,224},{40,232},{48,240},{56,2... | collective-permute-start | bytes 1228808 | tf_op jit(solution)/shard_map/ppermute | solution.py:41
  97.7 3.8 %collective-permute-start.29 = (bf16[8,64,128]{2,1,0:T(8,128)(2,1)S(1)}, bf16[8,64,128]{2,1,0:T(8,128)(2,1)S(1)}, u32[]{:S(2)}, u32[]{:S(2)}) collective-permute-start(bf16[8,64,128]{2,1,0:T(8,128)(2,1)S(1)} %get-tuple-element.58), channel_id=1, source_target_pairs={{0,48},{8,56},{16,0},{24,8},{32,16},{40,24},{48,32},{56,40},{64,11... | collective-permute-start | bytes 393224 | tf_op jit(solution)/shard_map/ppermute | solution.py:41
  101.5 4.6 %collective-permute-done.22.refs_1_ = bf16[25,64,128]{2,1,0:T(8,128)(2,1)S(1)} collective-permute-done((bf16[25,64,128]{2,1,0:T(8,128)(2,1)S(1)}, bf16[25,64,128]{2,1,0:T(8,128)(2,1)S(1)}, u32[]{:S(2)}, u32[]{:S(2)}) %collective-permute-start.22) | collective-permute-done | bytes 409632 | tf_op jit(solution)/shard_map/ppermute | solution.py:41
  106.1 8.1 %collective-permute-done.23.refs_2_ = bf16[25,64,128]{2,1,0:T(8,128)(2,1)S(1)} collective-permute-done((bf16[25,64,128]{2,1,0:T(8,128)(2,1)S(1)}, bf16[25,64,128]{2,1,0:T(8,128)(2,1)S(1)}, u32[]{:S(2)}, u32[]{:S(2)}) %collective-permute-start.23) | collective-permute-done | bytes 409632 | tf_op jit(solution)/shard_map/ppermute | solution.py:41
  114.2 1.7 %collective-permute-done.24.refs_3_ = bf16[25,64,128]{2,1,0:T(8,128)(2,1)S(1)} collective-permute-done((bf16[25,64,128]{2,1,0:T(8,128)(2,1)S(1)}, bf16[25,64,128]{2,1,0:T(8,128)(2,1)S(1)}, u32[]{:S(2)}, u32[]{:S(2)}) %collective-permute-start.24) | collective-permute-done | bytes 409632 | tf_op jit(solution)/shard_map/ppermute | solution.py:41
  116.2 3.8 %collective-permute-start.26 = (bf16[7,64,128]{2,1,0:T(8,128)(2,1)S(1)}, bf16[7,64,128]{2,1,0:T(8,128)(2,1)S(1)}, u32[]{:S(2)}, u32[]{:S(2)}) collective-permute-start(bf16[7,64,128]{2,1,0:T(8,128)(2,1)S(1)} %get-tuple-element.54), channel_id=1, source_target_pairs={{0,48},{8,56},{16,0},{24,8},{32,16},{40,24},{48,32},{56,40},{64,11... | collective-permute-start | bytes 344072 | tf_op jit(solution)/shard_map/ppermute | solution.py:41
  121.4 2.1 %collective-permute-start.32 = (bf16[2,64,128]{2,1,0:T(8,128)(2,1)S(1)}, bf16[2,64,128]{2,1,0:T(8,128)(2,1)S(1)}, u32[]{:S(2)}, u32[]{:S(2)}) collective-permute-start(bf16[2,64,128]{2,1,0:T(8,128)(2,1)S(1)} %get-tuple-element.62), channel_id=1, source_target_pairs={{0,192},{8,200},{16,208},{24,216},{32,224},{40,232},{48,240},{56,2... | collective-permute-start | bytes 98312 | tf_op jit(solution)/shard_map/ppermute | solution.py:41
  123.5 1.9 %collective-permute-done.31.rest_5_ = bf16[2,64,128]{2,1,0:T(8,128)(2,1)S(1)} collective-permute-done((bf16[2,64,128]{2,1,0:T(8,128)(2,1)S(1)}, bf16[2,64,128]{2,1,0:T(8,128)(2,1)S(1)}, u32[]{:S(2)}, u32[]{:S(2)}) %collective-permute-start.31) | collective-permute-done | bytes 32800 | tf_op jit(solution)/shard_map/ppermute | solution.py:41
  125.4 5.4 %collective-permute-done.33.rest_7_ = bf16[2,64,128]{2,1,0:T(8,128)(2,1)S(1)} collective-permute-done((bf16[2,64,128]{2,1,0:T(8,128)(2,1)S(1)}, bf16[2,64,128]{2,1,0:T(8,128)(2,1)S(1)}, u32[]{:S(2)}, u32[]{:S(2)}) %collective-permute-start.33) | collective-permute-done | bytes 32800 | tf_op jit(solution)/shard_map/ppermute | solution.py:41
  (67 shorter events, 17.8 us)
Async XLA Ops:
  2.6 11.1 %collective-permute-start = (bf16[9,64,128]{2,1,0:T(8,128)(2,1)S(1)}, bf16[9,64,128]{2,1,0:T(8,128)(2,1)S(1)}, u32[]{:S(2)}, u32[]{:S(2)}) collective-permute-start(bf16[9,64,128]{2,1,0:T(8,128)(2,1)S(1)} %prep.1.p0), channel_id=1, source_target_pairs={{0,16},{8,24},{16,32},{24,40},{32,48},{40,56},{48,0},{56,8},{64,80... | collective-permute-start | bytes 442376 | tf_op jit(solution)/shard_map/ppermute | solution.py:41
  4.6 9.1 %collective-permute-start.1 = (bf16[9,64,128]{2,1,0:T(8,128)(2,1)S(1)}, bf16[9,64,128]{2,1,0:T(8,128)(2,1)S(1)}, u32[]{:S(2)}, u32[]{:S(2)}) collective-permute-start(bf16[9,64,128]{2,1,0:T(8,128)(2,1)S(1)} %prep.1.p0), channel_id=1, source_target_pairs={{0,48},{8,56},{16,0},{24,8},{32,16},{40,24},{48,32},{56,40},{64,11... | collective-permute-start | bytes 442376 | tf_op jit(solution)/shard_map/ppermute | solution.py:41
  7.4 18.9 %collective-permute-start.2 = (bf16[9,64,128]{2,1,0:T(8,128)(2,1)S(1)}, bf16[9,64,128]{2,1,0:T(8,128)(2,1)S(1)}, u32[]{:S(2)}, u32[]{:S(2)}) collective-permute-start(bf16[9,64,128]{2,1,0:T(8,128)(2,1)S(1)} %prep.1.p0), channel_id=1, source_target_pairs={{0,32},{8,40},{16,48},{24,56},{32,0},{40,8},{48,16},{56,24},{64,96... | collective-permute-start | bytes 442376 | tf_op jit(solution)/shard_map/ppermute | solution.py:41
  8.0 24.8 %collective-permute-start.9 = (bf16[64,1024]{1,0:T(8,128)(2,1)}, bf16[64,1024]{1,0:T(8,128)(2,1)S(1)}, u32[]{:S(2)}, u32[]{:S(2)}) collective-permute-start(bf16[64,1024]{1,0:T(8,128)(2,1)} %up_ref.1), channel_id=1, source_target_pairs={{0,4},{1,5},{2,6},{3,7},{4,0},{5,1},{6,2},{7,3},{8,12},{9,13},{10,... | collective-permute-start | bytes 393224 | tf_op jit(solution)/shard_map/ppermute | solution.py:325
  26.3 26.3 %collective-permute-start.8 = (bf16[33,64,128]{2,1,0:T(8,128)(2,1)S(1)}, bf16[33,64,128]{2,1,0:T(8,128)(2,1)S(1)}, u32[]{:S(2)}, u32[]{:S(2)}) collective-permute-start(bf16[33,64,128]{2,1,0:T(8,128)(2,1)S(1)} %stack.1._.rest_0_.rest_4_), channel_id=1, source_target_pairs={{0,128},{8,136},{16,144},{24,152},{32,160},{40,168},{48,176},{56,1... | collective-permute-start | bytes 1622024 | tf_op jit(solution)/shard_map/ppermute | solution.py:41
  29.6 24.1 %collective-permute-start.4 = (bf16[33,64,128]{2,1,0:T(8,128)(2,1)S(1)}, bf16[33,64,128]{2,1,0:T(8,128)(2,1)S(1)}, u32[]{:S(2)}, u32[]{:S(2)}) collective-permute-start(bf16[33,64,128]{2,1,0:T(8,128)(2,1)S(1)} %stack.1._.rest_0_.rest_4_), channel_id=1, source_target_pairs={{0,64},{8,72},{16,80},{24,88},{32,96},{40,104},{48,112},{56,120},{... | collective-permute-start | bytes 1622024 | tf_op jit(solution)/shard_map/ppermute | solution.py:41
  30.3 23.8 %collective-permute-start.6 = (bf16[33,64,128]{2,1,0:T(8,128)(2,1)S(1)}, bf16[33,64,128]{2,1,0:T(8,128)(2,1)S(1)}, u32[]{:S(2)}, u32[]{:S(2)}) collective-permute-start(bf16[33,64,128]{2,1,0:T(8,128)(2,1)S(1)} %stack.1._.rest_0_.rest_4_), channel_id=1, source_target_pairs={{0,192},{8,200},{16,208},{24,216},{32,224},{40,232},{48,240},{56,2... | collective-permute-start | bytes 1622024 | tf_op jit(solution)/shard_map/ppermute | solution.py:41
  37.2 7.5 %collective-permute-start.10 = (bf16[128,1024]{1,0:T(8,128)(2,1)S(1)}, bf16[128,1024]{1,0:T(8,128)(2,1)S(1)}, u32[]{:S(2)}, u32[]{:S(2)}) collective-permute-start(bf16[128,1024]{1,0:T(8,128)(2,1)S(1)} %get-tuple-element.38.rest_8_), channel_id=1, source_target_pairs={{0,1},{1,2},{2,3},{3,0},{4,5},{5,6},{6,7},{7,4},{8,9},{9,10},{10,1... | collective-permute-start | bytes 786440 | tf_op jit(solution)/shard_map/ppermute | solution.py:330
  38.8 8.0 %collective-permute-start.11 = (bf16[128,1024]{1,0:T(8,128)(2,1)S(1)}, bf16[128,1024]{1,0:T(8,128)(2,1)S(1)}, u32[]{:S(2)}, u32[]{:S(2)}) collective-permute-start(bf16[128,1024]{1,0:T(8,128)(2,1)S(1)} %get-tuple-element.38.rest_8_), channel_id=1, source_target_pairs={{0,3},{1,0},{2,1},{3,2},{4,7},{5,4},{6,5},{7,6},{8,11},{9,8},{10,9... | collective-permute-start | bytes 786440 | tf_op jit(solution)/shard_map/ppermute | solution.py:330
  44.7 8.0 %collective-permute-start.12 = (bf16[128,1024]{1,0:T(8,128)(2,1)S(1)}, bf16[128,1024]{1,0:T(8,128)(2,1)S(1)}, u32[]{:S(2)}, u32[]{:S(2)}) collective-permute-start(bf16[128,1024]{1,0:T(8,128)(2,1)S(1)} %get-tuple-element.38.rest_8_), channel_id=1, source_target_pairs={{0,2},{1,3},{2,0},{3,1},{4,6},{5,7},{6,4},{7,5},{8,10},{9,11},{10,... | collective-permute-start | bytes 786440 | tf_op jit(solution)/shard_map/ppermute | solution.py:330
  46.8 10.0 %collective-permute-start.3 = (bf16[33,64,128]{2,1,0:T(8,128)(2,1)S(1)}, bf16[33,64,128]{2,1,0:T(8,128)(2,1)S(1)}, u32[]{:S(2)}, u32[]{:S(2)}) collective-permute-start(bf16[33,64,128]{2,1,0:T(8,128)(2,1)S(1)} %stack.1._.rest_0_.rest_4_), channel_id=1, source_target_pairs={{0,8},{8,0},{16,24},{24,16},{32,40},{40,32},{48,56},{56,48},{64,72... | collective-permute-start | bytes 1622024 | tf_op jit(solution)/shard_map/ppermute | solution.py:41
  52.6 4.1 %collective-permute-start.13 = (bf16[33,64,128]{2,1,0:T(8,128)(2,1)S(1)}, bf16[33,64,128]{2,1,0:T(8,128)(2,1)S(1)}, u32[]{:S(2)}, u32[]{:S(2)}) collective-permute-start(bf16[33,64,128]{2,1,0:T(8,128)(2,1)S(1)} %collective-permute-done.8.rest_3_.rest_7_), channel_id=1, source_target_pairs={{0,8},{8,0},{16,24},{24,16},{32,40},{40,32},{48,56},{56,48},{64,72... | collective-permute-start | bytes 1622024 | tf_op jit(solution)/shard_map/ppermute | solution.py:41
  59.5 12.6 %collective-permute-start.17 = (bf16[64,1024]{1,0:T(8,128)(2,1)S(1)}, bf16[64,1024]{1,0:T(8,128)(2,1)S(1)}, u32[]{:S(2)}, u32[]{:S(2)}) collective-permute-start(bf16[64,1024]{1,0:T(8,128)(2,1)S(1)} %get-tuple-element.37.rest_0_), channel_id=1, source_target_pairs={{0,4},{1,5},{2,6},{3,7},{4,0},{5,1},{6,2},{7,3},{8,12},{9,13},{10,... | collective-permute-start | bytes 393224 | tf_op jit(solution)/shard_map/ppermute | solution.py:45
  64.4 9.7 %collective-permute-start.14 = (bf16[64,1024]{1,0:T(8,128)(2,1)S(1)}, bf16[64,1024]{1,0:T(8,128)(2,1)S(1)}, u32[]{:S(2)}, u32[]{:S(2)}) collective-permute-start(bf16[64,1024]{1,0:T(8,128)(2,1)S(1)} %get-tuple-element.37.rest_0_), channel_id=1, source_target_pairs={{0,1},{1,2},{2,3},{3,0},{4,5},{5,6},{6,7},{7,4},{8,9},{9,10},{10,1... | collective-permute-start | bytes 393224 | tf_op jit(solution)/shard_map/ppermute | solution.py:46
  65.9 10.3 %collective-permute-start.15 = (bf16[64,1024]{1,0:T(8,128)(2,1)S(1)}, bf16[64,1024]{1,0:T(8,128)(2,1)S(1)}, u32[]{:S(2)}, u32[]{:S(2)}) collective-permute-start(bf16[64,1024]{1,0:T(8,128)(2,1)S(1)} %get-tuple-element.37.rest_0_), channel_id=1, source_target_pairs={{0,3},{1,0},{2,1},{3,2},{4,7},{5,4},{6,5},{7,6},{8,11},{9,8},{10,9... | collective-permute-start | bytes 393224 | tf_op jit(solution)/shard_map/ppermute | solution.py:46
  66.5 9.8 %collective-permute-start.16 = (bf16[64,1024]{1,0:T(8,128)(2,1)S(1)}, bf16[64,1024]{1,0:T(8,128)(2,1)S(1)}, u32[]{:S(2)}, u32[]{:S(2)}) collective-permute-start(bf16[64,1024]{1,0:T(8,128)(2,1)S(1)} %get-tuple-element.37.rest_0_), channel_id=1, source_target_pairs={{0,2},{1,3},{2,0},{3,1},{4,6},{5,7},{6,4},{7,5},{8,10},{9,11},{10,... | collective-permute-start | bytes 393224 | tf_op jit(solution)/shard_map/ppermute | solution.py:46
  72.1 5.0 %collective-permute-start.18 = (bf16[64,1024]{1,0:T(8,128)(2,1)S(1)}, bf16[64,1024]{1,0:T(8,128)(2,1)S(1)}, u32[]{:S(2)}, u32[]{:S(2)}) collective-permute-start(bf16[64,1024]{1,0:T(8,128)(2,1)S(1)} %collective-permute-done.17.rest_4_), channel_id=1, source_target_pairs={{0,1},{1,2},{2,3},{3,0},{4,5},{5,6},{6,7},{7,4},{8,9},{9,10},{10,1... | collective-permute-start | bytes 393224 | tf_op jit(solution)/shard_map/ppermute | solution.py:47
  73.6 6.4 %collective-permute-start.19 = (bf16[64,1024]{1,0:T(8,128)(2,1)S(1)}, bf16[64,1024]{1,0:T(8,128)(2,1)S(1)}, u32[]{:S(2)}, u32[]{:S(2)}) collective-permute-start(bf16[64,1024]{1,0:T(8,128)(2,1)S(1)} %collective-permute-done.17.rest_4_), channel_id=1, source_target_pairs={{0,3},{1,0},{2,1},{3,2},{4,7},{5,4},{6,5},{7,6},{8,11},{9,8},{10,9... | collective-permute-start | bytes 393224 | tf_op jit(solution)/shard_map/ppermute | solution.py:47
  74.1 7.6 %collective-permute-start.20 = (bf16[64,1024]{1,0:T(8,128)(2,1)S(1)}, bf16[64,1024]{1,0:T(8,128)(2,1)S(1)}, u32[]{:S(2)}, u32[]{:S(2)}) collective-permute-start(bf16[64,1024]{1,0:T(8,128)(2,1)S(1)} %collective-permute-done.17.rest_4_), channel_id=1, source_target_pairs={{0,2},{1,3},{2,0},{3,1},{4,6},{5,7},{6,4},{7,5},{8,10},{9,11},{10,... | collective-permute-start | bytes 393224 | tf_op jit(solution)/shard_map/ppermute | solution.py:47
  88.5 4.3 %collective-permute-start.21 = (bf16[132,64,128]{2,1,0:T(8,128)(2,1)S(1)}, bf16[132,64,128]{2,1,0:T(8,128)(2,1)S(1)}, u32[]{:S(2)}, u32[]{:S(2)}) collective-permute-start(bf16[132,64,128]{2,1,0:T(8,128)(2,1)S(1)} %back_swap.1), channel_id=1, source_target_pairs={{0,8},{8,0},{16,24},{24,16},{32,40},{40,32},{48,56},{56,48},{64,72... | collective-permute-start | bytes 6488072 | tf_op jit(solution)/shard_map/ppermute | solution.py:41
  93.3 12.8 %collective-permute-start.22 = (bf16[25,64,128]{2,1,0:T(8,128)(2,1)S(1)}, bf16[25,64,128]{2,1,0:T(8,128)(2,1)S(1)}, u32[]{:S(2)}, u32[]{:S(2)}) collective-permute-start(bf16[25,64,128]{2,1,0:T(8,128)(2,1)S(1)} %get-tuple-element.49), channel_id=1, source_target_pairs={{0,64},{8,72},{16,80},{24,88},{32,96},{40,104},{48,112},{56,120},{... | collective-permute-start | bytes 1228808 | tf_op jit(solution)/shard_map/ppermute | solution.py:41
  94.4 19.8 %collective-permute-start.23 = (bf16[25,64,128]{2,1,0:T(8,128)(2,1)S(1)}, bf16[25,64,128]{2,1,0:T(8,128)(2,1)S(1)}, u32[]{:S(2)}, u32[]{:S(2)}) collective-permute-start(bf16[25,64,128]{2,1,0:T(8,128)(2,1)S(1)} %get-tuple-element.50), channel_id=1, source_target_pairs={{0,192},{8,200},{16,208},{24,216},{32,224},{40,232},{48,240},{56,2... | collective-permute-start | bytes 1228808 | tf_op jit(solution)/shard_map/ppermute | solution.py:41
  96.7 19.3 %collective-permute-start.24 = (bf16[25,64,128]{2,1,0:T(8,128)(2,1)S(1)}, bf16[25,64,128]{2,1,0:T(8,128)(2,1)S(1)}, u32[]{:S(2)}, u32[]{:S(2)}) collective-permute-start(bf16[25,64,128]{2,1,0:T(8,128)(2,1)S(1)} %get-tuple-element.51), channel_id=1, source_target_pairs={{0,128},{8,136},{16,144},{24,152},{32,160},{40,168},{48,176},{56,1... | collective-permute-start | bytes 1228808 | tf_op jit(solution)/shard_map/ppermute | solution.py:41
  97.7 22.4 %collective-permute-start.28 = (bf16[8,64,128]{2,1,0:T(8,128)(2,1)S(1)}, bf16[8,64,128]{2,1,0:T(8,128)(2,1)S(1)}, u32[]{:S(2)}, u32[]{:S(2)}) collective-permute-start(bf16[8,64,128]{2,1,0:T(8,128)(2,1)S(1)} %get-tuple-element.57), channel_id=1, source_target_pairs={{0,16},{8,24},{16,32},{24,40},{32,48},{40,56},{48,0},{56,8},{64,80... | collective-permute-start | bytes 393224 | tf_op jit(solution)/shard_map/ppermute | solution.py:41
  97.7 22.4 %collective-permute-start.29 = (bf16[8,64,128]{2,1,0:T(8,128)(2,1)S(1)}, bf16[8,64,128]{2,1,0:T(8,128)(2,1)S(1)}, u32[]{:S(2)}, u32[]{:S(2)}) collective-permute-start(bf16[8,64,128]{2,1,0:T(8,128)(2,1)S(1)} %get-tuple-element.58), channel_id=1, source_target_pairs={{0,48},{8,56},{16,0},{24,8},{32,16},{40,24},{48,32},{56,40},{64,11... | collective-permute-start | bytes 393224 | tf_op jit(solution)/shard_map/ppermute | solution.py:41
  106.1 13.9 %collective-permute-start.30 = (bf16[8,64,128]{2,1,0:T(8,128)(2,1)S(1)}, bf16[8,64,128]{2,1,0:T(8,128)(2,1)S(1)}, u32[]{:S(2)}, u32[]{:S(2)}) collective-permute-start(bf16[8,64,128]{2,1,0:T(8,128)(2,1)S(1)} %get-tuple-element.59), channel_id=1, source_target_pairs={{0,32},{8,40},{16,48},{24,56},{32,0},{40,8},{48,16},{56,24},{64,96... | collective-permute-start | bytes 393224 | tf_op jit(solution)/shard_map/ppermute | solution.py:41
  116.1 14.6 %collective-permute-start.25 = (bf16[7,64,128]{2,1,0:T(8,128)(2,1)S(1)}, bf16[7,64,128]{2,1,0:T(8,128)(2,1)S(1)}, u32[]{:S(2)}, u32[]{:S(2)}) collective-permute-start(bf16[7,64,128]{2,1,0:T(8,128)(2,1)S(1)} %get-tuple-element.53), channel_id=1, source_target_pairs={{0,16},{8,24},{16,32},{24,40},{32,48},{40,56},{48,0},{56,8},{64,80... | collective-permute-start | bytes 344072 | tf_op jit(solution)/shard_map/ppermute | solution.py:41
  116.2 14.5 %collective-permute-start.26 = (bf16[7,64,128]{2,1,0:T(8,128)(2,1)S(1)}, bf16[7,64,128]{2,1,0:T(8,128)(2,1)S(1)}, u32[]{:S(2)}, u32[]{:S(2)}) collective-permute-start(bf16[7,64,128]{2,1,0:T(8,128)(2,1)S(1)} %get-tuple-element.54), channel_id=1, source_target_pairs={{0,48},{8,56},{16,0},{24,8},{32,16},{40,24},{48,32},{56,40},{64,11... | collective-permute-start | bytes 344072 | tf_op jit(solution)/shard_map/ppermute | solution.py:41
  120.1 10.7 %collective-permute-start.27 = (bf16[7,64,128]{2,1,0:T(8,128)(2,1)S(1)}, bf16[7,64,128]{2,1,0:T(8,128)(2,1)S(1)}, u32[]{:S(2)}, u32[]{:S(2)}) collective-permute-start(bf16[7,64,128]{2,1,0:T(8,128)(2,1)S(1)} %get-tuple-element.55), channel_id=1, source_target_pairs={{0,32},{8,40},{16,48},{24,56},{32,0},{40,8},{48,16},{56,24},{64,96... | collective-permute-start | bytes 344072 | tf_op jit(solution)/shard_map/ppermute | solution.py:41
  120.1 5.2 %collective-permute-start.31 = (bf16[2,64,128]{2,1,0:T(8,128)(2,1)S(1)}, bf16[2,64,128]{2,1,0:T(8,128)(2,1)S(1)}, u32[]{:S(2)}, u32[]{:S(2)}) collective-permute-start(bf16[2,64,128]{2,1,0:T(8,128)(2,1)S(1)} %get-tuple-element.61), channel_id=1, source_target_pairs={{0,64},{8,72},{16,80},{24,88},{32,96},{40,104},{48,112},{56,120},{... | collective-permute-start | bytes 98312 | tf_op jit(solution)/shard_map/ppermute | solution.py:41
  121.4 4.0 %collective-permute-start.32 = (bf16[2,64,128]{2,1,0:T(8,128)(2,1)S(1)}, bf16[2,64,128]{2,1,0:T(8,128)(2,1)S(1)}, u32[]{:S(2)}, u32[]{:S(2)}) collective-permute-start(bf16[2,64,128]{2,1,0:T(8,128)(2,1)S(1)} %get-tuple-element.62), channel_id=1, source_target_pairs={{0,192},{8,200},{16,208},{24,216},{32,224},{40,232},{48,240},{56,2... | collective-permute-start | bytes 98312 | tf_op jit(solution)/shard_map/ppermute | solution.py:41
  125.4 5.4 %collective-permute-start.33 = (bf16[2,64,128]{2,1,0:T(8,128)(2,1)S(1)}, bf16[2,64,128]{2,1,0:T(8,128)(2,1)S(1)}, u32[]{:S(2)}, u32[]{:S(2)}) collective-permute-start(bf16[2,64,128]{2,1,0:T(8,128)(2,1)S(1)} %get-tuple-element.63), channel_id=1, source_target_pairs={{0,128},{8,136},{16,144},{24,152},{32,160},{40,168},{48,176},{56,1... | collective-permute-start | bytes 98312 | tf_op jit(solution)/shard_map/ppermute | solution.py:41
  (11 other events, 124.4 us)

commit v3 on v2

--- a/solution.py
+++ b/solution.py
@@ -17,6 +17,7 @@
 STEPS = (0, 1, 3, 2)
 BACK = (0, 2, 1, 3)
 NY, NZ, NC = 4, 4, 2
+EARLY = False
 LIVE = 33
 NA = 6
 NB = 8 - NA
@@ -101,86 +102,92 @@
     out_ref[32] = extra.astype(BF)
 
 
-def pair_kernel(up_ref, far_ref, w_ref, tiles_ref, _, pair_ref, wt_ref, own_ref):
-    pair_ref[0:64, :] = up_ref[...]
-    pair_ref[64:128, :] = far_ref[...]
-    wt_ref[...] = w_ref[...].T
-    own_ref[...] = w_ref[pl.ds(pl.multiple_of(lax.axis_index("feat") * 64, 64), 64), :]
-
-
-def slot_sums(swap, ints_ref, srcs, tiles_ref, sb_ref, acc, ids_v, ids_s, sem):
-    y, z, c = here()
-    me = (y * 4 + z) * 2 + c
-    cc = 1 - c if swap else c
-    row = lax.broadcasted_iota(jnp.int32, (64, 128), 0)
-    ids_v[...] = jnp.zeros_like(ids_v)
-    for j in range(4):
-        mine = jnp.where(row == me, srcs[j][32].astype(F32), 0.0)
-        ids_v[j : j + 1, :] = jnp.sum(mine, axis=0, keepdims=True).astype(jnp.int32)
-    copy = pltpu.make_async_copy(ids_v, ids_s, sem)
-    copy.start()
-    copy.wait()
-    for j in range(4):
-        sy = behind(y, STEPS[j])
-        for i in range(4):
-            sz = behind(z, STEPS[i])
-            s = (sy * 4 + sz) * 2 + cc
-            count = ints_ref[8, s]
-            parts = []
-            for k in range(4):
-                b = ids_s[j, (sz * 2 + 1 - cc) * 16 + k]
-                sb_ref[sy, sz * 4 + k] = b
-                parts.append(dot(srcs[j][i * 8 + b], tiles_ref[s, k]))
-            for k in range(4):
-                t = jnp.where(k < count, ints_ref[4 + k, s], 8)
-                acc[t] += parts[k]
-
-
-def agg_own_kernel(ints_ref, *rest):
-    srcs = rest[:4]
-    tiles_ref, out_ref, sb_ref, acc, *scratch = rest[4:]
-    acc[...] = jnp.zeros_like(acc)
-    slot_sums(False, ints_ref, srcs, tiles_ref, sb_ref, acc, *scratch)
-    out_ref[...] = acc[0:8]
-
-
-def agg_swap_kernel(ints_ref, *rest):
-    srcs, owns = rest[:4], rest[4:8]
-    tiles_ref, adj_ref, x_ref, self_ref, sum_ref, out_ref, sb_ref, acc, *scratch = rest[8:]
-    y, _, c = here()
-    acc[0:8] = sum_ref[...]
-    acc[8] = jnp.zeros((64, 128), F32)
-    slot_sums(True, ints_ref, srcs, tiles_ref, sb_ref, acc, *scratch)
-    side = lax.rem(lax.div(lax.broadcasted_iota(jnp.int32, (64, 128), 1), 16), 2)
-    hub = jnp.zeros((64, 1024), F32)
-    for j in range(4):
-        sy = behind(y, STEPS[j])
-        both = jnp.where(side == c, owns[j][32].astype(F32), srcs[j][32].astype(F32)).astype(BF)
-        hub = hub + dot(both, adj_ref[pl.ds(pl.multiple_of(sy * 128, 128), 128), :])
-    for b in range(8):
-        cols = slice(b * 128, (b + 1) * 128)
-        total = x_ref[:, cols].astype(F32) * self_ref[:, cols] + hub[:, cols] + acc[b]
-        out_ref[:, cols] = total.astype(BF)
-
-
-def mid_kernel(*rest):
-    aggs = rest[:8]
-    ups = rest[8:12]
-    wt_ref, own_ref, act_ref, ga_ref, full, pre, down = rest[12:]
+def group_rows():
     group = lax.axis_index("feat")
     h, x = lax.div(group, 4), lax.rem(group, 4)
     first = []
     for j in range(8):
         hh = h if j < 4 else 1 - h
         first.append(pl.multiple_of((hh * 4 + behind(x, STEPS[j % 4])) * 64, 64))
+    return first
+
+
+def pair_kernel(up_ref, far_ref, w_ref, tiles_ref, _, pair_ref, wt_ref, own_ref, held):
+    pair_ref[0:64, :] = up_ref[...]
+    pair_ref[64:128, :] = far_ref[...]
+    first = group_rows()
     for j in range(8):
-        full[pl.ds(first[j], 64), :] = aggs[j][...]
-    own = own_ref[...]
+        held[j * 64 : (j + 1) * 64, :] = w_ref[pl.ds(first[j], 64), :]
+    held[...] = held[...].T
+    for j in range(8):
+        wt_ref[j * 64 : (j + 1) * 64, :] = held[pl.ds(first[j], 64), :]
+    own_ref[...] = wt_ref[:, 0:128].T
+
+
+def agg_kernel(part, ints_ref, *rest):
+    owns, swaps = rest[:2], rest[2:4]
+    if part == 0:
+        tiles_ref, adj_ref, x_ref, self_ref, out_ref, sb_ref, acc, ids_v, ids_s, sem = rest[4:]
+    else:
+        tiles_ref, adj_ref, sum_ref, out_ref, sb_ref, acc, ids_v, ids_s, sem = rest[4:]
+    y, z, c = here()
+    me = (y * 4 + z) * 2 + c
+    row = lax.broadcasted_iota(jnp.int32, (64, 128), 0)
+    ids_v[...] = jnp.zeros_like(ids_v)
+    for n, src in enumerate((*owns, *swaps)):
+        mine = jnp.where(row == me, src[32].astype(F32), 0.0)
+        ids_v[n : n + 1, :] = jnp.sum(mine, axis=0, keepdims=True).astype(jnp.int32)
+    copy = pltpu.make_async_copy(ids_v, ids_s, sem)
+    copy.start()
+    side = lax.rem(lax.div(lax.broadcasted_iota(jnp.int32, (64, 128), 1), 16), 2)
+    hub = jnp.zeros((64, 1024), F32)
+    for n in range(2):
+        sy = behind(y, STEPS[part * 2 + n])
+        both = jnp.where(side == c, owns[n][32].astype(F32), swaps[n][32].astype(F32)).astype(BF)
+        hub = hub + dot(both, adj_ref[pl.ds(pl.multiple_of(sy * 128, 128), 128), :])
+    for b in range(8):
+        cols = slice(b * 128, (b + 1) * 128)
+        if part == 0:
+            acc[b] = x_ref[:, cols].astype(F32) * self_ref[:, cols] + hub[:, cols]
+        else:
+            acc[b] = sum_ref[b] + hub[:, cols]
+    acc[8] = jnp.zeros((64, 128), F32)
+    copy.wait()
+    for m, srcs in enumerate((owns, swaps)):
+        cc = 1 - c if m else c
+        for n in range(2):
+            sy = behind(y, STEPS[part * 2 + n])
+            for i in range(4):
+                sz = behind(z, STEPS[i])
+                s = (sy * 4 + sz) * 2 + cc
+                count = ints_ref[8, s]
+                parts = []
+                for k in range(4):
+                    b = ids_s[m * 2 + n, (sz * 2 + 1 - cc) * 16 + k]
+                    sb_ref[m * 2 + n, sz * 4 + k] = b
+                    parts.append(dot(srcs[n][i * 8 + b], tiles_ref[s, k]))
+                for k in range(4):
+                    t = jnp.where(k < count, ints_ref[4 + k, s], 8)
+                    acc[t] += parts[k]
+    if part == 0:
+        out_ref[...] = acc[0:8]
+    else:
+        for b in range(8):
+            out_ref[:, b * 128 : (b + 1) * 128] = acc[b].astype(BF)
+
+
+def mid_kernel(*rest):
+    aggs, ups = rest[:8], rest[8:12]
+    wt_ref, own_ref, adj_ref, act_ref, ga_ref, hub_ref, full, pre, down = rest[12:]
+    hubs = jnp.zeros((64, 512), F32)
+    for j in range(8):
+        full[j * 64 : (j + 1) * 64, :] = aggs[j][...]
     for n in range(4):
         cols = slice(n * 256, (n + 1) * 256)
-        pre[...] = dot(wt_ref[...], full[:, cols])
+        pre[n % 2] = dot(wt_ref[...], full[:, cols])
         for j in range(8):
-            v = pre[pl.ds(first[j], 64), :]
+            rows = slice(j * 64, (j + 1) * 64)
+            v = pre[n % 2, rows]
             sq = v * v
             t = jnp.tanh(v * (0.7978845608 + (0.7978845608 * 0.044715) * sq))
             half = 0.5 + 0.5 * t
@@ -190,48 +197,66 @@
                 0.7978845608 + (0.7978845608 * 3 * 0.044715) * sq
             )
             up = ups[j % 4][(j // 4) * 64 : (j // 4 + 1) * 64, cols]
-            down[pl.ds(first[j], 64), :] = (up.astype(F32) * slope).astype(BF)
-        grads = dot(own, down[...]).astype(BF)
+            down[n % 2, rows] = (up.astype(F32) * slope).astype(BF)
+        grads = dot(own_ref[0:64, :], down[n % 2]).astype(BF)
         ga_ref[2 * n] = grads[:, :128]
         ga_ref[2 * n + 1] = grads[:, 128:]
-
-
-def back_kernel(swap, ints_ref, sb_ref, ga_ref, tiles_ref, adj_ref, out, acc):
+        hubs = hubs + dot_nt(grads, adj_ref[:, cols])
+    for j in range(4):
+        hub_ref[j] = hubs[:, j * 128 : (j + 1) * 128]
+
+
+GROUPS = ((1, 3), (0, 2))
+
+
+def back_kernel(swap, part, ints_ref, sb0_ref, sb1_ref, ga_ref, tiles_ref, hub_ref, *rest):
+    out, acc = rest[-2:]
     y, z, c = here()
     cc = 1 - c if swap else c
-    for j in range(4):
+    none = jnp.zeros((64, 128), BF)
+    for g, j in enumerate(GROUPS[part]):
         sy = ahead(y, STEPS[j])
-        hubs = jnp.zeros((64, 128), F32)
-        at = pl.ds(pl.multiple_of(sy * 128, 128), 128)
-        for b in range(8):
-            hubs = hubs + dot_nt(ga_ref[b], adj_ref[at, b * 128 : (b + 1) * 128])
-        out[128 + j] = hubs.astype(BF)
+        sb_ref = (sb0_ref, sb1_ref)[BACK[j] // 2]
+        sb_row = (2 if swap else 0) + BACK[j] % 2
+        out[64 + g] = hub_ref[sy].astype(BF)
         for i in range(4):
             sz = ahead(z, STEPS[i])
             s = (sy * 4 + sz) * 2 + cc
             count = ints_ref[8, s]
             acc[0:8] = jnp.zeros((8, 64, 128), F32)
-            parts = [dot_nt(ga_ref[ints_ref[4 + k, s]], tiles_ref[s, k]) for k in range(4)]
+            parts = []
+            for k in (0, 2):
+                one, two = (ga_ref[ints_ref[4 + k + n, s]] for n in range(2))
+                rows = [jnp.concatenate([one, none], axis=1), jnp.concatenate([none, two], axis=1)]
+                pair = jnp.concatenate([tiles_ref[s, k], tiles_ref[s, k + 1]], axis=1)
+                sums = dot_nt(jnp.concatenate(rows, axis=0), pair)
+                parts += [sums[:64], sums[64:]]
             for k in range(4):
-                b = jnp.where(k < count, sb_ref[sy, sz * 4 + k], 8)
+                b = jnp.where(k < count, sb_ref[sb_row, sz * 4 + k], 8)
                 acc[b] += parts[k]
-            n = (j * 4 + i) * 8
+            n = (g * 4 + i) * 8
             out[n : n + 8] = acc[0:8].astype(BF)
 
 
-def add_kernel(a, b, *outs):
-    def both(n):
-        return (a[n].astype(F32) + b[n].astype(F32)).astype(BF)
-
-    for j in range(4):
+def both(a, b, n):
+    return (a[n].astype(F32) + b[n].astype(F32)).astype(BF)
+
+
+def add_first_kernel(a, b, *outs):
+    for g in range(2):
         for i in range(4):
-            for r in range(8):
-                total = both((j * 4 + i) * 8 + r)
-                if r < NA:
-                    outs[j][i * NA + r] = total
-                else:
-                    outs[4 + i][j * NB + r - NA] = total
-        outs[j][4 * NA] = both(128 + j)
+            for r in range(NA):
+                outs[g][i * NA + r] = both(a, b, (g * 4 + i) * 8 + r)
+        outs[g][4 * NA] = both(a, b, 64 + g)
+
+
+def add_second_kernel(a0, b0, a, b, *outs):
+    add_first_kernel(a, b, *outs[:2])
+    for part, (p, q) in enumerate(((a0, b0), (a, b))):
+        for g, j in enumerate(GROUPS[part]):
+            for i in range(4):
+                for r in range(NB):
+                    outs[2 + i][j * NB + r] = both(p, q, (g * 4 + i) * 8 + NA + r)
 
 
 def four(refs, r):
@@ -321,16 +346,12 @@
     ps = [p0] + [row_send(p0, 0, k, 0) for k in STEPS[1:]]
     (s0,) = call(stack_kernel, "stack", [shape(LIVE)], ps)
     owns = [s0] + [row_send(s0, k, 0, 0) for k in STEPS[1:]]
-    up, _ = lax.optimization_barrier((grad_out, p0))
+    up, _ = lax.optimization_barrier((grad_out, s0))
     up_far = lax.ppermute(up, "feat", feat_perm(1, 0))
     pair, wt, own = call(
-        pair_kernel, "pair", [((128, 1024), BF), ((512, 512), BF), ((64, 512), BF)],
-        (grad_out, up_far, weight, tiles, s0), 0, (), 12, loose=1,
-    )
-    ups = [pair] + [lax.ppermute(pair, "feat", feat_perm(0, k)) for k in STEPS[1:]]
-    late = lax.optimization_barrier((owns[3], *ups))
-    owns[3], ups = late[0], late[1:]
-    swaps = [row_send(v, 0, 0, 1) for v in owns]
+        pair_kernel, "pair", [((128, 1024), BF), ((512, 512), BF), ((128, 512), BF)],
+        (grad_out, up_far, weight, tiles, s0), 0, [pltpu.VMEM((512, 512), BF)], 12, loose=1,
+    )
     slots = [
         pltpu.VMEM((9, 64, 128), F32),
         pltpu.VMEM((8, 128), jnp.int32),
@@ -338,35 +359,52 @@
         pltpu.SemaphoreType.DMA,
     ]
     listed = ((4, 16), jnp.int32)
-    part, sb_own = call(
-        agg_own_kernel, "agg_own", [((8, 64, 128), F32), listed],
-        (ints, *owns, tiles), 1, slots, 16, [VM, SM], 8 * MIB,
-    )
-    agg, sb_swap = call(
-        agg_swap_kernel, "agg_swap", [((64, 1024), BF), listed],
-        (ints, *swaps, *owns, tiles, hub_adjacency, node_feats, self_row, part),
-        1, slots, 16, [VM, SM], 8 * MIB,
+    swaps = [row_send(v, 0, 0, 1) for v in owns[:2]]
+    part, sb0 = call(
+        functools.partial(agg_kernel, 0), "agg_first", [((8, 64, 128), F32), listed],
+        (ints, *owns[:2], *swaps, tiles, hub_adjacency, node_feats, self_row), 1, slots, 16, [VM, SM], 8 * MIB,
+    )
+    later, _ = lax.optimization_barrier((pair, part)) if EARLY else (pair, part)
+    ups = [pair] + [lax.ppermute(v, "feat", feat_perm(0, k)) for v, k in zip((pair, pair, later), (2, 1, 3))]
+    ups = [ups[0], ups[2], ups[3], ups[1]]
+    late = lax.optimization_barrier((owns[3], *ups))
+    owns[3], ups = late[0], late[1:]
+    swaps = [row_send(v, 0, 0, 1) for v in owns[2:]]
+    agg, sb1 = call(
+        functools.partial(agg_kernel, 1), "agg_second", [((64, 1024), BF), listed],
+        (ints, *owns[2:], *swaps, tiles, hub_adjacency, part), 1, slots, 16, [VM, SM], 8 * MIB,
     )
     aggs = feat_gather(agg)
-    act, ga = call(
-        mid_kernel, "middle", [((64, 1024), BF), shape(8)], (*aggs, *ups, wt, own), 0,
+    act, ga, hubs = call(
+        mid_kernel, "middle", [((64, 1024), BF), shape(8), ((4, 64, 128), F32)], (*aggs, *ups, wt, own, hub_adjacency), 0,
         [
             pltpu.VMEM((512, 1024), BF),
-            pltpu.VMEM((512, 256), F32),
-            pltpu.VMEM((512, 256), BF),
+            pltpu.VMEM((2, 512, 256), F32),
+            pltpu.VMEM((2, 512, 256), BF),
         ],
         16, None, 16 * MIB,
     )
-    outs = []
-    for swap in (True, False):
+
+    def back(swap, part, *tokens):
         (out,) = call(
-            functools.partial(back_kernel, swap), "back_swap" if swap else "back_own",
-            [shape(132)], (ints, sb_swap if swap else sb_own, ga, tiles, hub_adjacency), 2,
-            [pltpu.VMEM((9, 64, 128), F32)], 16, None, 8 * MIB,
+            functools.partial(back_kernel, swap, part), "back_swap" if swap else "back_own", [shape(66)],
+            (ints, sb0, sb1, ga, tiles, hubs, *tokens), 3, [slots[0]], 16, None, 4 * MIB,
+            loose=len(tokens),
         )
-        outs.append(out)
-    came = row_send(outs[0], 0, 0, 1)
-    both = call(add_kernel, "add", [shape(WIDE_A)] * 4 + [shape(WIDE_B)] * 4, (outs[1], came), 0, (), 16)
+        return out
+
+    swap0 = back(True, 0)
+    came0 = row_send(swap0, 0, 0, 1)
+    swap1 = back(True, 1, swap0)
+    came1 = row_send(swap1, 0, 0, 1)
+    own0 = back(False, 0, swap1)
+    sums = [None] * 4
+    sums[1], sums[3] = call(add_first_kernel, "add_first", [shape(WIDE_A)] * 2, (own0, came0))
+    own1 = back(False, 1, sums[3])
+    sums[0], sums[2], *bs = call(
+        add_second_kernel, "add_second", [shape(WIDE_A)] * 2 + [shape(WIDE_B)] * 4, (own0, came0, own1, came1), 0, (), 12
+    )
+    both = [*sums, *bs]
     ras = [both[0]] + [row_send(both[j], STEPS[j], 0, 0) for j in (1, 2, 3)]
     rbs = [both[4]] + [row_send(both[4 + i], 0, STEPS[i], 0) for i in (1, 2, 3)]
     zas = call(sum_a_kernel, "sum_a", [shape(NA + 1)] * 4, ras)

time: 132 us -> 125 us (0.947)
  waiting for transfers between devices: 57.4 us -> 41.4 us
  starting transfers between devices: 50.7 us -> 62.3 us
  local copies, waits for them, and re-layouts: 5.07 us -> 3.12 us
    ppermute x23 -> x24, waiting for transfers between devices: 37.2 us -> 20.7 us  [row_send(): return lax.ppermute(value, 'row', row_perm(dy, dz, dc))]
    ppermute x23 -> x24, starting transfers between devices: 27.5 us -> 42.6 us  [row_send(): return lax.ppermute(value, 'row', row_perm(dy, dz, dc))]
    ppermute x1, starting transfers between devices: 4.94 us -> 1.63 us  [feat_gather(): across = lax.ppermute(value, 'feat', feat_perm(1, 0))]
    unnamed x18, local copies, waits for them, and re-layouts: 5.07 us -> 3.12 us
    ppermute x3, waiting for transfers between devices: 11.2 us -> 12.7 us  [shards(): lax.ppermute(v, 'feat', feat_perm(0, k))]
    pallas_call x12 -> x15, Pallas kernels: 17 us -> 16.3 us  [call(): pl.pallas_call(kernel, out_shape=shapes, in_specs=[HB] * hbm + [SM] * sca...]
  transfers between devices with their start and end apart: 34 -> 35, of which waited for: 15 -> 15; matrix products, arithmetic and copies ran while one was open for 0% -> 0% of each run, Pallas kernels for 4% -> 6%
where the time goes in v3:
time: 125 us
  starting transfers between devices  62.3 us (50%)
  waiting for transfers between devices  41.4 us (33%)
  Pallas kernels  16.3 us (13%)
  local copies, waits for them, and re-layouts  3.12 us (2%)
    ppermute x24, starting transfers between devices, row_send(): return lax.ppermute(value, 'row', row_perm(dy, dz, dc))  42.6 us
    ppermute x24, waiting for transfers between devices, row_send(): return lax.ppermute(value, 'row', row_perm(dy, dz, dc))  20.7 us
    pallas_call x15, Pallas kernels, call(): pl.pallas_call(kernel, out_shape=shapes, in_specs=[HB] * hbm + [SM] * sca...  16.3 us
    ppermute x3, waiting for transfers between devices, shards(): lax.ppermute(v, 'feat', feat_perm(0, k))  12.7 us
    ppermute x1, starting transfers between devices, shards(): up_far = lax.ppermute(up, 'feat', feat_perm(1, 0))  5.75 us
    ppermute x3, waiting for transfers between devices, feat_gather(): far = [lax.ppermute(across, 'feat', feat_perm(0, k)) for k in STEPS[1:]]  4.71 us
    ppermute x3, starting transfers between devices, feat_gather(): near = [lax.ppermute(value, 'feat', feat_perm(0, k)) for k in STEPS[1:]]  4.55 us
    ppermute x3, starting transfers between devices, feat_gather(): far = [lax.ppermute(across, 'feat', feat_perm(0, k)) for k in STEPS[1:]]  4.14 us
  transfers between devices with their start and end apart: 35, of which 15 were waited for; matrix products, arithmetic and copies ran while one was open for 0% of the time, Pallas kernels for 6%

profile of v3, /device:TPU:2, one launch (start us, length us, event | category | flops | bytes accessed | tf_op | source)
XLA Modules:
  0.0 124.8 jit_solution(9746035282187139980)
XLA Ops:
  2.6 3.4 %collective-permute-start.2 = (bf16[9,64,128]{2,1,0:T(8,128)(2,1)S(1)}, bf16[9,64,128]{2,1,0:T(8,128)(2,1)S(1)}, u32[]{:S(2)}, u32[]{:S(2)}) collective-permute-start(bf16[9,64,128]{2,1,0:T(8,128)(2,1)S(1)} %prep.1.p0), channel_id=1, source_target_pairs={{0,32},{8,40},{16,48},{24,56},{32,0},{40,8},{48,16},{56,24},{64,96... | collective-permute-start | bytes 442376 | tf_op jit(solution)/shard_map/ppermute | solution.py:42
  6.0 1.4 %collective-permute-start.1 = (bf16[9,64,128]{2,1,0:T(8,128)(2,1)S(1)}, bf16[9,64,128]{2,1,0:T(8,128)(2,1)S(1)}, u32[]{:S(2)}, u32[]{:S(2)}) collective-permute-start(bf16[9,64,128]{2,1,0:T(8,128)(2,1)S(1)} %prep.1.p0), channel_id=1, source_target_pairs={{0,48},{8,56},{16,0},{24,8},{32,16},{40,24},{48,32},{56,40},{64,11... | collective-permute-start | bytes 442376 | tf_op jit(solution)/shard_map/ppermute | solution.py:42
  8.0 6.1 %collective-permute-done.2.p3 = bf16[9,64,128]{2,1,0:T(8,128)(2,1)S(1)} collective-permute-done((bf16[9,64,128]{2,1,0:T(8,128)(2,1)S(1)}, bf16[9,64,128]{2,1,0:T(8,128)(2,1)S(1)}, u32[]{:S(2)}, u32[]{:S(2)}) %collective-permute-start.2) | collective-permute-done | bytes 147488 | tf_op jit(solution)/shard_map/ppermute | solution.py:42
  14.1 3.6 %collective-permute-done.p1 = bf16[9,64,128]{2,1,0:T(8,128)(2,1)S(1)} collective-permute-done((bf16[9,64,128]{2,1,0:T(8,128)(2,1)S(1)}, bf16[9,64,128]{2,1,0:T(8,128)(2,1)S(1)}, u32[]{:S(2)}, u32[]{:S(2)}) %collective-permute-start) | collective-permute-done | bytes 147488 | tf_op jit(solution)/shard_map/ppermute | solution.py:42
  17.7 5.7 %collective-permute-start.5 = (bf16[64,1024]{1,0:T(8,128)(2,1)S(1)}, bf16[64,1024]{1,0:T(8,128)(2,1)S(1)}, u32[]{:S(2)}, u32[]{:S(2)}) collective-permute-start(bf16[64,1024]{1,0:T(8,128)(2,1)S(1)} %copy-done.6), channel_id=1, source_target_pairs={{0,4},{1,5},{2,6},{3,7},{4,0},{5,1},{6,2},{7,3},{8,12},{9,13},{10,... | collective-permute-start | bytes 393224 | tf_op jit(solution)/shard_map/ppermute | solution.py:350
  23.5 1.6 %collective-permute-start.11 = (bf16[33,64,128]{2,1,0:T(8,128)(2,1)S(1)}, bf16[33,64,128]{2,1,0:T(8,128)(2,1)S(1)}, u32[]{:S(2)}, u32[]{:S(2)}) collective-permute-start(bf16[33,64,128]{2,1,0:T(8,128)(2,1)S(1)} %stack.1._.rest_0_), channel_id=1, source_target_pairs={{0,64},{8,72},{16,80},{24,88},{32,96},{40,104},{48,112},{56,120},{... | collective-permute-start | bytes 1622024 | tf_op jit(solution)/shard_map/ppermute | solution.py:42
  25.0 2.9 %collective-permute-start.4 = (bf16[33,64,128]{2,1,0:T(8,128)(2,1)S(1)}, bf16[33,64,128]{2,1,0:T(8,128)(2,1)S(1)}, u32[]{:S(2)}, u32[]{:S(2)}) collective-permute-start(bf16[33,64,128]{2,1,0:T(8,128)(2,1)S(1)} %stack.1._.rest_0_), channel_id=1, source_target_pairs={{0,128},{8,136},{16,144},{24,152},{32,160},{40,168},{48,176},{56,1... | collective-permute-start | bytes 1622024 | tf_op jit(solution)/shard_map/ppermute | solution.py:42
  29.3 2.2 %copy-done = bf16[1,32,4,128,128]{4,3,2,1,0:T(8,128)(2,1)S(1)} copy-done((bf16[1,32,4,128,128]{4,3,2,1,0:T(8,128)(2,1)S(1)}, bf16[1,32,4,128,128]{4,3,2,1,0:T(8,128)(2,1)}, u32[]{:S(2)}) %copy-start) | copy-done | bytes 4194328
  31.8 2.2 %collective-permute-start.8 = (bf16[128,1024]{1,0:T(8,128)(2,1)S(1)}, bf16[128,1024]{1,0:T(8,128)(2,1)S(1)}, u32[]{:S(2)}, u32[]{:S(2)}) collective-permute-start(bf16[128,1024]{1,0:T(8,128)(2,1)S(1)} %get-tuple-element.39.rest_8_), channel_id=1, source_target_pairs={{0,2},{1,3},{2,0},{3,1},{4,6},{5,7},{6,4},{7,5},{8,10},{9,11},{10,... | collective-permute-start | bytes 786440 | tf_op jit(solution)/shard_map/ppermute | solution.py:368
  35.5 6.8 %collective-permute-done.8.rest_11_ = bf16[128,1024]{1,0:T(8,128)(2,1)S(1)} collective-permute-done((bf16[128,1024]{1,0:T(8,128)(2,1)S(1)}, bf16[128,1024]{1,0:T(8,128)(2,1)S(1)}, u32[]{:S(2)}, u32[]{:S(2)}) %collective-permute-start.8) | collective-permute-done | bytes 262176 | tf_op jit(solution)/shard_map/ppermute | solution.py:368
  42.3 2.7 %collective-permute-done.7.rest_10_ = bf16[128,1024]{1,0:T(8,128)(2,1)S(1)} collective-permute-done((bf16[128,1024]{1,0:T(8,128)(2,1)S(1)}, bf16[128,1024]{1,0:T(8,128)(2,1)S(1)}, u32[]{:S(2)}, u32[]{:S(2)}) %collective-permute-start.7) | collective-permute-done | bytes 262176 | tf_op jit(solution)/shard_map/ppermute | solution.py:368
  45.5 3.1 %collective-permute-done.6.rest_9_ = bf16[128,1024]{1,0:T(8,128)(2,1)S(1)} collective-permute-done((bf16[128,1024]{1,0:T(8,128)(2,1)S(1)}, bf16[128,1024]{1,0:T(8,128)(2,1)S(1)}, u32[]{:S(2)}, u32[]{:S(2)}) %collective-permute-start.6) | collective-permute-done | bytes 262176 | tf_op jit(solution)/shard_map/ppermute | solution.py:368
  48.7 1.6 %collective-permute-done.4.rest_1_ = bf16[33,64,128]{2,1,0:T(8,128)(2,1)S(1)} collective-permute-done((bf16[33,64,128]{2,1,0:T(8,128)(2,1)S(1)}, bf16[33,64,128]{2,1,0:T(8,128)(2,1)S(1)}, u32[]{:S(2)}, u32[]{:S(2)}) %collective-permute-start.4) | collective-permute-done | bytes 540704 | tf_op jit(solution)/shard_map/ppermute | solution.py:42
  50.9 2.7 %agg_first.1 = (f32[8,64,128]{2,1,0:T(8,128)S(1)}, s32[4,16]{1,0:T(4,128)S(1)}) custom-call(s32[10,32]{1,0:T(8,128)S(1)} %add_add_fusion.ints_ref, bf16[33,64,128]{2,1,0:T(8,128)(2,1)S(1)} %stack.1._.rest_0_, bf16[33,64,128]{2,1,0:T(8,128)(2,1)S(1)} %collective-permute-done.11.rest_1_, bf16[33,64,128]{2,1,0:T(8,128)(2,1)S(1)} %collective-permute-done.12.rest_2_, ...), custom_call_target="tpu_custom_call" | custom-call | bytes 8388608 | tf_op jit(solution)/shard_map/agg_first/pallas_call | solution.py:305
  53.6 2.7 %agg_second.1 = (bf16[64,1024]{1,0:T(8,128)(2,1)S(1)}, s32[4,16]{1,0:T(4,128)S(1)}) custom-call(s32[10,32]{1,0:T(8,128)S(1)} %add_add_fusion.ints_ref, bf16[33,64,128]{2,1,0:T(8,128)(2,1)S(1)} %collective-permute-done.3.rest_0_, bf16[33,64,128]{2,1,0:T(8,128)(2,1)S(1)} %collective-permute-done.4.rest_1_, ...), custom_call_target="tpu_custom_call" | custom-call | bytes 8388608 | tf_op jit(solution)/shard_map/agg_second/pallas_call | solution.py:305
  56.2 1.6 %collective-permute-start.17 = (bf16[64,1024]{1,0:T(8,128)(2,1)S(1)}, bf16[64,1024]{1,0:T(8,128)(2,1)S(1)}, u32[]{:S(2)}, u32[]{:S(2)}) collective-permute-start(bf16[64,1024]{1,0:T(8,128)(2,1)S(1)} %get-tuple-element.38.rest_0_), channel_id=1, source_target_pairs={{0,4},{1,5},{2,6},{3,7},{4,0},{5,1},{6,2},{7,3},{8,12},{9,13},{10,... | collective-permute-start | bytes 393224 | tf_op jit(solution)/shard_map/ppermute | solution.py:46
  57.9 2.0 %collective-permute-start.16 = (bf16[64,1024]{1,0:T(8,128)(2,1)S(1)}, bf16[64,1024]{1,0:T(8,128)(2,1)S(1)}, u32[]{:S(2)}, u32[]{:S(2)}) collective-permute-start(bf16[64,1024]{1,0:T(8,128)(2,1)S(1)} %get-tuple-element.38.rest_0_), channel_id=1, source_target_pairs={{0,2},{1,3},{2,0},{3,1},{4,6},{5,7},{6,4},{7,5},{8,10},{9,11},{10,... | collective-permute-start | bytes 393224 | tf_op jit(solution)/shard_map/ppermute | solution.py:47
  59.9 2.5 %collective-permute-start.15 = (bf16[64,1024]{1,0:T(8,128)(2,1)S(1)}, bf16[64,1024]{1,0:T(8,128)(2,1)S(1)}, u32[]{:S(2)}, u32[]{:S(2)}) collective-permute-start(bf16[64,1024]{1,0:T(8,128)(2,1)S(1)} %get-tuple-element.38.rest_0_), channel_id=1, source_target_pairs={{0,3},{1,0},{2,1},{3,2},{4,7},{5,4},{6,5},{7,6},{8,11},{9,8},{10,9... | collective-permute-start | bytes 393224 | tf_op jit(solution)/shard_map/ppermute | solution.py:47
  62.4 3.3 %collective-permute-done.17.rest_4_ = bf16[64,1024]{1,0:T(8,128)(2,1)S(1)} collective-permute-done((bf16[64,1024]{1,0:T(8,128)(2,1)S(1)}, bf16[64,1024]{1,0:T(8,128)(2,1)S(1)}, u32[]{:S(2)}, u32[]{:S(2)}) %collective-permute-start.17) | collective-permute-done | bytes 131104 | tf_op jit(solution)/shard_map/ppermute | solution.py:46
  65.7 2.1 %collective-permute-start.20 = (bf16[64,1024]{1,0:T(8,128)(2,1)S(1)}, bf16[64,1024]{1,0:T(8,128)(2,1)S(1)}, u32[]{:S(2)}, u32[]{:S(2)}) collective-permute-start(bf16[64,1024]{1,0:T(8,128)(2,1)S(1)} %collective-permute-done.17.rest_4_), channel_id=1, source_target_pairs={{0,2},{1,3},{2,0},{3,1},{4,6},{5,7},{6,4},{7,5},{8,10},{9,11},{10,... | collective-permute-start | bytes 393224 | tf_op jit(solution)/shard_map/ppermute | solution.py:48
  69.9 3.3 %collective-permute-done.20.rest_7_ = bf16[64,1024]{1,0:T(8,128)(2,1)S(1)} collective-permute-done((bf16[64,1024]{1,0:T(8,128)(2,1)S(1)}, bf16[64,1024]{1,0:T(8,128)(2,1)S(1)}, u32[]{:S(2)}, u32[]{:S(2)}) %collective-permute-start.20) | collective-permute-done | bytes 131104 | tf_op jit(solution)/shard_map/ppermute | solution.py:48
  74.6 3.1 %middle.1 = (bf16[64,1024]{1,0:T(8,128)(2,1)}, bf16[8,64,128]{2,1,0:T(8,128)(2,1)S(1)}, f32[4,64,128]{2,1,0:T(8,128)S(1)}) custom-call(bf16[64,1024]{1,0:T(8,128)(2,1)S(1)} %get-tuple-element.38.rest_0_, bf16[64,1024]{1,0:T(8,128)(2,1)S(1)} %collective-permute-done.14.rest_1_, bf16[64,1024]{1,0:T(8,128)(2,1)S(1)} %collective-permute-done.15.rest_2_, ...), custom_call_target="tpu_custom_call" | custom-call | bytes 16777216 | tf_op jit(solution)/shard_map/middle/pallas_call | solution.py:305
  83.9 2.5 %collective-permute-start.25 = (bf16[25,64,128]{2,1,0:T(8,128)(2,1)S(1)}, bf16[25,64,128]{2,1,0:T(8,128)(2,1)S(1)}, u32[]{:S(2)}, u32[]{:S(2)}) collective-permute-start(bf16[25,64,128]{2,1,0:T(8,128)(2,1)S(1)} %get-tuple-element.50.rest_0_), channel_id=1, source_target_pairs={{0,128},{8,136},{16,144},{24,152},{32,160},{40,168},{48,176},{56,1... | collective-permute-start | bytes 1228808 | tf_op jit(solution)/shard_map/ppermute | solution.py:42
  88.0 1.6 %collective-permute-start.24 = (bf16[25,64,128]{2,1,0:T(8,128)(2,1)S(1)}, bf16[25,64,128]{2,1,0:T(8,128)(2,1)S(1)}, u32[]{:S(2)}, u32[]{:S(2)}) collective-permute-start(bf16[25,64,128]{2,1,0:T(8,128)(2,1)S(1)} %get-tuple-element.53), channel_id=1, source_target_pairs={{0,192},{8,200},{16,208},{24,216},{32,224},{40,232},{48,240},{56,2... | collective-permute-start | bytes 1228808 | tf_op jit(solution)/shard_map/ppermute | solution.py:42
  89.6 5.6 %collective-permute-start.29 = (bf16[8,64,128]{2,1,0:T(8,128)(2,1)S(1)}, bf16[8,64,128]{2,1,0:T(8,128)(2,1)S(1)}, u32[]{:S(2)}, u32[]{:S(2)}) collective-permute-start(bf16[8,64,128]{2,1,0:T(8,128)(2,1)S(1)} %get-tuple-element.59), channel_id=1, source_target_pairs={{0,16},{8,24},{16,32},{24,40},{32,48},{40,56},{48,0},{56,8},{64,80... | collective-permute-start | bytes 393224 | tf_op jit(solution)/shard_map/ppermute | solution.py:42
  95.9 6.0 %collective-permute-start.31 = (bf16[8,64,128]{2,1,0:T(8,128)(2,1)S(1)}, bf16[8,64,128]{2,1,0:T(8,128)(2,1)S(1)}, u32[]{:S(2)}, u32[]{:S(2)}) collective-permute-start(bf16[8,64,128]{2,1,0:T(8,128)(2,1)S(1)} %get-tuple-element.61), channel_id=1, source_target_pairs={{0,32},{8,40},{16,48},{24,56},{32,0},{40,8},{48,16},{56,24},{64,96... | collective-permute-start | bytes 393224 | tf_op jit(solution)/shard_map/ppermute | solution.py:42
  101.9 2.6 %collective-permute-done.25.refs_3_ = bf16[25,64,128]{2,1,0:T(8,128)(2,1)S(1)} collective-permute-done((bf16[25,64,128]{2,1,0:T(8,128)(2,1)S(1)}, bf16[25,64,128]{2,1,0:T(8,128)(2,1)S(1)}, u32[]{:S(2)}, u32[]{:S(2)}) %collective-permute-start.25) | collective-permute-done | bytes 409632 | tf_op jit(solution)/shard_map/ppermute | solution.py:42
  104.9 5.7 %collective-permute-start.26 = (bf16[7,64,128]{2,1,0:T(8,128)(2,1)S(1)}, bf16[7,64,128]{2,1,0:T(8,128)(2,1)S(1)}, u32[]{:S(2)}, u32[]{:S(2)}) collective-permute-start(bf16[7,64,128]{2,1,0:T(8,128)(2,1)S(1)} %get-tuple-element.55), channel_id=1, source_target_pairs={{0,16},{8,24},{16,32},{24,40},{32,48},{40,56},{48,0},{56,8},{64,80... | collective-permute-start | bytes 344072 | tf_op jit(solution)/shard_map/ppermute | solution.py:42
  110.6 2.3 %collective-permute-start.28 = (bf16[7,64,128]{2,1,0:T(8,128)(2,1)S(1)}, bf16[7,64,128]{2,1,0:T(8,128)(2,1)S(1)}, u32[]{:S(2)}, u32[]{:S(2)}) collective-permute-start(bf16[7,64,128]{2,1,0:T(8,128)(2,1)S(1)} %get-tuple-element.57), channel_id=1, source_target_pairs={{0,32},{8,40},{16,48},{24,56},{32,0},{40,8},{48,16},{56,24},{64,96... | collective-permute-start | bytes 344072 | tf_op jit(solution)/shard_map/ppermute | solution.py:42
  113.0 2.0 %collective-permute-start.32 = (bf16[2,64,128]{2,1,0:T(8,128)(2,1)S(1)}, bf16[2,64,128]{2,1,0:T(8,128)(2,1)S(1)}, u32[]{:S(2)}, u32[]{:S(2)}) collective-permute-start(bf16[2,64,128]{2,1,0:T(8,128)(2,1)S(1)} %get-tuple-element.63), channel_id=1, source_target_pairs={{0,64},{8,72},{16,80},{24,88},{32,96},{40,104},{48,112},{56,120},{... | collective-permute-start | bytes 98312 | tf_op jit(solution)/shard_map/ppermute | solution.py:42
  116.4 1.9 %collective-permute-done.32.rest_5_ = bf16[2,64,128]{2,1,0:T(8,128)(2,1)S(1)} collective-permute-done((bf16[2,64,128]{2,1,0:T(8,128)(2,1)S(1)}, bf16[2,64,128]{2,1,0:T(8,128)(2,1)S(1)}, u32[]{:S(2)}, u32[]{:S(2)}) %collective-permute-start.32) | collective-permute-done | bytes 32800 | tf_op jit(solution)/shard_map/ppermute | solution.py:42
  119.6 4.0 %collective-permute-done.34.rest_7_ = bf16[2,64,128]{2,1,0:T(8,128)(2,1)S(1)} collective-permute-done((bf16[2,64,128]{2,1,0:T(8,128)(2,1)S(1)}, bf16[2,64,128]{2,1,0:T(8,128)(2,1)S(1)}, u32[]{:S(2)}, u32[]{:S(2)}) %collective-permute-start.34) | collective-permute-done | bytes 32800 | tf_op jit(solution)/shard_map/ppermute | solution.py:42
  (72 shorter events, 22.9 us)
Async XLA Ops:
  2.6 11.5 %collective-permute-start.2 = (bf16[9,64,128]{2,1,0:T(8,128)(2,1)S(1)}, bf16[9,64,128]{2,1,0:T(8,128)(2,1)S(1)}, u32[]{:S(2)}, u32[]{:S(2)}) collective-permute-start(bf16[9,64,128]{2,1,0:T(8,128)(2,1)S(1)} %prep.1.p0), channel_id=1, source_target_pairs={{0,32},{8,40},{16,48},{24,56},{32,0},{40,8},{48,16},{56,24},{64,96... | collective-permute-start | bytes 442376 | tf_op jit(solution)/shard_map/ppermute | solution.py:42
  6.0 8.1 %collective-permute-start.1 = (bf16[9,64,128]{2,1,0:T(8,128)(2,1)S(1)}, bf16[9,64,128]{2,1,0:T(8,128)(2,1)S(1)}, u32[]{:S(2)}, u32[]{:S(2)}) collective-permute-start(bf16[9,64,128]{2,1,0:T(8,128)(2,1)S(1)} %prep.1.p0), channel_id=1, source_target_pairs={{0,48},{8,56},{16,0},{24,8},{32,16},{40,24},{48,32},{56,40},{64,11... | collective-permute-start | bytes 442376 | tf_op jit(solution)/shard_map/ppermute | solution.py:42
  7.4 10.2 %collective-permute-start = (bf16[9,64,128]{2,1,0:T(8,128)(2,1)S(1)}, bf16[9,64,128]{2,1,0:T(8,128)(2,1)S(1)}, u32[]{:S(2)}, u32[]{:S(2)}) collective-permute-start(bf16[9,64,128]{2,1,0:T(8,128)(2,1)S(1)} %prep.1.p0), channel_id=1, source_target_pairs={{0,16},{8,24},{16,32},{24,40},{32,48},{40,56},{48,0},{56,8},{64,80... | collective-permute-start | bytes 442376 | tf_op jit(solution)/shard_map/ppermute | solution.py:42
  17.7 11.6 %collective-permute-start.5 = (bf16[64,1024]{1,0:T(8,128)(2,1)S(1)}, bf16[64,1024]{1,0:T(8,128)(2,1)S(1)}, u32[]{:S(2)}, u32[]{:S(2)}) collective-permute-start(bf16[64,1024]{1,0:T(8,128)(2,1)S(1)} %copy-done.6), channel_id=1, source_target_pairs={{0,4},{1,5},{2,6},{3,7},{4,0},{5,1},{6,2},{7,3},{8,12},{9,13},{10,... | collective-permute-start | bytes 393224 | tf_op jit(solution)/shard_map/ppermute | solution.py:350
  23.5 21.6 %collective-permute-start.11 = (bf16[33,64,128]{2,1,0:T(8,128)(2,1)S(1)}, bf16[33,64,128]{2,1,0:T(8,128)(2,1)S(1)}, u32[]{:S(2)}, u32[]{:S(2)}) collective-permute-start(bf16[33,64,128]{2,1,0:T(8,128)(2,1)S(1)} %stack.1._.rest_0_), channel_id=1, source_target_pairs={{0,64},{8,72},{16,80},{24,88},{32,96},{40,104},{48,112},{56,120},{... | collective-permute-start | bytes 1622024 | tf_op jit(solution)/shard_map/ppermute | solution.py:42
  25.0 25.3 %collective-permute-start.4 = (bf16[33,64,128]{2,1,0:T(8,128)(2,1)S(1)}, bf16[33,64,128]{2,1,0:T(8,128)(2,1)S(1)}, u32[]{:S(2)}, u32[]{:S(2)}) collective-permute-start(bf16[33,64,128]{2,1,0:T(8,128)(2,1)S(1)} %stack.1._.rest_0_), channel_id=1, source_target_pairs={{0,128},{8,136},{16,144},{24,152},{32,160},{40,168},{48,176},{56,1... | collective-permute-start | bytes 1622024 | tf_op jit(solution)/shard_map/ppermute | solution.py:42
  27.9 22.4 %collective-permute-start.3 = (bf16[33,64,128]{2,1,0:T(8,128)(2,1)S(1)}, bf16[33,64,128]{2,1,0:T(8,128)(2,1)S(1)}, u32[]{:S(2)}, u32[]{:S(2)}) collective-permute-start(bf16[33,64,128]{2,1,0:T(8,128)(2,1)S(1)} %stack.1._.rest_0_), channel_id=1, source_target_pairs={{0,192},{8,200},{16,208},{24,216},{32,224},{40,232},{48,240},{56,2... | collective-permute-start | bytes 1622024 | tf_op jit(solution)/shard_map/ppermute | solution.py:42
  31.8 10.5 %collective-permute-start.8 = (bf16[128,1024]{1,0:T(8,128)(2,1)S(1)}, bf16[128,1024]{1,0:T(8,128)(2,1)S(1)}, u32[]{:S(2)}, u32[]{:S(2)}) collective-permute-start(bf16[128,1024]{1,0:T(8,128)(2,1)S(1)} %get-tuple-element.39.rest_8_), channel_id=1, source_target_pairs={{0,2},{1,3},{2,0},{3,1},{4,6},{5,7},{6,4},{7,5},{8,10},{9,11},{10,... | collective-permute-start | bytes 786440 | tf_op jit(solution)/shard_map/ppermute | solution.py:368
  34.0 11.0 %collective-permute-start.7 = (bf16[128,1024]{1,0:T(8,128)(2,1)S(1)}, bf16[128,1024]{1,0:T(8,128)(2,1)S(1)}, u32[]{:S(2)}, u32[]{:S(2)}) collective-permute-start(bf16[128,1024]{1,0:T(8,128)(2,1)S(1)} %get-tuple-element.39.rest_8_), channel_id=1, source_target_pairs={{0,3},{1,0},{2,1},{3,2},{4,7},{5,4},{6,5},{7,6},{8,11},{9,8},{10,9... | collective-permute-start | bytes 786440 | tf_op jit(solution)/shard_map/ppermute | solution.py:368
  42.3 6.4 %collective-permute-start.6 = (bf16[128,1024]{1,0:T(8,128)(2,1)S(1)}, bf16[128,1024]{1,0:T(8,128)(2,1)S(1)}, u32[]{:S(2)}, u32[]{:S(2)}) collective-permute-start(bf16[128,1024]{1,0:T(8,128)(2,1)S(1)} %get-tuple-element.39.rest_8_), channel_id=1, source_target_pairs={{0,1},{1,2},{2,3},{3,0},{4,5},{5,6},{6,7},{7,4},{8,9},{9,10},{10,1... | collective-permute-start | bytes 786440 | tf_op jit(solution)/shard_map/ppermute | solution.py:368
  45.0 5.8 %collective-permute-start.12 = (bf16[33,64,128]{2,1,0:T(8,128)(2,1)S(1)}, bf16[33,64,128]{2,1,0:T(8,128)(2,1)S(1)}, u32[]{:S(2)}, u32[]{:S(2)}) collective-permute-start(bf16[33,64,128]{2,1,0:T(8,128)(2,1)S(1)} %stack.1._.rest_0_), channel_id=1, source_target_pairs={{0,8},{8,0},{16,24},{24,16},{32,40},{40,32},{48,56},{56,48},{64,72... | collective-permute-start | bytes 1622024 | tf_op jit(solution)/shard_map/ppermute | solution.py:42
  45.0 5.8 %collective-permute-start.13 = (bf16[33,64,128]{2,1,0:T(8,128)(2,1)S(1)}, bf16[33,64,128]{2,1,0:T(8,128)(2,1)S(1)}, u32[]{:S(2)}, u32[]{:S(2)}) collective-permute-start(bf16[33,64,128]{2,1,0:T(8,128)(2,1)S(1)} %collective-permute-done.11.rest_1_), channel_id=1, source_target_pairs={{0,8},{8,0},{16,24},{24,16},{32,40},{40,32},{48,56},{56,48},{64,72... | collective-permute-start | bytes 1622024 | tf_op jit(solution)/shard_map/ppermute | solution.py:42
  56.2 9.5 %collective-permute-start.17 = (bf16[64,1024]{1,0:T(8,128)(2,1)S(1)}, bf16[64,1024]{1,0:T(8,128)(2,1)S(1)}, u32[]{:S(2)}, u32[]{:S(2)}) collective-permute-start(bf16[64,1024]{1,0:T(8,128)(2,1)S(1)} %get-tuple-element.38.rest_0_), channel_id=1, source_target_pairs={{0,4},{1,5},{2,6},{3,7},{4,0},{5,1},{6,2},{7,3},{8,12},{9,13},{10,... | collective-permute-start | bytes 393224 | tf_op jit(solution)/shard_map/ppermute | solution.py:46
  57.9 11.4 %collective-permute-start.16 = (bf16[64,1024]{1,0:T(8,128)(2,1)S(1)}, bf16[64,1024]{1,0:T(8,128)(2,1)S(1)}, u32[]{:S(2)}, u32[]{:S(2)}) collective-permute-start(bf16[64,1024]{1,0:T(8,128)(2,1)S(1)} %get-tuple-element.38.rest_0_), channel_id=1, source_target_pairs={{0,2},{1,3},{2,0},{3,1},{4,6},{5,7},{6,4},{7,5},{8,10},{9,11},{10,... | collective-permute-start | bytes 393224 | tf_op jit(solution)/shard_map/ppermute | solution.py:47
  59.9 10.0 %collective-permute-start.15 = (bf16[64,1024]{1,0:T(8,128)(2,1)S(1)}, bf16[64,1024]{1,0:T(8,128)(2,1)S(1)}, u32[]{:S(2)}, u32[]{:S(2)}) collective-permute-start(bf16[64,1024]{1,0:T(8,128)(2,1)S(1)} %get-tuple-element.38.rest_0_), channel_id=1, source_target_pairs={{0,3},{1,0},{2,1},{3,2},{4,7},{5,4},{6,5},{7,6},{8,11},{9,8},{10,9... | collective-permute-start | bytes 393224 | tf_op jit(solution)/shard_map/ppermute | solution.py:47
  62.4 7.5 %collective-permute-start.14 = (bf16[64,1024]{1,0:T(8,128)(2,1)S(1)}, bf16[64,1024]{1,0:T(8,128)(2,1)S(1)}, u32[]{:S(2)}, u32[]{:S(2)}) collective-permute-start(bf16[64,1024]{1,0:T(8,128)(2,1)S(1)} %get-tuple-element.38.rest_0_), channel_id=1, source_target_pairs={{0,1},{1,2},{2,3},{3,0},{4,5},{5,6},{6,7},{7,4},{8,9},{9,10},{10,1... | collective-permute-start | bytes 393224 | tf_op jit(solution)/shard_map/ppermute | solution.py:47
  65.7 7.5 %collective-permute-start.20 = (bf16[64,1024]{1,0:T(8,128)(2,1)S(1)}, bf16[64,1024]{1,0:T(8,128)(2,1)S(1)}, u32[]{:S(2)}, u32[]{:S(2)}) collective-permute-start(bf16[64,1024]{1,0:T(8,128)(2,1)S(1)} %collective-permute-done.17.rest_4_), channel_id=1, source_target_pairs={{0,2},{1,3},{2,0},{3,1},{4,6},{5,7},{6,4},{7,5},{8,10},{9,11},{10,... | collective-permute-start | bytes 393224 | tf_op jit(solution)/shard_map/ppermute | solution.py:48
  67.9 6.7 %collective-permute-start.19 = (bf16[64,1024]{1,0:T(8,128)(2,1)S(1)}, bf16[64,1024]{1,0:T(8,128)(2,1)S(1)}, u32[]{:S(2)}, u32[]{:S(2)}) collective-permute-start(bf16[64,1024]{1,0:T(8,128)(2,1)S(1)} %collective-permute-done.17.rest_4_), channel_id=1, source_target_pairs={{0,3},{1,0},{2,1},{3,2},{4,7},{5,4},{6,5},{7,6},{8,11},{9,8},{10,9... | collective-permute-start | bytes 393224 | tf_op jit(solution)/shard_map/ppermute | solution.py:48
  69.2 5.4 %collective-permute-start.18 = (bf16[64,1024]{1,0:T(8,128)(2,1)S(1)}, bf16[64,1024]{1,0:T(8,128)(2,1)S(1)}, u32[]{:S(2)}, u32[]{:S(2)}) collective-permute-start(bf16[64,1024]{1,0:T(8,128)(2,1)S(1)} %collective-permute-done.17.rest_4_), channel_id=1, source_target_pairs={{0,1},{1,2},{2,3},{3,0},{4,5},{5,6},{6,7},{7,4},{8,9},{9,10},{10,1... | collective-permute-start | bytes 393224 | tf_op jit(solution)/shard_map/ppermute | solution.py:48
  80.5 7.2 %collective-permute-start.22 = (bf16[66,64,128]{2,1,0:T(8,128)(2,1)S(1)}, bf16[66,64,128]{2,1,0:T(8,128)(2,1)S(1)}, u32[]{:S(2)}, u32[]{:S(2)}) collective-permute-start(bf16[66,64,128]{2,1,0:T(8,128)(2,1)S(1)} %back_swap.3.rest_0_), channel_id=1, source_target_pairs={{0,8},{8,0},{16,24},{24,16},{32,40},{40,32},{48,56},{56,48},{64,72... | collective-permute-start | bytes 3244040 | tf_op jit(solution)/shard_map/ppermute | solution.py:42
  82.6 13.2 %collective-permute-start.23 = (bf16[25,64,128]{2,1,0:T(8,128)(2,1)S(1)}, bf16[25,64,128]{2,1,0:T(8,128)(2,1)S(1)}, u32[]{:S(2)}, u32[]{:S(2)}) collective-permute-start(bf16[25,64,128]{2,1,0:T(8,128)(2,1)S(1)} %get-tuple-element.52), channel_id=1, source_target_pairs={{0,64},{8,72},{16,80},{24,88},{32,96},{40,104},{48,112},{56,120},{... | collective-permute-start | bytes 1228808 | tf_op jit(solution)/shard_map/ppermute | solution.py:42
  83.9 20.6 %collective-permute-start.25 = (bf16[25,64,128]{2,1,0:T(8,128)(2,1)S(1)}, bf16[25,64,128]{2,1,0:T(8,128)(2,1)S(1)}, u32[]{:S(2)}, u32[]{:S(2)}) collective-permute-start(bf16[25,64,128]{2,1,0:T(8,128)(2,1)S(1)} %get-tuple-element.50.rest_0_), channel_id=1, source_target_pairs={{0,128},{8,136},{16,144},{24,152},{32,160},{40,168},{48,176},{56,1... | collective-permute-start | bytes 1228808 | tf_op jit(solution)/shard_map/ppermute | solution.py:42
  88.0 16.7 %collective-permute-start.24 = (bf16[25,64,128]{2,1,0:T(8,128)(2,1)S(1)}, bf16[25,64,128]{2,1,0:T(8,128)(2,1)S(1)}, u32[]{:S(2)}, u32[]{:S(2)}) collective-permute-start(bf16[25,64,128]{2,1,0:T(8,128)(2,1)S(1)} %get-tuple-element.53), channel_id=1, source_target_pairs={{0,192},{8,200},{16,208},{24,216},{32,224},{40,232},{48,240},{56,2... | collective-permute-start | bytes 1228808 | tf_op jit(solution)/shard_map/ppermute | solution.py:42
  89.6 21.0 %collective-permute-start.29 = (bf16[8,64,128]{2,1,0:T(8,128)(2,1)S(1)}, bf16[8,64,128]{2,1,0:T(8,128)(2,1)S(1)}, u32[]{:S(2)}, u32[]{:S(2)}) collective-permute-start(bf16[8,64,128]{2,1,0:T(8,128)(2,1)S(1)} %get-tuple-element.59), channel_id=1, source_target_pairs={{0,16},{8,24},{16,32},{24,40},{32,48},{40,56},{48,0},{56,8},{64,80... | collective-permute-start | bytes 393224 | tf_op jit(solution)/shard_map/ppermute | solution.py:42
  95.3 17.7 %collective-permute-start.30 = (bf16[8,64,128]{2,1,0:T(8,128)(2,1)S(1)}, bf16[8,64,128]{2,1,0:T(8,128)(2,1)S(1)}, u32[]{:S(2)}, u32[]{:S(2)}) collective-permute-start(bf16[8,64,128]{2,1,0:T(8,128)(2,1)S(1)} %get-tuple-element.60), channel_id=1, source_target_pairs={{0,48},{8,56},{16,0},{24,8},{32,16},{40,24},{48,32},{56,40},{64,11... | collective-permute-start | bytes 393224 | tf_op jit(solution)/shard_map/ppermute | solution.py:42
  95.9 17.1 %collective-permute-start.31 = (bf16[8,64,128]{2,1,0:T(8,128)(2,1)S(1)}, bf16[8,64,128]{2,1,0:T(8,128)(2,1)S(1)}, u32[]{:S(2)}, u32[]{:S(2)}) collective-permute-start(bf16[8,64,128]{2,1,0:T(8,128)(2,1)S(1)} %get-tuple-element.61), channel_id=1, source_target_pairs={{0,32},{8,40},{16,48},{24,56},{32,0},{40,8},{48,16},{56,24},{64,96... | collective-permute-start | bytes 393224 | tf_op jit(solution)/shard_map/ppermute | solution.py:42
  104.9 18.7 %collective-permute-start.26 = (bf16[7,64,128]{2,1,0:T(8,128)(2,1)S(1)}, bf16[7,64,128]{2,1,0:T(8,128)(2,1)S(1)}, u32[]{:S(2)}, u32[]{:S(2)}) collective-permute-start(bf16[7,64,128]{2,1,0:T(8,128)(2,1)S(1)} %get-tuple-element.55), channel_id=1, source_target_pairs={{0,16},{8,24},{16,32},{24,40},{32,48},{40,56},{48,0},{56,8},{64,80... | collective-permute-start | bytes 344072 | tf_op jit(solution)/shard_map/ppermute | solution.py:42
  110.6 13.1 %collective-permute-start.27 = (bf16[7,64,128]{2,1,0:T(8,128)(2,1)S(1)}, bf16[7,64,128]{2,1,0:T(8,128)(2,1)S(1)}, u32[]{:S(2)}, u32[]{:S(2)}) collective-permute-start(bf16[7,64,128]{2,1,0:T(8,128)(2,1)S(1)} %get-tuple-element.56), channel_id=1, source_target_pairs={{0,48},{8,56},{16,0},{24,8},{32,16},{40,24},{48,32},{56,40},{64,11... | collective-permute-start | bytes 344072 | tf_op jit(solution)/shard_map/ppermute | solution.py:42
  110.6 13.1 %collective-permute-start.28 = (bf16[7,64,128]{2,1,0:T(8,128)(2,1)S(1)}, bf16[7,64,128]{2,1,0:T(8,128)(2,1)S(1)}, u32[]{:S(2)}, u32[]{:S(2)}) collective-permute-start(bf16[7,64,128]{2,1,0:T(8,128)(2,1)S(1)} %get-tuple-element.57), channel_id=1, source_target_pairs={{0,32},{8,40},{16,48},{24,56},{32,0},{40,8},{48,16},{56,24},{64,96... | collective-permute-start | bytes 344072 | tf_op jit(solution)/shard_map/ppermute | solution.py:42
  113.0 5.2 %collective-permute-start.32 = (bf16[2,64,128]{2,1,0:T(8,128)(2,1)S(1)}, bf16[2,64,128]{2,1,0:T(8,128)(2,1)S(1)}, u32[]{:S(2)}, u32[]{:S(2)}) collective-permute-start(bf16[2,64,128]{2,1,0:T(8,128)(2,1)S(1)} %get-tuple-element.63), channel_id=1, source_target_pairs={{0,64},{8,72},{16,80},{24,88},{32,96},{40,104},{48,112},{56,120},{... | collective-permute-start | bytes 98312 | tf_op jit(solution)/shard_map/ppermute | solution.py:42
  115.1 4.6 %collective-permute-start.33 = (bf16[2,64,128]{2,1,0:T(8,128)(2,1)S(1)}, bf16[2,64,128]{2,1,0:T(8,128)(2,1)S(1)}, u32[]{:S(2)}, u32[]{:S(2)}) collective-permute-start(bf16[2,64,128]{2,1,0:T(8,128)(2,1)S(1)} %get-tuple-element.64), channel_id=1, source_target_pairs={{0,192},{8,200},{16,208},{24,216},{32,224},{40,232},{48,240},{56,2... | collective-permute-start | bytes 98312 | tf_op jit(solution)/shard_map/ppermute | solution.py:42
  118.2 5.4 %collective-permute-start.34 = (bf16[2,64,128]{2,1,0:T(8,128)(2,1)S(1)}, bf16[2,64,128]{2,1,0:T(8,128)(2,1)S(1)}, u32[]{:S(2)}, u32[]{:S(2)}) collective-permute-start(bf16[2,64,128]{2,1,0:T(8,128)(2,1)S(1)} %get-tuple-element.65), channel_id=1, source_target_pairs={{0,128},{8,136},{16,144},{24,152},{32,160},{40,168},{48,176},{56,1... | collective-permute-start | bytes 98312 | tf_op jit(solution)/shard_map/ppermute | solution.py:42
  (12 other events, 151.6 us)

commit v4 on v3

--- a/solution.py
+++ b/solution.py
@@ -19,9 +19,6 @@
 NY, NZ, NC = 4, 4, 2
 EARLY = False
 LIVE = 33
-NA = 6
-NB = 8 - NA
-WIDE_A, WIDE_B = 4 * NA + 1, 4 * NB
 
 
 def row_perm(dy, dz, dc):
@@ -94,7 +91,8 @@
     out_ref[8, 32:64, :] = extra[32:64].astype(BF)
 
 
-def stack_kernel(p0, p1, p2, p3, out_ref):
+def stack_kernel(p0, p1, p2, p3, *rest):
+    out_ref = rest[-1]
     extra = jnp.zeros((64, 128), F32)
     for i, p in enumerate((p0, p1, p2, p3)):
         out_ref[i * 8 : (i + 1) * 8] = p[0:8]
@@ -112,9 +110,7 @@
     return first
 
 
-def pair_kernel(up_ref, far_ref, w_ref, tiles_ref, _, pair_ref, wt_ref, own_ref, held):
-    pair_ref[0:64, :] = up_ref[...]
-    pair_ref[64:128, :] = far_ref[...]
+def weight_kernel(w_ref, tiles_ref, _, wt_ref, own_ref, held):
     first = group_rows()
     for j in range(8):
         held[j * 64 : (j + 1) * 64, :] = w_ref[pl.ds(first[j], 64), :]
@@ -177,8 +173,8 @@
 
 
 def mid_kernel(*rest):
-    aggs, ups = rest[:8], rest[8:12]
-    wt_ref, own_ref, adj_ref, act_ref, ga_ref, hub_ref, full, pre, down = rest[12:]
+    aggs, ups = rest[:8], rest[8:16]
+    wt_ref, own_ref, adj_ref, act_ref, ga_ref, hub_ref, full, pre, down = rest[16:]
     hubs = jnp.zeros((64, 512), F32)
     for j in range(8):
         full[j * 64 : (j + 1) * 64, :] = aggs[j][...]
@@ -196,7 +192,7 @@
             slope = half + (0.5 * v) * (1.0 - t * t) * (
                 0.7978845608 + (0.7978845608 * 3 * 0.044715) * sq
             )
-            up = ups[j % 4][(j // 4) * 64 : (j // 4 + 1) * 64, cols]
+            up = ups[j][:, cols]
             down[n % 2, rows] = (up.astype(F32) * slope).astype(BF)
         grads = dot(own_ref[0:64, :], down[n % 2]).astype(BF)
         ga_ref[2 * n] = grads[:, :128]
@@ -206,7 +202,7 @@
         hub_ref[j] = hubs[:, j * 128 : (j + 1) * 128]
 
 
-GROUPS = ((1, 3), (0, 2))
+GROUPS = ((3, 0), (1, 2))
 
 
 def back_kernel(swap, part, ints_ref, sb0_ref, sb1_ref, ga_ref, tiles_ref, hub_ref, *rest):
@@ -244,42 +240,45 @@
 
 def add_first_kernel(a, b, *outs):
     for g in range(2):
-        for i in range(4):
-            for r in range(NA):
-                outs[g][i * NA + r] = both(a, b, (g * 4 + i) * 8 + r)
-        outs[g][4 * NA] = both(a, b, 64 + g)
-
-
-def add_second_kernel(a0, b0, a, b, *outs):
-    add_first_kernel(a, b, *outs[:2])
-    for part, (p, q) in enumerate(((a0, b0), (a, b))):
-        for g, j in enumerate(GROUPS[part]):
-            for i in range(4):
-                for r in range(NB):
-                    outs[2 + i][j * NB + r] = both(p, q, (g * 4 + i) * 8 + NA + r)
+        for r in range(32):
+            outs[g][r] = both(a, b, g * 32 + r)
+        outs[g][32] = both(a, b, 64 + g)
+
+
+def add_second_kernel(a, b, *outs):
+    hubs = both(a, b, 64)
+    for i in range(4):
+        for r in range(8):
+            outs[i][r] = both(a, b, i * 8 + r)
+        outs[i][8] = hubs
+    for r in range(32):
+        outs[4][r] = both(a, b, 32 + r)
+    outs[4][32] = both(a, b, 65)
 
 
 def four(refs, r):
     return (refs[0][r].astype(F32) + refs[1][r].astype(F32)) + (refs[2][r].astype(F32) + refs[3][r].astype(F32))
 
 
-def sum_a_kernel(*refs):
-    hubs = four(refs[:4], 4 * NA).astype(BF)
+def sum_near_kernel(a, b, c, *outs):
+    def three(r):
+        return (a[r].astype(F32) + (b[r].astype(F32) + c[r].astype(F32))).astype(BF)
+
+    hubs = three(32)
     for i in range(4):
-        for b in range(NA):
-            refs[4 + i][b] = four(refs[:4], i * NA + b).astype(BF)
-        refs[4 + i][NA] = hubs
-
-
-def sum_b_kernel(*refs):
-    for j in range(4):
-        for b in range(NB):
-            refs[4 + j][b] = four(refs[:4], j * NB + b).astype(BF)
+        for r in range(8):
+            outs[i][r] = three(i * 8 + r)
+        outs[i][8] = hubs
+
+
+def sum_far_kernel(*refs):
+    for r in range(9):
+        refs[-1][r] = four(refs[:4], r).astype(BF)
 
 
 def last_kernel(*rest):
-    pas, pbs = rest[:4], rest[4:8]
-    ga_ref, self_ref, ids_ref, out_ref = rest[8:]
+    near, far = rest[:4], rest[4]
+    ga_ref, self_ref, ids_ref, out_ref = rest[5:]
     _, z, c = here()
 
     def halves(v):
@@ -289,14 +288,14 @@
     lane = lax.broadcasted_iota(jnp.int32, (128, 16), 0)
     which = lax.broadcasted_iota(jnp.int32, (128, 16), 1)
     take = (lane == (z * 2 + c) * 16 + which).astype(F32).astype(BF)
-    high, low = halves(four(pas, NA))
+    high, low = halves(four(near, 8) + far[8].astype(F32))
     high, low = halves(dot(high, take) + dot(low, take))
     node = lax.broadcasted_iota(jnp.int32, (1024, 16), 0)
     spread = (node == ids_ref[...]).astype(F32).astype(BF)
     hubs = dot_nt(high, spread) + dot_nt(low, spread)
     for b in range(8):
         cols = slice(b * 128, (b + 1) * 128)
-        total = four(pas, b) if b < NA else four(pbs, b - NA)
+        total = four(near, b) + far[b].astype(F32)
         out_ref[:, cols] = (ga_ref[b].astype(F32) * self_ref[:, cols] + hubs[:, cols] + total).astype(BF)
 
 
@@ -344,13 +343,16 @@
 
     (p0,) = call(prep_kernel, "prep", [shape(9)], (node_feats, ints))
     ps = [p0] + [row_send(p0, 0, k, 0) for k in STEPS[1:]]
-    (s0,) = call(stack_kernel, "stack", [shape(LIVE)], ps)
+    up_late, _ = lax.optimization_barrier((grad_out, p0))
+    up_near = [lax.ppermute(up_late, "feat", feat_perm(0, k)) for k in STEPS[1:]]
+    (s0,) = call(stack_kernel, "stack", [shape(LIVE)], (*ps, *up_near), loose=3)
     owns = [s0] + [row_send(s0, k, 0, 0) for k in STEPS[1:]]
+    swap0 = row_send(s0, 0, 0, 1)
     up, _ = lax.optimization_barrier((grad_out, s0))
     up_far = lax.ppermute(up, "feat", feat_perm(1, 0))
-    pair, wt, own = call(
-        pair_kernel, "pair", [((128, 1024), BF), ((512, 512), BF), ((128, 512), BF)],
-        (grad_out, up_far, weight, tiles, s0), 0, [pltpu.VMEM((512, 512), BF)], 12, loose=1,
+    wt, own = call(
+        weight_kernel, "weights", [((512, 512), BF), ((128, 512), BF)],
+        (weight, tiles, s0), 0, [pltpu.VMEM((512, 512), BF)], 12, loose=1,
     )
     slots = [
         pltpu.VMEM((9, 64, 128), F32),
@@ -359,16 +361,17 @@
         pltpu.SemaphoreType.DMA,
     ]
     listed = ((4, 16), jnp.int32)
-    swaps = [row_send(v, 0, 0, 1) for v in owns[:2]]
+    swaps = [swap0, row_send(owns[1], 0, 0, 1)]
     part, sb0 = call(
         functools.partial(agg_kernel, 0), "agg_first", [((8, 64, 128), F32), listed],
         (ints, *owns[:2], *swaps, tiles, hub_adjacency, node_feats, self_row), 1, slots, 16, [VM, SM], 8 * MIB,
     )
-    later, _ = lax.optimization_barrier((pair, part)) if EARLY else (pair, part)
-    ups = [pair] + [lax.ppermute(v, "feat", feat_perm(0, k)) for v, k in zip((pair, pair, later), (2, 1, 3))]
-    ups = [ups[0], ups[2], ups[3], ups[1]]
-    late = lax.optimization_barrier((owns[3], *ups))
-    owns[3], ups = late[0], late[1:]
+    later, _ = lax.optimization_barrier((up_far, own))
+    up_two = lax.ppermute(up_far, "feat", feat_perm(0, 2))
+    up_one = lax.ppermute(up_far, "feat", feat_perm(0, 1))
+    up_three = lax.ppermute(later, "feat", feat_perm(0, 3))
+    owns[3], *up_far = lax.optimization_barrier((owns[3], up_far, up_one, up_three, up_two))
+    ups = [grad_out, *up_near, *up_far]
     swaps = [row_send(v, 0, 0, 1) for v in owns[2:]]
     agg, sb1 = call(
         functools.partial(agg_kernel, 1), "agg_second", [((64, 1024), BF), listed],
@@ -398,20 +401,16 @@
     swap1 = back(True, 1, swap0)
     came1 = row_send(swap1, 0, 0, 1)
     own0 = back(False, 0, swap1)
-    sums = [None] * 4
-    sums[1], sums[3] = call(add_first_kernel, "add_first", [shape(WIDE_A)] * 2, (own0, came0))
-    own1 = back(False, 1, sums[3])
-    sums[0], sums[2], *bs = call(
-        add_second_kernel, "add_second", [shape(WIDE_A)] * 2 + [shape(WIDE_B)] * 4, (own0, came0, own1, came1), 0, (), 12
-    )
-    both = [*sums, *bs]
-    ras = [both[0]] + [row_send(both[j], STEPS[j], 0, 0) for j in (1, 2, 3)]
-    rbs = [both[4]] + [row_send(both[4 + i], 0, STEPS[i], 0) for i in (1, 2, 3)]
-    zas = call(sum_a_kernel, "sum_a", [shape(NA + 1)] * 4, ras)
-    ybs = call(sum_b_kernel, "sum_b", [shape(NB)] * 4, rbs)
-    zas = [zas[0]] + [row_send(zas[i], 0, STEPS[i], 0) for i in (1, 2, 3)]
-    ybs = [ybs[0]] + [row_send(ybs[j], STEPS[j], 0, 0) for j in (1, 2, 3)]
-    (grad_in,) = call(last_kernel, "last", [((64, 1024), BF)], (*zas, *ybs, ga, self_row, ids))
+    *far_sums, near_sum = call(add_second_kernel, "add_first", [shape(9)] * 4 + [shape(LIVE)], (own0, came0), 0, (), 12)
+    own1 = back(False, 1, near_sum)
+    up_sum, down_sum = call(add_first_kernel, "add_second", [shape(LIVE)] * 2, (own1, came1))
+    fars = [far_sums[0]] + [row_send(far_sums[i], 0, STEPS[i], 0) for i in (1, 2, 3)]
+    nears = (near_sum, row_send(up_sum, 1, 0, 0), row_send(down_sum, 3, 0, 0))
+    zs = call(sum_near_kernel, "sum_near", [shape(9)] * 4, nears)
+    (far,) = call(sum_far_kernel, "sum_far", [shape(9)], (*fars, zs[0]), loose=1)
+    zs = [zs[0]] + [row_send(zs[i], 0, STEPS[i], 0) for i in (1, 2, 3)]
+    far = row_send(far, 2, 0, 0)
+    (grad_in,) = call(last_kernel, "last", [((64, 1024), BF)], (*zs, far, ga, self_row, ids))
     return (act, grad_in)
 
 

time: 125 us -> 121 us (0.968); the launches traced: 125 us -> 119 us
  starting transfers between devices: 62.3 us -> 57.3 us
    ppermute x24 -> x21, starting transfers between devices: 42.6 us -> 28.2 us  [row_send(): return lax.ppermute(value, 'row', row_perm(dy, dz, dc))]
    ppermute x1, waiting for transfers between devices: 0.01 us -> 5.32 us  [shards(): up_far = lax.ppermute(up, 'feat', feat_perm(1, 0))]
    ppermute x3 -> x6, starting transfers between devices: 3.65 us -> 8.65 us  [the longest x3 4.25 us: shards(): lax.ppermute(up_late, 'feat', feat_perm(0, k))]
    ppermute x1, starting transfers between devices: 1.63 us -> 6.44 us  [feat_gather(): across = lax.ppermute(value, 'feat', feat_perm(1, 0))]
    ppermute x3 -> x6, waiting for transfers between devices: 12.7 us -> 8.61 us  [the longest x3 4.59 us: shards(): lax.ppermute(up_late, 'feat', feat_perm(0, k))]
    ppermute x3, waiting for transfers between devices: 0.01 us -> 3.46 us  [feat_gather(): near = [lax.ppermute(value, 'feat', feat_perm(0, k)) for k in STEPS[1:]]]
    ppermute x1, waiting for transfers between devices: 3.32 us -> 0.01 us  [feat_gather(): across = lax.ppermute(value, 'feat', feat_perm(1, 0))]
    ppermute x24 -> x21, waiting for transfers between devices: 20.7 us -> 19.8 us  [row_send(): return lax.ppermute(value, 'row', row_perm(dy, dz, dc))]
  transfers between devices with their start and end apart: 35 -> 35, of which waited for: 15 -> 17; matrix products, arithmetic and copies ran while one was open for 0% -> 0% of each run, Pallas kernels for 6% -> 6%
where the time goes in v4:
time: 121 us; the launch traced here: 119 us
  starting transfers between devices  57.3 us (47%)
  waiting for transfers between devices  40.7 us (34%)
  Pallas kernels  16.5 us (14%)
  local copies, waits for them, and re-layouts  3.12 us (3%)
    ppermute x21, starting transfers between devices, row_send(): return lax.ppermute(value, 'row', row_perm(dy, dz, dc))  28.2 us
    ppermute x21, waiting for transfers between devices, row_send(): return lax.ppermute(value, 'row', row_perm(dy, dz, dc))  19.8 us
    pallas_call x15, Pallas kernels, call(): pl.pallas_call(kernel, out_shape=shapes, in_specs=[HB] * hbm + [SM] * sca...  16.5 us
    ppermute x1, starting transfers between devices, feat_gather(): across = lax.ppermute(value, 'feat', feat_perm(1, 0))  6.44 us
    ppermute x1, starting transfers between devices, shards(): up_far = lax.ppermute(up, 'feat', feat_perm(1, 0))  5.68 us
    ppermute x1, waiting for transfers between devices, shards(): up_far = lax.ppermute(up, 'feat', feat_perm(1, 0))  5.32 us
    ppermute x3, starting transfers between devices, feat_gather(): near = [lax.ppermute(value, 'feat', feat_perm(0, k)) for k in STEPS[1:]]  4.64 us
    ppermute x3, waiting for transfers between devices, shards(): lax.ppermute(up_late, 'feat', feat_perm(0, k))  4.59 us
  transfers between devices with their start and end apart: 35, of which 17 were waited for; matrix products, arithmetic and copies ran while one was open for 0% of the time, Pallas kernels for 6%

profile of v4, /device:TPU:2, one launch (start us, length us, event | category | flops | bytes accessed | tf_op | source)
XLA Modules:
  0.0 119.3 jit_solution(788749431887085522)
XLA Ops:
  2.6 2.2 %collective-permute-start.5 = (bf16[64,1024]{1,0:T(8,128)(2,1)}, bf16[64,1024]{1,0:T(8,128)(2,1)S(1)}, u32[]{:S(2)}, u32[]{:S(2)}) collective-permute-start(bf16[64,1024]{1,0:T(8,128)(2,1)} %rest_8_.1), channel_id=1, source_target_pairs={{0,2},{1,3},{2,0},{3,1},{4,6},{5,7},{6,4},{7,5},{8,10},{9,11},{10,... | collective-permute-start | bytes 393224 | tf_op jit(solution)/shard_map/ppermute | solution.py:347
  4.8 3.3 %collective-permute-start.2 = (bf16[9,64,128]{2,1,0:T(8,128)(2,1)S(1)}, bf16[9,64,128]{2,1,0:T(8,128)(2,1)S(1)}, u32[]{:S(2)}, u32[]{:S(2)}) collective-permute-start(bf16[9,64,128]{2,1,0:T(8,128)(2,1)S(1)} %prep.1.p0), channel_id=1, source_target_pairs={{0,32},{8,40},{16,48},{24,56},{32,0},{40,8},{48,16},{56,24},{64,96... | collective-permute-start | bytes 442376 | tf_op jit(solution)/shard_map/ppermute | solution.py:39
  10.1 1.4 %collective-permute-start.4 = (bf16[64,1024]{1,0:T(8,128)(2,1)}, bf16[64,1024]{1,0:T(8,128)(2,1)S(1)}, u32[]{:S(2)}, u32[]{:S(2)}) collective-permute-start(bf16[64,1024]{1,0:T(8,128)(2,1)} %rest_8_.1), channel_id=1, source_target_pairs={{0,3},{1,0},{2,1},{3,2},{4,7},{5,4},{6,5},{7,6},{8,11},{9,8},{10,9... | collective-permute-start | bytes 393224 | tf_op jit(solution)/shard_map/ppermute | solution.py:347
  12.2 3.1 %collective-permute-done.4.rest_1_.rest_10_ = bf16[64,1024]{1,0:T(8,128)(2,1)S(1)} collective-permute-done((bf16[64,1024]{1,0:T(8,128)(2,1)}, bf16[64,1024]{1,0:T(8,128)(2,1)S(1)}, u32[]{:S(2)}, u32[]{:S(2)}) %collective-permute-start.4) | collective-permute-done | bytes 131104 | tf_op jit(solution)/shard_map/ppermute | solution.py:347
  15.3 1.4 %collective-permute-done.3.rest_0_.rest_9_ = bf16[64,1024]{1,0:T(8,128)(2,1)S(1)} collective-permute-done((bf16[64,1024]{1,0:T(8,128)(2,1)}, bf16[64,1024]{1,0:T(8,128)(2,1)S(1)}, u32[]{:S(2)}, u32[]{:S(2)}) %collective-permute-start.3) | collective-permute-done | bytes 131104 | tf_op jit(solution)/shard_map/ppermute | solution.py:347
  16.8 2.7 %collective-permute-done.p1 = bf16[9,64,128]{2,1,0:T(8,128)(2,1)S(1)} collective-permute-done((bf16[9,64,128]{2,1,0:T(8,128)(2,1)S(1)}, bf16[9,64,128]{2,1,0:T(8,128)(2,1)S(1)}, u32[]{:S(2)}, u32[]{:S(2)}) %collective-permute-start) | collective-permute-done | bytes 147488 | tf_op jit(solution)/shard_map/ppermute | solution.py:39
  19.6 1.7 %collective-permute-start.14 = (bf16[33,64,128]{2,1,0:T(8,128)(2,1)S(1)}, bf16[33,64,128]{2,1,0:T(8,128)(2,1)S(1)}, u32[]{:S(2)}, u32[]{:S(2)}) collective-permute-start(bf16[33,64,128]{2,1,0:T(8,128)(2,1)S(1)} %stack.1._.rest_0_), channel_id=1, source_target_pairs={{0,64},{8,72},{16,80},{24,88},{32,96},{40,104},{48,112},{56,120},{... | collective-permute-start | bytes 1622024 | tf_op jit(solution)/shard_map/ppermute | solution.py:39
  21.2 2.9 %collective-permute-start.7 = (bf16[33,64,128]{2,1,0:T(8,128)(2,1)S(1)}, bf16[33,64,128]{2,1,0:T(8,128)(2,1)S(1)}, u32[]{:S(2)}, u32[]{:S(2)}) collective-permute-start(bf16[33,64,128]{2,1,0:T(8,128)(2,1)S(1)} %stack.1._.rest_0_), channel_id=1, source_target_pairs={{0,128},{8,136},{16,144},{24,152},{32,160},{40,168},{48,176},{56,1... | collective-permute-start | bytes 1622024 | tf_op jit(solution)/shard_map/ppermute | solution.py:39
  25.5 5.7 %collective-permute-start.8 = (bf16[64,1024]{1,0:T(8,128)(2,1)S(1)}, bf16[64,1024]{1,0:T(8,128)(2,1)S(1)}, u32[]{:S(2)}, u32[]{:S(2)}) collective-permute-start(bf16[64,1024]{1,0:T(8,128)(2,1)S(1)} %copy-done.6), channel_id=1, source_target_pairs={{0,4},{1,5},{2,6},{3,7},{4,0},{5,1},{6,2},{7,3},{8,12},{9,13},{10,... | collective-permute-start | bytes 393224 | tf_op jit(solution)/shard_map/ppermute | solution.py:352
  31.1 5.3 %collective-permute-done.8.rest_12_ = bf16[64,1024]{1,0:T(8,128)(2,1)S(1)} collective-permute-done((bf16[64,1024]{1,0:T(8,128)(2,1)S(1)}, bf16[64,1024]{1,0:T(8,128)(2,1)S(1)}, u32[]{:S(2)}, u32[]{:S(2)}) %collective-permute-start.8) | collective-permute-done | bytes 131104 | tf_op jit(solution)/shard_map/ppermute | solution.py:352
  37.9 2.2 %copy-done = bf16[1,32,4,128,128]{4,3,2,1,0:T(8,128)(2,1)S(1)} copy-done((bf16[1,32,4,128,128]{4,3,2,1,0:T(8,128)(2,1)S(1)}, bf16[1,32,4,128,128]{4,3,2,1,0:T(8,128)(2,1)}, u32[]{:S(2)}) %copy-start) | copy-done | bytes 4194328
  40.4 1.6 %collective-permute-start.9 = (bf16[64,1024]{1,0:T(8,128)(2,1)S(1)}, bf16[64,1024]{1,0:T(8,128)(2,1)S(1)}, u32[]{:S(2)}, u32[]{:S(2)}) collective-permute-start(bf16[64,1024]{1,0:T(8,128)(2,1)S(1)} %collective-permute-done.8.rest_12_), channel_id=1, source_target_pairs={{0,1},{1,2},{2,3},{3,0},{4,5},{5,6},{6,7},{7,4},{8,9},{9,10},{10,1... | collective-permute-start | bytes 393224 | tf_op jit(solution)/shard_map/ppermute | solution.py:371
  42.9 1.4 %collective-permute-start.10 = (bf16[64,1024]{1,0:T(8,128)(2,1)S(1)}, bf16[64,1024]{1,0:T(8,128)(2,1)S(1)}, u32[]{:S(2)}, u32[]{:S(2)}) collective-permute-start(bf16[64,1024]{1,0:T(8,128)(2,1)S(1)} %collective-permute-done.8.rest_12_), channel_id=1, source_target_pairs={{0,3},{1,0},{2,1},{3,2},{4,7},{5,4},{6,5},{7,6},{8,11},{9,8},{10,9... | collective-permute-start | bytes 393224 | tf_op jit(solution)/shard_map/ppermute | solution.py:372
  45.9 2.0 %collective-permute-done.10.rest_14_ = bf16[64,1024]{1,0:T(8,128)(2,1)S(1)} collective-permute-done((bf16[64,1024]{1,0:T(8,128)(2,1)S(1)}, bf16[64,1024]{1,0:T(8,128)(2,1)S(1)}, u32[]{:S(2)}, u32[]{:S(2)}) %collective-permute-start.10) | collective-permute-done | bytes 131104 | tf_op jit(solution)/shard_map/ppermute | solution.py:372
  48.5 2.7 %agg_first.1 = (f32[8,64,128]{2,1,0:T(8,128)S(1)}, s32[4,16]{1,0:T(4,128)S(1)}) custom-call(s32[10,32]{1,0:T(8,128)S(1)} %add_add_fusion.ints_ref, bf16[33,64,128]{2,1,0:T(8,128)(2,1)S(1)} %stack.1._.rest_0_, bf16[33,64,128]{2,1,0:T(8,128)(2,1)S(1)} %collective-permute-done.14.rest_1_, bf16[33,64,128]{2,1,0:T(8,128)(2,1)S(1)} %collective-permute-done.15.rest_2_, ...), custom_call_target="tpu_custom_call" | custom-call | bytes 8388608 | tf_op jit(solution)/shard_map/agg_first/pallas_call | solution.py:304
  51.2 2.7 %agg_second.1 = (bf16[64,1024]{1,0:T(8,128)(2,1)S(1)}, s32[4,16]{1,0:T(4,128)S(1)}) custom-call(s32[10,32]{1,0:T(8,128)S(1)} %add_add_fusion.ints_ref, bf16[33,64,128]{2,1,0:T(8,128)(2,1)S(1)} %collective-permute-done.6.rest_0_, bf16[33,64,128]{2,1,0:T(8,128)(2,1)S(1)} %collective-permute-done.7.rest_1_, ...), custom_call_target="tpu_custom_call" | custom-call | bytes 8388608 | tf_op jit(solution)/shard_map/agg_second/pallas_call | solution.py:304
  53.8 6.4 %collective-permute-start.20 = (bf16[64,1024]{1,0:T(8,128)(2,1)S(1)}, bf16[64,1024]{1,0:T(8,128)(2,1)S(1)}, u32[]{:S(2)}, u32[]{:S(2)}) collective-permute-start(bf16[64,1024]{1,0:T(8,128)(2,1)S(1)} %get-tuple-element.36.rest_0_), channel_id=1, source_target_pairs={{0,4},{1,5},{2,6},{3,7},{4,0},{5,1},{6,2},{7,3},{8,12},{9,13},{10,... | collective-permute-start | bytes 393224 | tf_op jit(solution)/shard_map/ppermute | solution.py:43
  60.3 2.6 %collective-permute-start.19 = (bf16[64,1024]{1,0:T(8,128)(2,1)S(1)}, bf16[64,1024]{1,0:T(8,128)(2,1)S(1)}, u32[]{:S(2)}, u32[]{:S(2)}) collective-permute-start(bf16[64,1024]{1,0:T(8,128)(2,1)S(1)} %get-tuple-element.36.rest_0_), channel_id=1, source_target_pairs={{0,2},{1,3},{2,0},{3,1},{4,6},{5,7},{6,4},{7,5},{8,10},{9,11},{10,... | collective-permute-start | bytes 393224 | tf_op jit(solution)/shard_map/ppermute | solution.py:44
  64.9 2.1 %collective-permute-start.23 = (bf16[64,1024]{1,0:T(8,128)(2,1)S(1)}, bf16[64,1024]{1,0:T(8,128)(2,1)S(1)}, u32[]{:S(2)}, u32[]{:S(2)}) collective-permute-start(bf16[64,1024]{1,0:T(8,128)(2,1)S(1)} %collective-permute-done.20.rest_4_), channel_id=1, source_target_pairs={{0,2},{1,3},{2,0},{3,1},{4,6},{5,7},{6,4},{7,5},{8,10},{9,11},{10,... | collective-permute-start | bytes 393224 | tf_op jit(solution)/shard_map/ppermute | solution.py:45
  69.3 2.7 %collective-permute-done.18.rest_2_ = bf16[64,1024]{1,0:T(8,128)(2,1)S(1)} collective-permute-done((bf16[64,1024]{1,0:T(8,128)(2,1)S(1)}, bf16[64,1024]{1,0:T(8,128)(2,1)S(1)}, u32[]{:S(2)}, u32[]{:S(2)}) %collective-permute-start.18) | collective-permute-done | bytes 131104 | tf_op jit(solution)/shard_map/ppermute | solution.py:44
  72.1 1.7 %collective-permute-done.23.rest_7_ = bf16[64,1024]{1,0:T(8,128)(2,1)S(1)} collective-permute-done((bf16[64,1024]{1,0:T(8,128)(2,1)S(1)}, bf16[64,1024]{1,0:T(8,128)(2,1)S(1)}, u32[]{:S(2)}, u32[]{:S(2)}) %collective-permute-start.23) | collective-permute-done | bytes 131104 | tf_op jit(solution)/shard_map/ppermute | solution.py:45
  73.8 1.8 %collective-permute-done.22.rest_6_ = bf16[64,1024]{1,0:T(8,128)(2,1)S(1)} collective-permute-done((bf16[64,1024]{1,0:T(8,128)(2,1)S(1)}, bf16[64,1024]{1,0:T(8,128)(2,1)S(1)}, u32[]{:S(2)}, u32[]{:S(2)}) %collective-permute-start.22) | collective-permute-done | bytes 131104 | tf_op jit(solution)/shard_map/ppermute | solution.py:45
  75.6 3.3 %middle.1 = (bf16[64,1024]{1,0:T(8,128)(2,1)}, bf16[8,64,128]{2,1,0:T(8,128)(2,1)S(1)}, f32[4,64,128]{2,1,0:T(8,128)S(1)}) custom-call(bf16[64,1024]{1,0:T(8,128)(2,1)S(1)} %get-tuple-element.36.rest_0_, bf16[64,1024]{1,0:T(8,128)(2,1)S(1)} %collective-permute-done.17.rest_1_, bf16[64,1024]{1,0:T(8,128)(2,1)S(1)} %collective-permute-done.18.rest_2_, ...), custom_call_target="tpu_custom_call" | custom-call | bytes 16777216 | tf_op jit(solution)/shard_map/middle/pallas_call | solution.py:304
  86.5 2.6 %collective-permute-start.27 = (bf16[33,64,128]{2,1,0:T(8,128)(2,1)S(1)}, bf16[33,64,128]{2,1,0:T(8,128)(2,1)S(1)}, u32[]{:S(2)}, u32[]{:S(2)}) collective-permute-start(bf16[33,64,128]{2,1,0:T(8,128)(2,1)S(1)} %get-tuple-element.49), channel_id=1, source_target_pairs={{0,192},{8,200},{16,208},{24,216},{32,224},{40,232},{48,240},{56,2... | collective-permute-start | bytes 1622024 | tf_op jit(solution)/shard_map/ppermute | solution.py:39
  89.1 2.5 %collective-permute-start.31 = (bf16[9,64,128]{2,1,0:T(8,128)(2,1)S(1)}, bf16[9,64,128]{2,1,0:T(8,128)(2,1)S(1)}, u32[]{:S(2)}, u32[]{:S(2)}) collective-permute-start(bf16[9,64,128]{2,1,0:T(8,128)(2,1)S(1)} %get-tuple-element.55), channel_id=1, source_target_pairs={{0,16},{8,24},{16,32},{24,40},{32,48},{40,56},{48,0},{56,8},{64,80... | collective-permute-start | bytes 442376 | tf_op jit(solution)/shard_map/ppermute | solution.py:39
  92.9 1.7 %collective-permute-start.33 = (bf16[9,64,128]{2,1,0:T(8,128)(2,1)S(1)}, bf16[9,64,128]{2,1,0:T(8,128)(2,1)S(1)}, u32[]{:S(2)}, u32[]{:S(2)}) collective-permute-start(bf16[9,64,128]{2,1,0:T(8,128)(2,1)S(1)} %get-tuple-element.57), channel_id=1, source_target_pairs={{0,32},{8,40},{16,48},{24,56},{32,0},{40,8},{48,16},{56,24},{64,96... | collective-permute-start | bytes 442376 | tf_op jit(solution)/shard_map/ppermute | solution.py:39
  94.6 6.6 %collective-permute-done.26.b = bf16[33,64,128]{2,1,0:T(8,128)(2,1)S(1)} collective-permute-done((bf16[33,64,128]{2,1,0:T(8,128)(2,1)S(1)}, bf16[33,64,128]{2,1,0:T(8,128)(2,1)S(1)}, u32[]{:S(2)}, u32[]{:S(2)}) %collective-permute-start.26) | collective-permute-done | bytes 540704 | tf_op jit(solution)/shard_map/ppermute | solution.py:39
  101.4 2.5 %collective-permute-start.28 = (bf16[9,64,128]{2,1,0:T(8,128)(2,1)S(1)}, bf16[9,64,128]{2,1,0:T(8,128)(2,1)S(1)}, u32[]{:S(2)}, u32[]{:S(2)}) collective-permute-start(bf16[9,64,128]{2,1,0:T(8,128)(2,1)S(1)} %get-tuple-element.51), channel_id=1, source_target_pairs={{0,16},{8,24},{16,32},{24,40},{32,48},{40,56},{48,0},{56,8},{64,80... | collective-permute-start | bytes 442376 | tf_op jit(solution)/shard_map/ppermute | solution.py:39
  105.3 1.7 %collective-permute-start.30 = (bf16[9,64,128]{2,1,0:T(8,128)(2,1)S(1)}, bf16[9,64,128]{2,1,0:T(8,128)(2,1)S(1)}, u32[]{:S(2)}, u32[]{:S(2)}) collective-permute-start(bf16[9,64,128]{2,1,0:T(8,128)(2,1)S(1)} %get-tuple-element.53), channel_id=1, source_target_pairs={{0,32},{8,40},{16,48},{24,56},{32,0},{40,8},{48,16},{56,24},{64,96... | collective-permute-start | bytes 442376 | tf_op jit(solution)/shard_map/ppermute | solution.py:39
  108.7 1.5 %collective-permute-done.28.rest_1_ = bf16[9,64,128]{2,1,0:T(8,128)(2,1)S(1)} collective-permute-done((bf16[9,64,128]{2,1,0:T(8,128)(2,1)S(1)}, bf16[9,64,128]{2,1,0:T(8,128)(2,1)S(1)}, u32[]{:S(2)}, u32[]{:S(2)}) %collective-permute-start.28) | collective-permute-done | bytes 147488 | tf_op jit(solution)/shard_map/ppermute | solution.py:39
  110.1 1.7 %collective-permute-done.29.rest_2_ = bf16[9,64,128]{2,1,0:T(8,128)(2,1)S(1)} collective-permute-done((bf16[9,64,128]{2,1,0:T(8,128)(2,1)S(1)}, bf16[9,64,128]{2,1,0:T(8,128)(2,1)S(1)}, u32[]{:S(2)}, u32[]{:S(2)}) %collective-permute-start.29) | collective-permute-done | bytes 147488 | tf_op jit(solution)/shard_map/ppermute | solution.py:39
  111.9 6.3 %collective-permute-done.30.rest_3_ = bf16[9,64,128]{2,1,0:T(8,128)(2,1)S(1)} collective-permute-done((bf16[9,64,128]{2,1,0:T(8,128)(2,1)S(1)}, bf16[9,64,128]{2,1,0:T(8,128)(2,1)S(1)}, u32[]{:S(2)}, u32[]{:S(2)}) %collective-permute-start.30) | collective-permute-done | bytes 147488 | tf_op jit(solution)/shard_map/ppermute | solution.py:39
  (72 shorter events, 28.4 us)
Async XLA Ops:
  2.6 9.0 %collective-permute-start.5 = (bf16[64,1024]{1,0:T(8,128)(2,1)}, bf16[64,1024]{1,0:T(8,128)(2,1)S(1)}, u32[]{:S(2)}, u32[]{:S(2)}) collective-permute-start(bf16[64,1024]{1,0:T(8,128)(2,1)} %rest_8_.1), channel_id=1, source_target_pairs={{0,2},{1,3},{2,0},{3,1},{4,6},{5,7},{6,4},{7,5},{8,10},{9,11},{10,... | collective-permute-start | bytes 393224 | tf_op jit(solution)/shard_map/ppermute | solution.py:347
  4.8 12.0 %collective-permute-start.2 = (bf16[9,64,128]{2,1,0:T(8,128)(2,1)S(1)}, bf16[9,64,128]{2,1,0:T(8,128)(2,1)S(1)}, u32[]{:S(2)}, u32[]{:S(2)}) collective-permute-start(bf16[9,64,128]{2,1,0:T(8,128)(2,1)S(1)} %prep.1.p0), channel_id=1, source_target_pairs={{0,32},{8,40},{16,48},{24,56},{32,0},{40,8},{48,16},{56,24},{64,96... | collective-permute-start | bytes 442376 | tf_op jit(solution)/shard_map/ppermute | solution.py:39
  8.1 8.7 %collective-permute-start.1 = (bf16[9,64,128]{2,1,0:T(8,128)(2,1)S(1)}, bf16[9,64,128]{2,1,0:T(8,128)(2,1)S(1)}, u32[]{:S(2)}, u32[]{:S(2)}) collective-permute-start(bf16[9,64,128]{2,1,0:T(8,128)(2,1)S(1)} %prep.1.p0), channel_id=1, source_target_pairs={{0,48},{8,56},{16,0},{24,8},{32,16},{40,24},{48,32},{56,40},{64,11... | collective-permute-start | bytes 442376 | tf_op jit(solution)/shard_map/ppermute | solution.py:39
  9.5 10.0 %collective-permute-start = (bf16[9,64,128]{2,1,0:T(8,128)(2,1)S(1)}, bf16[9,64,128]{2,1,0:T(8,128)(2,1)S(1)}, u32[]{:S(2)}, u32[]{:S(2)}) collective-permute-start(bf16[9,64,128]{2,1,0:T(8,128)(2,1)S(1)} %prep.1.p0), channel_id=1, source_target_pairs={{0,16},{8,24},{16,32},{24,40},{32,48},{40,56},{48,0},{56,8},{64,80... | collective-permute-start | bytes 442376 | tf_op jit(solution)/shard_map/ppermute | solution.py:39
  10.1 5.2 %collective-permute-start.4 = (bf16[64,1024]{1,0:T(8,128)(2,1)}, bf16[64,1024]{1,0:T(8,128)(2,1)S(1)}, u32[]{:S(2)}, u32[]{:S(2)}) collective-permute-start(bf16[64,1024]{1,0:T(8,128)(2,1)} %rest_8_.1), channel_id=1, source_target_pairs={{0,3},{1,0},{2,1},{3,2},{4,7},{5,4},{6,5},{7,6},{8,11},{9,8},{10,9... | collective-permute-start | bytes 393224 | tf_op jit(solution)/shard_map/ppermute | solution.py:347
  11.6 5.2 %collective-permute-start.3 = (bf16[64,1024]{1,0:T(8,128)(2,1)}, bf16[64,1024]{1,0:T(8,128)(2,1)S(1)}, u32[]{:S(2)}, u32[]{:S(2)}) collective-permute-start(bf16[64,1024]{1,0:T(8,128)(2,1)} %rest_8_.1), channel_id=1, source_target_pairs={{0,1},{1,2},{2,3},{3,0},{4,5},{5,6},{6,7},{7,4},{8,9},{9,10},{10,1... | collective-permute-start | bytes 393224 | tf_op jit(solution)/shard_map/ppermute | solution.py:347
  19.6 25.9 %collective-permute-start.14 = (bf16[33,64,128]{2,1,0:T(8,128)(2,1)S(1)}, bf16[33,64,128]{2,1,0:T(8,128)(2,1)S(1)}, u32[]{:S(2)}, u32[]{:S(2)}) collective-permute-start(bf16[33,64,128]{2,1,0:T(8,128)(2,1)S(1)} %stack.1._.rest_0_), channel_id=1, source_target_pairs={{0,64},{8,72},{16,80},{24,88},{32,96},{40,104},{48,112},{56,120},{... | collective-permute-start | bytes 1622024 | tf_op jit(solution)/shard_map/ppermute | solution.py:39
  21.2 26.7 %collective-permute-start.7 = (bf16[33,64,128]{2,1,0:T(8,128)(2,1)S(1)}, bf16[33,64,128]{2,1,0:T(8,128)(2,1)S(1)}, u32[]{:S(2)}, u32[]{:S(2)}) collective-permute-start(bf16[33,64,128]{2,1,0:T(8,128)(2,1)S(1)} %stack.1._.rest_0_), channel_id=1, source_target_pairs={{0,128},{8,136},{16,144},{24,152},{32,160},{40,168},{48,176},{56,1... | collective-permute-start | bytes 1622024 | tf_op jit(solution)/shard_map/ppermute | solution.py:39
  24.1 23.8 %collective-permute-start.6 = (bf16[33,64,128]{2,1,0:T(8,128)(2,1)S(1)}, bf16[33,64,128]{2,1,0:T(8,128)(2,1)S(1)}, u32[]{:S(2)}, u32[]{:S(2)}) collective-permute-start(bf16[33,64,128]{2,1,0:T(8,128)(2,1)S(1)} %stack.1._.rest_0_), channel_id=1, source_target_pairs={{0,192},{8,200},{16,208},{24,216},{32,224},{40,232},{48,240},{56,2... | collective-permute-start | bytes 1622024 | tf_op jit(solution)/shard_map/ppermute | solution.py:39
  25.5 11.0 %collective-permute-start.8 = (bf16[64,1024]{1,0:T(8,128)(2,1)S(1)}, bf16[64,1024]{1,0:T(8,128)(2,1)S(1)}, u32[]{:S(2)}, u32[]{:S(2)}) collective-permute-start(bf16[64,1024]{1,0:T(8,128)(2,1)S(1)} %copy-done.6), channel_id=1, source_target_pairs={{0,4},{1,5},{2,6},{3,7},{4,0},{5,1},{6,2},{7,3},{8,12},{9,13},{10,... | collective-permute-start | bytes 393224 | tf_op jit(solution)/shard_map/ppermute | solution.py:352
  36.5 6.5 %collective-permute-start.11 = (bf16[64,1024]{1,0:T(8,128)(2,1)S(1)}, bf16[64,1024]{1,0:T(8,128)(2,1)S(1)}, u32[]{:S(2)}, u32[]{:S(2)}) collective-permute-start(bf16[64,1024]{1,0:T(8,128)(2,1)S(1)} %collective-permute-done.8.rest_12_), channel_id=1, source_target_pairs={{0,2},{1,3},{2,0},{3,1},{4,6},{5,7},{6,4},{7,5},{8,10},{9,11},{10,... | collective-permute-start | bytes 393224 | tf_op jit(solution)/shard_map/ppermute | solution.py:370
  40.4 5.0 %collective-permute-start.9 = (bf16[64,1024]{1,0:T(8,128)(2,1)S(1)}, bf16[64,1024]{1,0:T(8,128)(2,1)S(1)}, u32[]{:S(2)}, u32[]{:S(2)}) collective-permute-start(bf16[64,1024]{1,0:T(8,128)(2,1)S(1)} %collective-permute-done.8.rest_12_), channel_id=1, source_target_pairs={{0,1},{1,2},{2,3},{3,0},{4,5},{5,6},{6,7},{7,4},{8,9},{9,10},{10,1... | collective-permute-start | bytes 393224 | tf_op jit(solution)/shard_map/ppermute | solution.py:371
  42.9 5.0 %collective-permute-start.10 = (bf16[64,1024]{1,0:T(8,128)(2,1)S(1)}, bf16[64,1024]{1,0:T(8,128)(2,1)S(1)}, u32[]{:S(2)}, u32[]{:S(2)}) collective-permute-start(bf16[64,1024]{1,0:T(8,128)(2,1)S(1)} %collective-permute-done.8.rest_12_), channel_id=1, source_target_pairs={{0,3},{1,0},{2,1},{3,2},{4,7},{5,4},{6,5},{7,6},{8,11},{9,8},{10,9... | collective-permute-start | bytes 393224 | tf_op jit(solution)/shard_map/ppermute | solution.py:372
  47.9 3.2 %collective-permute-start.13 = (bf16[33,64,128]{2,1,0:T(8,128)(2,1)S(1)}, bf16[33,64,128]{2,1,0:T(8,128)(2,1)S(1)}, u32[]{:S(2)}, u32[]{:S(2)}) collective-permute-start(bf16[33,64,128]{2,1,0:T(8,128)(2,1)S(1)} %collective-permute-done.7.rest_1_), channel_id=1, source_target_pairs={{0,8},{8,0},{16,24},{24,16},{32,40},{40,32},{48,56},{56,48},{64,72... | collective-permute-start | bytes 1622024 | tf_op jit(solution)/shard_map/ppermute | solution.py:39
  53.8 11.1 %collective-permute-start.20 = (bf16[64,1024]{1,0:T(8,128)(2,1)S(1)}, bf16[64,1024]{1,0:T(8,128)(2,1)S(1)}, u32[]{:S(2)}, u32[]{:S(2)}) collective-permute-start(bf16[64,1024]{1,0:T(8,128)(2,1)S(1)} %get-tuple-element.36.rest_0_), channel_id=1, source_target_pairs={{0,4},{1,5},{2,6},{3,7},{4,0},{5,1},{6,2},{7,3},{8,12},{9,13},{10,... | collective-permute-start | bytes 393224 | tf_op jit(solution)/shard_map/ppermute | solution.py:43
  60.3 7.9 %collective-permute-start.19 = (bf16[64,1024]{1,0:T(8,128)(2,1)S(1)}, bf16[64,1024]{1,0:T(8,128)(2,1)S(1)}, u32[]{:S(2)}, u32[]{:S(2)}) collective-permute-start(bf16[64,1024]{1,0:T(8,128)(2,1)S(1)} %get-tuple-element.36.rest_0_), channel_id=1, source_target_pairs={{0,2},{1,3},{2,0},{3,1},{4,6},{5,7},{6,4},{7,5},{8,10},{9,11},{10,... | collective-permute-start | bytes 393224 | tf_op jit(solution)/shard_map/ppermute | solution.py:44
  62.9 9.2 %collective-permute-start.18 = (bf16[64,1024]{1,0:T(8,128)(2,1)S(1)}, bf16[64,1024]{1,0:T(8,128)(2,1)S(1)}, u32[]{:S(2)}, u32[]{:S(2)}) collective-permute-start(bf16[64,1024]{1,0:T(8,128)(2,1)S(1)} %get-tuple-element.36.rest_0_), channel_id=1, source_target_pairs={{0,3},{1,0},{2,1},{3,2},{4,7},{5,4},{6,5},{7,6},{8,11},{9,8},{10,9... | collective-permute-start | bytes 393224 | tf_op jit(solution)/shard_map/ppermute | solution.py:44
  63.5 8.5 %collective-permute-start.17 = (bf16[64,1024]{1,0:T(8,128)(2,1)S(1)}, bf16[64,1024]{1,0:T(8,128)(2,1)S(1)}, u32[]{:S(2)}, u32[]{:S(2)}) collective-permute-start(bf16[64,1024]{1,0:T(8,128)(2,1)S(1)} %get-tuple-element.36.rest_0_), channel_id=1, source_target_pairs={{0,1},{1,2},{2,3},{3,0},{4,5},{5,6},{6,7},{7,4},{8,9},{9,10},{10,1... | collective-permute-start | bytes 393224 | tf_op jit(solution)/shard_map/ppermute | solution.py:44
  64.9 8.8 %collective-permute-start.23 = (bf16[64,1024]{1,0:T(8,128)(2,1)S(1)}, bf16[64,1024]{1,0:T(8,128)(2,1)S(1)}, u32[]{:S(2)}, u32[]{:S(2)}) collective-permute-start(bf16[64,1024]{1,0:T(8,128)(2,1)S(1)} %collective-permute-done.20.rest_4_), channel_id=1, source_target_pairs={{0,2},{1,3},{2,0},{3,1},{4,6},{5,7},{6,4},{7,5},{8,10},{9,11},{10,... | collective-permute-start | bytes 393224 | tf_op jit(solution)/shard_map/ppermute | solution.py:45
  67.0 8.6 %collective-permute-start.22 = (bf16[64,1024]{1,0:T(8,128)(2,1)S(1)}, bf16[64,1024]{1,0:T(8,128)(2,1)S(1)}, u32[]{:S(2)}, u32[]{:S(2)}) collective-permute-start(bf16[64,1024]{1,0:T(8,128)(2,1)S(1)} %collective-permute-done.20.rest_4_), channel_id=1, source_target_pairs={{0,3},{1,0},{2,1},{3,2},{4,7},{5,4},{6,5},{7,6},{8,11},{9,8},{10,9... | collective-permute-start | bytes 393224 | tf_op jit(solution)/shard_map/ppermute | solution.py:45
  68.1 7.5 %collective-permute-start.21 = (bf16[64,1024]{1,0:T(8,128)(2,1)S(1)}, bf16[64,1024]{1,0:T(8,128)(2,1)S(1)}, u32[]{:S(2)}, u32[]{:S(2)}) collective-permute-start(bf16[64,1024]{1,0:T(8,128)(2,1)S(1)} %collective-permute-done.20.rest_4_), channel_id=1, source_target_pairs={{0,1},{1,2},{2,3},{3,0},{4,5},{5,6},{6,7},{7,4},{8,9},{9,10},{10,1... | collective-permute-start | bytes 393224 | tf_op jit(solution)/shard_map/ppermute | solution.py:45
  80.3 3.6 %collective-permute-start.24 = (bf16[66,64,128]{2,1,0:T(8,128)(2,1)S(1)}, bf16[66,64,128]{2,1,0:T(8,128)(2,1)S(1)}, u32[]{:S(2)}, u32[]{:S(2)}) collective-permute-start(bf16[66,64,128]{2,1,0:T(8,128)(2,1)S(1)} %back_swap.2.rest_0_), channel_id=1, source_target_pairs={{0,8},{8,0},{16,24},{24,16},{32,40},{40,32},{48,56},{56,48},{64,72... | collective-permute-start | bytes 3244040 | tf_op jit(solution)/shard_map/ppermute | solution.py:39
  81.7 3.8 %collective-permute-start.25 = (bf16[66,64,128]{2,1,0:T(8,128)(2,1)S(1)}, bf16[66,64,128]{2,1,0:T(8,128)(2,1)S(1)}, u32[]{:S(2)}, u32[]{:S(2)}) collective-permute-start(bf16[66,64,128]{2,1,0:T(8,128)(2,1)S(1)} %back_swap.3.rest_0_), channel_id=1, source_target_pairs={{0,8},{8,0},{16,24},{24,16},{32,40},{40,32},{48,56},{56,48},{64,72... | collective-permute-start | bytes 3244040 | tf_op jit(solution)/shard_map/ppermute | solution.py:39
  85.7 15.5 %collective-permute-start.26 = (bf16[33,64,128]{2,1,0:T(8,128)(2,1)S(1)}, bf16[33,64,128]{2,1,0:T(8,128)(2,1)S(1)}, u32[]{:S(2)}, u32[]{:S(2)}) collective-permute-start(bf16[33,64,128]{2,1,0:T(8,128)(2,1)S(1)} %get-tuple-element.48), channel_id=1, source_target_pairs={{0,64},{8,72},{16,80},{24,88},{32,96},{40,104},{48,112},{56,120},{... | collective-permute-start | bytes 1622024 | tf_op jit(solution)/shard_map/ppermute | solution.py:39
  86.5 14.7 %collective-permute-start.27 = (bf16[33,64,128]{2,1,0:T(8,128)(2,1)S(1)}, bf16[33,64,128]{2,1,0:T(8,128)(2,1)S(1)}, u32[]{:S(2)}, u32[]{:S(2)}) collective-permute-start(bf16[33,64,128]{2,1,0:T(8,128)(2,1)S(1)} %get-tuple-element.49), channel_id=1, source_target_pairs={{0,192},{8,200},{16,208},{24,216},{32,224},{40,232},{48,240},{56,2... | collective-permute-start | bytes 1622024 | tf_op jit(solution)/shard_map/ppermute | solution.py:39
  89.1 16.3 %collective-permute-start.31 = (bf16[9,64,128]{2,1,0:T(8,128)(2,1)S(1)}, bf16[9,64,128]{2,1,0:T(8,128)(2,1)S(1)}, u32[]{:S(2)}, u32[]{:S(2)}) collective-permute-start(bf16[9,64,128]{2,1,0:T(8,128)(2,1)S(1)} %get-tuple-element.55), channel_id=1, source_target_pairs={{0,16},{8,24},{16,32},{24,40},{32,48},{40,56},{48,0},{56,8},{64,80... | collective-permute-start | bytes 442376 | tf_op jit(solution)/shard_map/ppermute | solution.py:39
  91.5 15.5 %collective-permute-start.32 = (bf16[9,64,128]{2,1,0:T(8,128)(2,1)S(1)}, bf16[9,64,128]{2,1,0:T(8,128)(2,1)S(1)}, u32[]{:S(2)}, u32[]{:S(2)}) collective-permute-start(bf16[9,64,128]{2,1,0:T(8,128)(2,1)S(1)} %get-tuple-element.56), channel_id=1, source_target_pairs={{0,48},{8,56},{16,0},{24,8},{32,16},{40,24},{48,32},{56,40},{64,11... | collective-permute-start | bytes 442376 | tf_op jit(solution)/shard_map/ppermute | solution.py:39
  92.9 15.1 %collective-permute-start.33 = (bf16[9,64,128]{2,1,0:T(8,128)(2,1)S(1)}, bf16[9,64,128]{2,1,0:T(8,128)(2,1)S(1)}, u32[]{:S(2)}, u32[]{:S(2)}) collective-permute-start(bf16[9,64,128]{2,1,0:T(8,128)(2,1)S(1)} %get-tuple-element.57), channel_id=1, source_target_pairs={{0,32},{8,40},{16,48},{24,56},{32,0},{40,8},{48,16},{56,24},{64,96... | collective-permute-start | bytes 442376 | tf_op jit(solution)/shard_map/ppermute | solution.py:39
  101.4 8.7 %collective-permute-start.28 = (bf16[9,64,128]{2,1,0:T(8,128)(2,1)S(1)}, bf16[9,64,128]{2,1,0:T(8,128)(2,1)S(1)}, u32[]{:S(2)}, u32[]{:S(2)}) collective-permute-start(bf16[9,64,128]{2,1,0:T(8,128)(2,1)S(1)} %get-tuple-element.51), channel_id=1, source_target_pairs={{0,16},{8,24},{16,32},{24,40},{32,48},{40,56},{48,0},{56,8},{64,80... | collective-permute-start | bytes 442376 | tf_op jit(solution)/shard_map/ppermute | solution.py:39
  103.9 7.9 %collective-permute-start.29 = (bf16[9,64,128]{2,1,0:T(8,128)(2,1)S(1)}, bf16[9,64,128]{2,1,0:T(8,128)(2,1)S(1)}, u32[]{:S(2)}, u32[]{:S(2)}) collective-permute-start(bf16[9,64,128]{2,1,0:T(8,128)(2,1)S(1)} %get-tuple-element.52), channel_id=1, source_target_pairs={{0,48},{8,56},{16,0},{24,8},{32,16},{40,24},{48,32},{56,40},{64,11... | collective-permute-start | bytes 442376 | tf_op jit(solution)/shard_map/ppermute | solution.py:39
  105.3 12.8 %collective-permute-start.30 = (bf16[9,64,128]{2,1,0:T(8,128)(2,1)S(1)}, bf16[9,64,128]{2,1,0:T(8,128)(2,1)S(1)}, u32[]{:S(2)}, u32[]{:S(2)}) collective-permute-start(bf16[9,64,128]{2,1,0:T(8,128)(2,1)S(1)} %get-tuple-element.53), channel_id=1, source_target_pairs={{0,32},{8,40},{16,48},{24,56},{32,0},{40,8},{48,16},{56,24},{64,96... | collective-permute-start | bytes 442376 | tf_op jit(solution)/shard_map/ppermute | solution.py:39
  108.0 10.2 %collective-permute-start.34 = (bf16[9,64,128]{2,1,0:T(8,128)(2,1)S(1)}, bf16[9,64,128]{2,1,0:T(8,128)(2,1)S(1)}, u32[]{:S(2)}, u32[]{:S(2)}) collective-permute-start(bf16[9,64,128]{2,1,0:T(8,128)(2,1)S(1)} %sum_far.1), channel_id=1, source_target_pairs={{0,128},{8,136},{16,144},{24,152},{32,160},{40,168},{48,176},{56,1... | collective-permute-start | bytes 442376 | tf_op jit(solution)/shard_map/ppermute | solution.py:39
  (12 other events, 150.3 us)

commit v5 on v4

--- a/solution.py
+++ b/solution.py
@@ -202,36 +202,37 @@
         hub_ref[j] = hubs[:, j * 128 : (j + 1) * 128]
 
 
-GROUPS = ((3, 0), (1, 2))
-
-
-def back_kernel(swap, part, ints_ref, sb0_ref, sb1_ref, ga_ref, tiles_ref, hub_ref, *rest):
-    out, acc = rest[-2:]
+GROUPS = ((1, 2), (3, 0))
+
+
+def back_kernel(works, ints_ref, sb0_ref, sb1_ref, ga_ref, tiles_ref, hub_ref, *rest):
+    outs, acc = rest[-1 - len(works) : -1], rest[-1]
     y, z, c = here()
-    cc = 1 - c if swap else c
     none = jnp.zeros((64, 128), BF)
-    for g, j in enumerate(GROUPS[part]):
-        sy = ahead(y, STEPS[j])
-        sb_ref = (sb0_ref, sb1_ref)[BACK[j] // 2]
-        sb_row = (2 if swap else 0) + BACK[j] % 2
-        out[64 + g] = hub_ref[sy].astype(BF)
-        for i in range(4):
-            sz = ahead(z, STEPS[i])
-            s = (sy * 4 + sz) * 2 + cc
-            count = ints_ref[8, s]
-            acc[0:8] = jnp.zeros((8, 64, 128), F32)
-            parts = []
-            for k in (0, 2):
-                one, two = (ga_ref[ints_ref[4 + k + n, s]] for n in range(2))
-                rows = [jnp.concatenate([one, none], axis=1), jnp.concatenate([none, two], axis=1)]
-                pair = jnp.concatenate([tiles_ref[s, k], tiles_ref[s, k + 1]], axis=1)
-                sums = dot_nt(jnp.concatenate(rows, axis=0), pair)
-                parts += [sums[:64], sums[64:]]
-            for k in range(4):
-                b = jnp.where(k < count, sb_ref[sb_row, sz * 4 + k], 8)
-                acc[b] += parts[k]
-            n = (g * 4 + i) * 8
-            out[n : n + 8] = acc[0:8].astype(BF)
+    for (swap, part), out in zip(works, outs):
+        cc = 1 - c if swap else c
+        for g, j in enumerate(GROUPS[part]):
+            sy = ahead(y, STEPS[j])
+            sb_ref = (sb0_ref, sb1_ref)[BACK[j] // 2]
+            sb_row = (2 if swap else 0) + BACK[j] % 2
+            out[64 + g] = hub_ref[sy].astype(BF)
+            for i in range(4):
+                sz = ahead(z, STEPS[i])
+                s = (sy * 4 + sz) * 2 + cc
+                count = ints_ref[8, s]
+                acc[0:8] = jnp.zeros((8, 64, 128), F32)
+                parts = []
+                for k in (0, 2):
+                    one, two = (ga_ref[ints_ref[4 + k + n, s]] for n in range(2))
+                    rows = [jnp.concatenate([one, none], axis=1), jnp.concatenate([none, two], axis=1)]
+                    pair = jnp.concatenate([tiles_ref[s, k], tiles_ref[s, k + 1]], axis=1)
+                    sums = dot_nt(jnp.concatenate(rows, axis=0), pair)
+                    parts += [sums[:64], sums[64:]]
+                for k in range(4):
+                    b = jnp.where(k < count, sb_ref[sb_row, sz * 4 + k], 8)
+                    acc[b] += parts[k]
+                n = (g * 4 + i) * 8
+                out[n : n + 8] = acc[0:8].astype(BF)
 
 
 def both(a, b, n):
@@ -245,7 +246,7 @@
         outs[g][32] = both(a, b, 64 + g)
 
 
-def add_second_kernel(a, b, *outs):
+def add_second_kernel(a, b, _, *outs):
     hubs = both(a, b, 64)
     for i in range(4):
         for r in range(8):
@@ -388,27 +389,26 @@
         16, None, 16 * MIB,
     )
 
-    def back(swap, part, *tokens):
-        (out,) = call(
-            functools.partial(back_kernel, swap, part), "back_swap" if swap else "back_own", [shape(66)],
+    def back(name, works, *tokens):
+        return call(
+            functools.partial(back_kernel, works), name, [shape(66)] * len(works),
             (ints, sb0, sb1, ga, tiles, hubs, *tokens), 3, [slots[0]], 16, None, 4 * MIB,
             loose=len(tokens),
         )
-        return out
-
-    swap0 = back(True, 0)
-    came0 = row_send(swap0, 0, 0, 1)
-    swap1 = back(True, 1, swap0)
-    came1 = row_send(swap1, 0, 0, 1)
-    own0 = back(False, 0, swap1)
-    *far_sums, near_sum = call(add_second_kernel, "add_first", [shape(9)] * 4 + [shape(LIVE)], (own0, came0), 0, (), 12)
-    own1 = back(False, 1, near_sum)
-    up_sum, down_sum = call(add_first_kernel, "add_second", [shape(LIVE)] * 2, (own1, came1))
+
+    (away0,) = back("back_first", ((True, 0),))
+    came0 = row_send(away0, 0, 0, 1)
+    away1, own0, own1 = back("back_rest", ((True, 1), (False, 0), (False, 1)), away0)
+    came1 = row_send(away1, 0, 0, 1)
+    up_sum, down_sum = call(add_first_kernel, "add_first", [shape(LIVE)] * 2, (own0, came0))
+    *far_sums, near_sum = call(
+        add_second_kernel, "add_second", [shape(9)] * 4 + [shape(LIVE)], (own1, came1, up_sum), 0, (), 12, loose=1
+    )
     fars = [far_sums[0]] + [row_send(far_sums[i], 0, STEPS[i], 0) for i in (1, 2, 3)]
     nears = (near_sum, row_send(up_sum, 1, 0, 0), row_send(down_sum, 3, 0, 0))
     zs = call(sum_near_kernel, "sum_near", [shape(9)] * 4, nears)
-    (far,) = call(sum_far_kernel, "sum_far", [shape(9)], (*fars, zs[0]), loose=1)
     zs = [zs[0]] + [row_send(zs[i], 0, STEPS[i], 0) for i in (1, 2, 3)]
+    (far,) = call(sum_far_kernel, "sum_far", [shape(9)], (*fars, zs[1]), loose=1)
     far = row_send(far, 2, 0, 0)
     (grad_in,) = call(last_kernel, "last", [((64, 1024), BF)], (*zs, far, ga, self_row, ids))
     return (act, grad_in)

time: 121 us -> 120 us (level)
  waiting for transfers between devices: 40.7 us -> 46.8 us
  starting transfers between devices: 57.3 us -> 51.5 us
  Pallas kernels: 16.5 us -> 14.8 us
    ppermute x1, waiting for transfers between devices: 0.01 us -> 4.17 us  [feat_gather(): across = lax.ppermute(value, 'feat', feat_perm(1, 0))]
    ppermute x3, waiting for transfers between devices: 3.46 us -> 0.01 us  [feat_gather(): near = [lax.ppermute(value, 'feat', feat_perm(0, k)) for k in STEPS[1:]]]
    ppermute x21, waiting for transfers between devices: 19.8 us -> 23 us  [row_send(): return lax.ppermute(value, 'row', row_perm(dy, dz, dc))]
    ppermute x1, waiting for transfers between devices: 5.32 us -> 3.02 us  [shards(): up_far = lax.ppermute(up, 'feat', feat_perm(1, 0))]
    ppermute x3, waiting for transfers between devices: 3.55 us -> 5.67 us  [feat_gather(): far = [lax.ppermute(across, 'feat', feat_perm(0, k)) for k in STEPS[1:]]]
    pallas_call x15 -> x13, Pallas kernels: 16.5 us -> 14.8 us  [call(): pl.pallas_call(kernel, out_shape=shapes, in_specs=[HB] * hbm + [SM] * sca...]
    ppermute x21, starting transfers between devices: 28.2 us -> 26.6 us  [row_send(): return lax.ppermute(value, 'row', row_perm(dy, dz, dc))]
    ppermute x1, starting transfers between devices: 6.44 us -> 4.91 us  [feat_gather(): across = lax.ppermute(value, 'feat', feat_perm(1, 0))]
  transfers between devices with their start and end apart: 35 -> 35, of which waited for: 17 -> 16; matrix products, arithmetic and copies ran while one was open for 0% -> 0% of each run, Pallas kernels for 6% -> 5%
where the time goes in v5:
time: 120 us; the launch traced here: 118 us
  starting transfers between devices  51.5 us (43%)
  waiting for transfers between devices  46.8 us (39%)
  Pallas kernels  14.8 us (12%)
  local copies, waits for them, and re-layouts  3.12 us (3%)
    ppermute x21, starting transfers between devices, row_send(): return lax.ppermute(value, 'row', row_perm(dy, dz, dc))  26.6 us
    ppermute x21, waiting for transfers between devices, row_send(): return lax.ppermute(value, 'row', row_perm(dy, dz, dc))  23 us
    pallas_call x13, Pallas kernels, call(): pl.pallas_call(kernel, out_shape=shapes, in_specs=[HB] * hbm + [SM] * sca...  14.8 us
    ppermute x3, waiting for transfers between devices, feat_gather(): far = [lax.ppermute(across, 'feat', feat_perm(0, k)) for k in STEPS[1:]]  5.67 us
    ppermute x1, starting transfers between devices, shards(): up_far = lax.ppermute(up, 'feat', feat_perm(1, 0))  5.5 us
    ppermute x3, waiting for transfers between devices, shards(): lax.ppermute(up_late, 'feat', feat_perm(0, k))  5.28 us
    ppermute x1, starting transfers between devices, feat_gather(): across = lax.ppermute(value, 'feat', feat_perm(1, 0))  4.91 us
    ppermute x3, starting transfers between devices, shards(): lax.ppermute(up_late, 'feat', feat_perm(0, k))  4.24 us
  transfers between devices with their start and end apart: 35, of which 16 were waited for; matrix products, arithmetic and copies ran while one was open for 0% of the time, Pallas kernels for 5%

profile of v5, /device:TPU:2, one launch (start us, length us, event | category | flops | bytes accessed | tf_op | source)
XLA Modules:
  0.0 117.8 jit_solution(6339998673427408621)
XLA Ops:
  2.6 1.6 %collective-permute-start.3 = (bf16[64,1024]{1,0:T(8,128)(2,1)}, bf16[64,1024]{1,0:T(8,128)(2,1)S(1)}, u32[]{:S(2)}, u32[]{:S(2)}) collective-permute-start(bf16[64,1024]{1,0:T(8,128)(2,1)} %rest_8_.1), channel_id=1, source_target_pairs={{0,1},{1,2},{2,3},{3,0},{4,5},{5,6},{6,7},{7,4},{8,9},{9,10},{10,1... | collective-permute-start | bytes 393224 | tf_op jit(solution)/shard_map/ppermute | solution.py:348
  4.2 1.9 %collective-permute-start = (bf16[9,64,128]{2,1,0:T(8,128)(2,1)S(1)}, bf16[9,64,128]{2,1,0:T(8,128)(2,1)S(1)}, u32[]{:S(2)}, u32[]{:S(2)}) collective-permute-start(bf16[9,64,128]{2,1,0:T(8,128)(2,1)S(1)} %prep.1.p0), channel_id=1, source_target_pairs={{0,16},{8,24},{16,32},{24,40},{32,48},{40,56},{48,0},{56,8},{64,80... | collective-permute-start | bytes 442376 | tf_op jit(solution)/shard_map/ppermute | solution.py:39
  6.1 2.7 %collective-permute-start.1 = (bf16[9,64,128]{2,1,0:T(8,128)(2,1)S(1)}, bf16[9,64,128]{2,1,0:T(8,128)(2,1)S(1)}, u32[]{:S(2)}, u32[]{:S(2)}) collective-permute-start(bf16[9,64,128]{2,1,0:T(8,128)(2,1)S(1)} %prep.1.p0), channel_id=1, source_target_pairs={{0,48},{8,56},{16,0},{24,8},{32,16},{40,24},{48,32},{56,40},{64,11... | collective-permute-start | bytes 442376 | tf_op jit(solution)/shard_map/ppermute | solution.py:39
  10.0 2.1 %collective-permute-start.5 = (bf16[64,1024]{1,0:T(8,128)(2,1)}, bf16[64,1024]{1,0:T(8,128)(2,1)S(1)}, u32[]{:S(2)}, u32[]{:S(2)}) collective-permute-start(bf16[64,1024]{1,0:T(8,128)(2,1)} %rest_8_.1), channel_id=1, source_target_pairs={{0,2},{1,3},{2,0},{3,1},{4,6},{5,7},{6,4},{7,5},{8,10},{9,11},{10,... | collective-permute-start | bytes 393224 | tf_op jit(solution)/shard_map/ppermute | solution.py:348
  12.2 3.9 %collective-permute-done.4.rest_1_.rest_10_ = bf16[64,1024]{1,0:T(8,128)(2,1)S(1)} collective-permute-done((bf16[64,1024]{1,0:T(8,128)(2,1)}, bf16[64,1024]{1,0:T(8,128)(2,1)S(1)}, u32[]{:S(2)}, u32[]{:S(2)}) %collective-permute-start.4) | collective-permute-done | bytes 131104 | tf_op jit(solution)/shard_map/ppermute | solution.py:348
  17.4 4.4 %collective-permute-done.2.p3 = bf16[9,64,128]{2,1,0:T(8,128)(2,1)S(1)} collective-permute-done((bf16[9,64,128]{2,1,0:T(8,128)(2,1)S(1)}, bf16[9,64,128]{2,1,0:T(8,128)(2,1)S(1)}, u32[]{:S(2)}, u32[]{:S(2)}) %collective-permute-start.2) | collective-permute-done | bytes 147488 | tf_op jit(solution)/shard_map/ppermute | solution.py:39
  21.9 1.7 %collective-permute-start.14 = (bf16[33,64,128]{2,1,0:T(8,128)(2,1)S(1)}, bf16[33,64,128]{2,1,0:T(8,128)(2,1)S(1)}, u32[]{:S(2)}, u32[]{:S(2)}) collective-permute-start(bf16[33,64,128]{2,1,0:T(8,128)(2,1)S(1)} %stack.1._.rest_0_), channel_id=1, source_target_pairs={{0,64},{8,72},{16,80},{24,88},{32,96},{40,104},{48,112},{56,120},{... | collective-permute-start | bytes 1622024 | tf_op jit(solution)/shard_map/ppermute | solution.py:39
  23.6 2.9 %collective-permute-start.7 = (bf16[33,64,128]{2,1,0:T(8,128)(2,1)S(1)}, bf16[33,64,128]{2,1,0:T(8,128)(2,1)S(1)}, u32[]{:S(2)}, u32[]{:S(2)}) collective-permute-start(bf16[33,64,128]{2,1,0:T(8,128)(2,1)S(1)} %stack.1._.rest_0_), channel_id=1, source_target_pairs={{0,128},{8,136},{16,144},{24,152},{32,160},{40,168},{48,176},{56,1... | collective-permute-start | bytes 1622024 | tf_op jit(solution)/shard_map/ppermute | solution.py:39
  27.8 5.5 %collective-permute-start.8 = (bf16[64,1024]{1,0:T(8,128)(2,1)S(1)}, bf16[64,1024]{1,0:T(8,128)(2,1)S(1)}, u32[]{:S(2)}, u32[]{:S(2)}) collective-permute-start(bf16[64,1024]{1,0:T(8,128)(2,1)S(1)} %copy-done.6), channel_id=1, source_target_pairs={{0,4},{1,5},{2,6},{3,7},{4,0},{5,1},{6,2},{7,3},{8,12},{9,13},{10,... | collective-permute-start | bytes 393224 | tf_op jit(solution)/shard_map/ppermute | solution.py:353
  33.3 2.2 %copy-done = bf16[1,32,4,128,128]{4,3,2,1,0:T(8,128)(2,1)S(1)} copy-done((bf16[1,32,4,128,128]{4,3,2,1,0:T(8,128)(2,1)S(1)}, bf16[1,32,4,128,128]{4,3,2,1,0:T(8,128)(2,1)}, u32[]{:S(2)}) %copy-start) | copy-done | bytes 4194328
  35.8 3.0 %collective-permute-done.8.rest_12_ = bf16[64,1024]{1,0:T(8,128)(2,1)S(1)} collective-permute-done((bf16[64,1024]{1,0:T(8,128)(2,1)S(1)}, bf16[64,1024]{1,0:T(8,128)(2,1)S(1)}, u32[]{:S(2)}, u32[]{:S(2)}) %collective-permute-start.8) | collective-permute-done | bytes 131104 | tf_op jit(solution)/shard_map/ppermute | solution.py:353
  39.4 2.1 %collective-permute-start.11 = (bf16[64,1024]{1,0:T(8,128)(2,1)S(1)}, bf16[64,1024]{1,0:T(8,128)(2,1)S(1)}, u32[]{:S(2)}, u32[]{:S(2)}) collective-permute-start(bf16[64,1024]{1,0:T(8,128)(2,1)S(1)} %collective-permute-done.8.rest_12_), channel_id=1, source_target_pairs={{0,2},{1,3},{2,0},{3,1},{4,6},{5,7},{6,4},{7,5},{8,10},{9,11},{10,... | collective-permute-start | bytes 393224 | tf_op jit(solution)/shard_map/ppermute | solution.py:371
  41.5 2.3 %collective-permute-done.10.rest_14_ = bf16[64,1024]{1,0:T(8,128)(2,1)S(1)} collective-permute-done((bf16[64,1024]{1,0:T(8,128)(2,1)S(1)}, bf16[64,1024]{1,0:T(8,128)(2,1)S(1)}, u32[]{:S(2)}, u32[]{:S(2)}) %collective-permute-start.10) | collective-permute-done | bytes 131104 | tf_op jit(solution)/shard_map/ppermute | solution.py:373
  46.4 2.4 %collective-permute-done.9.rest_13_ = bf16[64,1024]{1,0:T(8,128)(2,1)S(1)} collective-permute-done((bf16[64,1024]{1,0:T(8,128)(2,1)S(1)}, bf16[64,1024]{1,0:T(8,128)(2,1)S(1)}, u32[]{:S(2)}, u32[]{:S(2)}) %collective-permute-start.9) | collective-permute-done | bytes 131104 | tf_op jit(solution)/shard_map/ppermute | solution.py:372
  48.8 1.4 %collective-permute-done.7.rest_1_ = bf16[33,64,128]{2,1,0:T(8,128)(2,1)S(1)} collective-permute-done((bf16[33,64,128]{2,1,0:T(8,128)(2,1)S(1)}, bf16[33,64,128]{2,1,0:T(8,128)(2,1)S(1)}, u32[]{:S(2)}, u32[]{:S(2)}) %collective-permute-start.7) | collective-permute-done | bytes 540704 | tf_op jit(solution)/shard_map/ppermute | solution.py:39
  50.8 2.7 %agg_first.1 = (f32[8,64,128]{2,1,0:T(8,128)S(1)}, s32[4,16]{1,0:T(4,128)S(1)}) custom-call(s32[10,32]{1,0:T(8,128)S(1)} %add_add_fusion.ints_ref, bf16[33,64,128]{2,1,0:T(8,128)(2,1)S(1)} %stack.1._.rest_0_, bf16[33,64,128]{2,1,0:T(8,128)(2,1)S(1)} %collective-permute-done.14.rest_1_, bf16[33,64,128]{2,1,0:T(8,128)(2,1)S(1)} %collective-permute-done.15.rest_2_, ...), custom_call_target="tpu_custom_call" | custom-call | bytes 8388608 | tf_op jit(solution)/shard_map/agg_first/pallas_call | solution.py:305
  53.5 2.7 %agg_second.1 = (bf16[64,1024]{1,0:T(8,128)(2,1)S(1)}, s32[4,16]{1,0:T(4,128)S(1)}) custom-call(s32[10,32]{1,0:T(8,128)S(1)} %add_add_fusion.ints_ref, bf16[33,64,128]{2,1,0:T(8,128)(2,1)S(1)} %collective-permute-done.6.rest_0_, bf16[33,64,128]{2,1,0:T(8,128)(2,1)S(1)} %collective-permute-done.7.rest_1_, ...), custom_call_target="tpu_custom_call" | custom-call | bytes 8388608 | tf_op jit(solution)/shard_map/agg_second/pallas_call | solution.py:305
  56.2 4.9 %collective-permute-start.20 = (bf16[64,1024]{1,0:T(8,128)(2,1)S(1)}, bf16[64,1024]{1,0:T(8,128)(2,1)S(1)}, u32[]{:S(2)}, u32[]{:S(2)}) collective-permute-start(bf16[64,1024]{1,0:T(8,128)(2,1)S(1)} %get-tuple-element.39.rest_0_), channel_id=1, source_target_pairs={{0,4},{1,5},{2,6},{3,7},{4,0},{5,1},{6,2},{7,3},{8,12},{9,13},{10,... | collective-permute-start | bytes 393224 | tf_op jit(solution)/shard_map/ppermute | solution.py:43
  64.2 4.2 %collective-permute-done.20.rest_4_ = bf16[64,1024]{1,0:T(8,128)(2,1)S(1)} collective-permute-done((bf16[64,1024]{1,0:T(8,128)(2,1)S(1)}, bf16[64,1024]{1,0:T(8,128)(2,1)S(1)}, u32[]{:S(2)}, u32[]{:S(2)}) %collective-permute-start.20) | collective-permute-done | bytes 131104 | tf_op jit(solution)/shard_map/ppermute | solution.py:43
  71.7 2.2 %collective-permute-done.21.rest_5_ = bf16[64,1024]{1,0:T(8,128)(2,1)S(1)} collective-permute-done((bf16[64,1024]{1,0:T(8,128)(2,1)S(1)}, bf16[64,1024]{1,0:T(8,128)(2,1)S(1)}, u32[]{:S(2)}, u32[]{:S(2)}) %collective-permute-start.21) | collective-permute-done | bytes 131104 | tf_op jit(solution)/shard_map/ppermute | solution.py:45
  73.8 2.1 %collective-permute-done.22.rest_6_ = bf16[64,1024]{1,0:T(8,128)(2,1)S(1)} collective-permute-done((bf16[64,1024]{1,0:T(8,128)(2,1)S(1)}, bf16[64,1024]{1,0:T(8,128)(2,1)S(1)}, u32[]{:S(2)}, u32[]{:S(2)}) %collective-permute-start.22) | collective-permute-done | bytes 131104 | tf_op jit(solution)/shard_map/ppermute | solution.py:45
  75.9 1.4 %collective-permute-done.23.rest_7_ = bf16[64,1024]{1,0:T(8,128)(2,1)S(1)} collective-permute-done((bf16[64,1024]{1,0:T(8,128)(2,1)S(1)}, bf16[64,1024]{1,0:T(8,128)(2,1)S(1)}, u32[]{:S(2)}, u32[]{:S(2)}) %collective-permute-start.23) | collective-permute-done | bytes 131104 | tf_op jit(solution)/shard_map/ppermute | solution.py:45
  77.3 3.3 %middle.1 = (bf16[64,1024]{1,0:T(8,128)(2,1)}, bf16[8,64,128]{2,1,0:T(8,128)(2,1)S(1)}, f32[4,64,128]{2,1,0:T(8,128)S(1)}) custom-call(bf16[64,1024]{1,0:T(8,128)(2,1)S(1)} %get-tuple-element.39.rest_0_, bf16[64,1024]{1,0:T(8,128)(2,1)S(1)} %collective-permute-done.17.rest_1_, bf16[64,1024]{1,0:T(8,128)(2,1)S(1)} %collective-permute-done.18.rest_2_, ...), custom_call_target="tpu_custom_call" | custom-call | bytes 16777216 | tf_op jit(solution)/shard_map/middle/pallas_call | solution.py:305
  82.1 2.4 %back_rest.1 = (bf16[66,64,128]{2,1,0:T(8,128)(2,1)S(1)}, bf16[66,64,128]{2,1,0:T(8,128)(2,1)S(1)}, bf16[66,64,128]{2,1,0:T(8,128)(2,1)S(1)}) custom-call(s32[10,32]{1,0:T(8,128)S(1)} %add_add_fusion.ints_ref, s32[4,16]{1,0:T(4,128)S(1)} %get-tuple-element.46.sb0_ref, s32[4,16]{1,0:T(4,128)S(1)} %get-tuple-element.47.sb1_ref, ...), custom_call_target="tpu_custom_call" | custom-call | bytes 4194304 | tf_op jit(solution)/shard_map/back_rest/pallas_call | solution.py:305
  85.3 1.5 %collective-permute-start.26 = (bf16[33,64,128]{2,1,0:T(8,128)(2,1)S(1)}, bf16[33,64,128]{2,1,0:T(8,128)(2,1)S(1)}, u32[]{:S(2)}, u32[]{:S(2)}) collective-permute-start(bf16[33,64,128]{2,1,0:T(8,128)(2,1)S(1)} %get-tuple-element.53._), channel_id=1, source_target_pairs={{0,64},{8,72},{16,80},{24,88},{32,96},{40,104},{48,112},{56,120},{... | collective-permute-start | bytes 1622024 | tf_op jit(solution)/shard_map/ppermute | solution.py:39
  86.8 2.0 %collective-permute-start.27 = (bf16[33,64,128]{2,1,0:T(8,128)(2,1)S(1)}, bf16[33,64,128]{2,1,0:T(8,128)(2,1)S(1)}, u32[]{:S(2)}, u32[]{:S(2)}) collective-permute-start(bf16[33,64,128]{2,1,0:T(8,128)(2,1)S(1)} %get-tuple-element.55), channel_id=1, source_target_pairs={{0,192},{8,200},{16,208},{24,216},{32,224},{40,232},{48,240},{56,2... | collective-permute-start | bytes 1622024 | tf_op jit(solution)/shard_map/ppermute | solution.py:39
  89.1 3.8 %collective-permute-start.32 = (bf16[9,64,128]{2,1,0:T(8,128)(2,1)S(1)}, bf16[9,64,128]{2,1,0:T(8,128)(2,1)S(1)}, u32[]{:S(2)}, u32[]{:S(2)}) collective-permute-start(bf16[9,64,128]{2,1,0:T(8,128)(2,1)S(1)} %get-tuple-element.62), channel_id=1, source_target_pairs={{0,48},{8,56},{16,0},{24,8},{32,16},{40,24},{48,32},{56,40},{64,11... | collective-permute-start | bytes 442376 | tf_op jit(solution)/shard_map/ppermute | solution.py:39
  93.0 8.0 %collective-permute-done.26.b = bf16[33,64,128]{2,1,0:T(8,128)(2,1)S(1)} collective-permute-done((bf16[33,64,128]{2,1,0:T(8,128)(2,1)S(1)}, bf16[33,64,128]{2,1,0:T(8,128)(2,1)S(1)}, u32[]{:S(2)}, u32[]{:S(2)}) %collective-permute-start.26) | collective-permute-done | bytes 540704 | tf_op jit(solution)/shard_map/ppermute | solution.py:39
  101.3 3.8 %collective-permute-start.29 = (bf16[9,64,128]{2,1,0:T(8,128)(2,1)S(1)}, bf16[9,64,128]{2,1,0:T(8,128)(2,1)S(1)}, u32[]{:S(2)}, u32[]{:S(2)}) collective-permute-start(bf16[9,64,128]{2,1,0:T(8,128)(2,1)S(1)} %get-tuple-element.58), channel_id=1, source_target_pairs={{0,48},{8,56},{16,0},{24,8},{32,16},{40,24},{48,32},{56,40},{64,11... | collective-permute-start | bytes 442376 | tf_op jit(solution)/shard_map/ppermute | solution.py:39
  105.1 4.7 %collective-permute-done.28.refs_4_.rest_1_ = bf16[9,64,128]{2,1,0:T(8,128)(2,1)S(1)} collective-permute-done((bf16[9,64,128]{2,1,0:T(8,128)(2,1)S(1)}, bf16[9,64,128]{2,1,0:T(8,128)(2,1)S(1)}, u32[]{:S(2)}, u32[]{:S(2)}) %collective-permute-start.28) | collective-permute-done | bytes 147488 | tf_op jit(solution)/shard_map/ppermute | solution.py:39
  109.9 2.3 %collective-permute-start.34 = (bf16[9,64,128]{2,1,0:T(8,128)(2,1)S(1)}, bf16[9,64,128]{2,1,0:T(8,128)(2,1)S(1)}, u32[]{:S(2)}, u32[]{:S(2)}) collective-permute-start(bf16[9,64,128]{2,1,0:T(8,128)(2,1)S(1)} %sum_far.1), channel_id=1, source_target_pairs={{0,128},{8,136},{16,144},{24,152},{32,160},{40,168},{48,176},{56,1... | collective-permute-start | bytes 442376 | tf_op jit(solution)/shard_map/ppermute | solution.py:39
  112.3 3.6 %collective-permute-done.30.rest_3_ = bf16[9,64,128]{2,1,0:T(8,128)(2,1)S(1)} collective-permute-done((bf16[9,64,128]{2,1,0:T(8,128)(2,1)S(1)}, bf16[9,64,128]{2,1,0:T(8,128)(2,1)S(1)}, u32[]{:S(2)}, u32[]{:S(2)}) %collective-permute-start.30) | collective-permute-done | bytes 147488 | tf_op jit(solution)/shard_map/ppermute | solution.py:39
  (70 shorter events, 21.2 us)
Async XLA Ops:
  2.6 7.4 %collective-permute-start.3 = (bf16[64,1024]{1,0:T(8,128)(2,1)}, bf16[64,1024]{1,0:T(8,128)(2,1)S(1)}, u32[]{:S(2)}, u32[]{:S(2)}) collective-permute-start(bf16[64,1024]{1,0:T(8,128)(2,1)} %rest_8_.1), channel_id=1, source_target_pairs={{0,1},{1,2},{2,3},{3,0},{4,5},{5,6},{6,7},{7,4},{8,9},{9,10},{10,1... | collective-permute-start | bytes 393224 | tf_op jit(solution)/shard_map/ppermute | solution.py:348
  4.2 13.2 %collective-permute-start = (bf16[9,64,128]{2,1,0:T(8,128)(2,1)S(1)}, bf16[9,64,128]{2,1,0:T(8,128)(2,1)S(1)}, u32[]{:S(2)}, u32[]{:S(2)}) collective-permute-start(bf16[9,64,128]{2,1,0:T(8,128)(2,1)S(1)} %prep.1.p0), channel_id=1, source_target_pairs={{0,16},{8,24},{16,32},{24,40},{32,48},{40,56},{48,0},{56,8},{64,80... | collective-permute-start | bytes 442376 | tf_op jit(solution)/shard_map/ppermute | solution.py:39
  6.1 11.3 %collective-permute-start.1 = (bf16[9,64,128]{2,1,0:T(8,128)(2,1)S(1)}, bf16[9,64,128]{2,1,0:T(8,128)(2,1)S(1)}, u32[]{:S(2)}, u32[]{:S(2)}) collective-permute-start(bf16[9,64,128]{2,1,0:T(8,128)(2,1)S(1)} %prep.1.p0), channel_id=1, source_target_pairs={{0,48},{8,56},{16,0},{24,8},{32,16},{40,24},{48,32},{56,40},{64,11... | collective-permute-start | bytes 442376 | tf_op jit(solution)/shard_map/ppermute | solution.py:39
  8.8 13.0 %collective-permute-start.2 = (bf16[9,64,128]{2,1,0:T(8,128)(2,1)S(1)}, bf16[9,64,128]{2,1,0:T(8,128)(2,1)S(1)}, u32[]{:S(2)}, u32[]{:S(2)}) collective-permute-start(bf16[9,64,128]{2,1,0:T(8,128)(2,1)S(1)} %prep.1.p0), channel_id=1, source_target_pairs={{0,32},{8,40},{16,48},{24,56},{32,0},{40,8},{48,16},{56,24},{64,96... | collective-permute-start | bytes 442376 | tf_op jit(solution)/shard_map/ppermute | solution.py:39
  9.5 6.5 %collective-permute-start.4 = (bf16[64,1024]{1,0:T(8,128)(2,1)}, bf16[64,1024]{1,0:T(8,128)(2,1)S(1)}, u32[]{:S(2)}, u32[]{:S(2)}) collective-permute-start(bf16[64,1024]{1,0:T(8,128)(2,1)} %rest_8_.1), channel_id=1, source_target_pairs={{0,3},{1,0},{2,1},{3,2},{4,7},{5,4},{6,5},{7,6},{8,11},{9,8},{10,9... | collective-permute-start | bytes 393224 | tf_op jit(solution)/shard_map/ppermute | solution.py:348
  10.0 7.4 %collective-permute-start.5 = (bf16[64,1024]{1,0:T(8,128)(2,1)}, bf16[64,1024]{1,0:T(8,128)(2,1)S(1)}, u32[]{:S(2)}, u32[]{:S(2)}) collective-permute-start(bf16[64,1024]{1,0:T(8,128)(2,1)} %rest_8_.1), channel_id=1, source_target_pairs={{0,2},{1,3},{2,0},{3,1},{4,6},{5,7},{6,4},{7,5},{8,10},{9,11},{10,... | collective-permute-start | bytes 393224 | tf_op jit(solution)/shard_map/ppermute | solution.py:348
  21.9 24.0 %collective-permute-start.14 = (bf16[33,64,128]{2,1,0:T(8,128)(2,1)S(1)}, bf16[33,64,128]{2,1,0:T(8,128)(2,1)S(1)}, u32[]{:S(2)}, u32[]{:S(2)}) collective-permute-start(bf16[33,64,128]{2,1,0:T(8,128)(2,1)S(1)} %stack.1._.rest_0_), channel_id=1, source_target_pairs={{0,64},{8,72},{16,80},{24,88},{32,96},{40,104},{48,112},{56,120},{... | collective-permute-start | bytes 1622024 | tf_op jit(solution)/shard_map/ppermute | solution.py:39
  23.6 26.7 %collective-permute-start.7 = (bf16[33,64,128]{2,1,0:T(8,128)(2,1)S(1)}, bf16[33,64,128]{2,1,0:T(8,128)(2,1)S(1)}, u32[]{:S(2)}, u32[]{:S(2)}) collective-permute-start(bf16[33,64,128]{2,1,0:T(8,128)(2,1)S(1)} %stack.1._.rest_0_), channel_id=1, source_target_pairs={{0,128},{8,136},{16,144},{24,152},{32,160},{40,168},{48,176},{56,1... | collective-permute-start | bytes 1622024 | tf_op jit(solution)/shard_map/ppermute | solution.py:39
  26.5 23.8 %collective-permute-start.6 = (bf16[33,64,128]{2,1,0:T(8,128)(2,1)S(1)}, bf16[33,64,128]{2,1,0:T(8,128)(2,1)S(1)}, u32[]{:S(2)}, u32[]{:S(2)}) collective-permute-start(bf16[33,64,128]{2,1,0:T(8,128)(2,1)S(1)} %stack.1._.rest_0_), channel_id=1, source_target_pairs={{0,192},{8,200},{16,208},{24,216},{32,224},{40,232},{48,240},{56,2... | collective-permute-start | bytes 1622024 | tf_op jit(solution)/shard_map/ppermute | solution.py:39
  27.8 11.0 %collective-permute-start.8 = (bf16[64,1024]{1,0:T(8,128)(2,1)S(1)}, bf16[64,1024]{1,0:T(8,128)(2,1)S(1)}, u32[]{:S(2)}, u32[]{:S(2)}) collective-permute-start(bf16[64,1024]{1,0:T(8,128)(2,1)S(1)} %copy-done.6), channel_id=1, source_target_pairs={{0,4},{1,5},{2,6},{3,7},{4,0},{5,1},{6,2},{7,3},{8,12},{9,13},{10,... | collective-permute-start | bytes 393224 | tf_op jit(solution)/shard_map/ppermute | solution.py:353
  38.9 5.0 %collective-permute-start.10 = (bf16[64,1024]{1,0:T(8,128)(2,1)S(1)}, bf16[64,1024]{1,0:T(8,128)(2,1)S(1)}, u32[]{:S(2)}, u32[]{:S(2)}) collective-permute-start(bf16[64,1024]{1,0:T(8,128)(2,1)S(1)} %collective-permute-done.8.rest_12_), channel_id=1, source_target_pairs={{0,3},{1,0},{2,1},{3,2},{4,7},{5,4},{6,5},{7,6},{8,11},{9,8},{10,9... | collective-permute-start | bytes 393224 | tf_op jit(solution)/shard_map/ppermute | solution.py:373
  39.4 6.5 %collective-permute-start.11 = (bf16[64,1024]{1,0:T(8,128)(2,1)S(1)}, bf16[64,1024]{1,0:T(8,128)(2,1)S(1)}, u32[]{:S(2)}, u32[]{:S(2)}) collective-permute-start(bf16[64,1024]{1,0:T(8,128)(2,1)S(1)} %collective-permute-done.8.rest_12_), channel_id=1, source_target_pairs={{0,2},{1,3},{2,0},{3,1},{4,6},{5,7},{6,4},{7,5},{8,10},{9,11},{10,... | collective-permute-start | bytes 393224 | tf_op jit(solution)/shard_map/ppermute | solution.py:371
  43.8 5.0 %collective-permute-start.9 = (bf16[64,1024]{1,0:T(8,128)(2,1)S(1)}, bf16[64,1024]{1,0:T(8,128)(2,1)S(1)}, u32[]{:S(2)}, u32[]{:S(2)}) collective-permute-start(bf16[64,1024]{1,0:T(8,128)(2,1)S(1)} %collective-permute-done.8.rest_12_), channel_id=1, source_target_pairs={{0,1},{1,2},{2,3},{3,0},{4,5},{5,6},{6,7},{7,4},{8,9},{9,10},{10,1... | collective-permute-start | bytes 393224 | tf_op jit(solution)/shard_map/ppermute | solution.py:372
  45.9 4.9 %collective-permute-start.15 = (bf16[33,64,128]{2,1,0:T(8,128)(2,1)S(1)}, bf16[33,64,128]{2,1,0:T(8,128)(2,1)S(1)}, u32[]{:S(2)}, u32[]{:S(2)}) collective-permute-start(bf16[33,64,128]{2,1,0:T(8,128)(2,1)S(1)} %stack.1._.rest_0_), channel_id=1, source_target_pairs={{0,8},{8,0},{16,24},{24,16},{32,40},{40,32},{48,56},{56,48},{64,72... | collective-permute-start | bytes 1622024 | tf_op jit(solution)/shard_map/ppermute | solution.py:39
  45.9 4.9 %collective-permute-start.16 = (bf16[33,64,128]{2,1,0:T(8,128)(2,1)S(1)}, bf16[33,64,128]{2,1,0:T(8,128)(2,1)S(1)}, u32[]{:S(2)}, u32[]{:S(2)}) collective-permute-start(bf16[33,64,128]{2,1,0:T(8,128)(2,1)S(1)} %collective-permute-done.14.rest_1_), channel_id=1, source_target_pairs={{0,8},{8,0},{16,24},{24,16},{32,40},{40,32},{48,56},{56,48},{64,72... | collective-permute-start | bytes 1622024 | tf_op jit(solution)/shard_map/ppermute | solution.py:39
  56.2 12.2 %collective-permute-start.20 = (bf16[64,1024]{1,0:T(8,128)(2,1)S(1)}, bf16[64,1024]{1,0:T(8,128)(2,1)S(1)}, u32[]{:S(2)}, u32[]{:S(2)}) collective-permute-start(bf16[64,1024]{1,0:T(8,128)(2,1)S(1)} %get-tuple-element.39.rest_0_), channel_id=1, source_target_pairs={{0,4},{1,5},{2,6},{3,7},{4,0},{5,1},{6,2},{7,3},{8,12},{9,13},{10,... | collective-permute-start | bytes 393224 | tf_op jit(solution)/shard_map/ppermute | solution.py:43
  61.1 9.3 %collective-permute-start.17 = (bf16[64,1024]{1,0:T(8,128)(2,1)S(1)}, bf16[64,1024]{1,0:T(8,128)(2,1)S(1)}, u32[]{:S(2)}, u32[]{:S(2)}) collective-permute-start(bf16[64,1024]{1,0:T(8,128)(2,1)S(1)} %get-tuple-element.39.rest_0_), channel_id=1, source_target_pairs={{0,1},{1,2},{2,3},{3,0},{4,5},{5,6},{6,7},{7,4},{8,9},{9,10},{10,1... | collective-permute-start | bytes 393224 | tf_op jit(solution)/shard_map/ppermute | solution.py:44
  62.3 9.4 %collective-permute-start.18 = (bf16[64,1024]{1,0:T(8,128)(2,1)S(1)}, bf16[64,1024]{1,0:T(8,128)(2,1)S(1)}, u32[]{:S(2)}, u32[]{:S(2)}) collective-permute-start(bf16[64,1024]{1,0:T(8,128)(2,1)S(1)} %get-tuple-element.39.rest_0_), channel_id=1, source_target_pairs={{0,3},{1,0},{2,1},{3,2},{4,7},{5,4},{6,5},{7,6},{8,11},{9,8},{10,9... | collective-permute-start | bytes 393224 | tf_op jit(solution)/shard_map/ppermute | solution.py:44
  63.1 8.6 %collective-permute-start.19 = (bf16[64,1024]{1,0:T(8,128)(2,1)S(1)}, bf16[64,1024]{1,0:T(8,128)(2,1)S(1)}, u32[]{:S(2)}, u32[]{:S(2)}) collective-permute-start(bf16[64,1024]{1,0:T(8,128)(2,1)S(1)} %get-tuple-element.39.rest_0_), channel_id=1, source_target_pairs={{0,2},{1,3},{2,0},{3,1},{4,6},{5,7},{6,4},{7,5},{8,10},{9,11},{10,... | collective-permute-start | bytes 393224 | tf_op jit(solution)/shard_map/ppermute | solution.py:44
  68.4 5.5 %collective-permute-start.21 = (bf16[64,1024]{1,0:T(8,128)(2,1)S(1)}, bf16[64,1024]{1,0:T(8,128)(2,1)S(1)}, u32[]{:S(2)}, u32[]{:S(2)}) collective-permute-start(bf16[64,1024]{1,0:T(8,128)(2,1)S(1)} %collective-permute-done.20.rest_4_), channel_id=1, source_target_pairs={{0,1},{1,2},{2,3},{3,0},{4,5},{5,6},{6,7},{7,4},{8,9},{9,10},{10,1... | collective-permute-start | bytes 393224 | tf_op jit(solution)/shard_map/ppermute | solution.py:45
  69.6 6.3 %collective-permute-start.22 = (bf16[64,1024]{1,0:T(8,128)(2,1)S(1)}, bf16[64,1024]{1,0:T(8,128)(2,1)S(1)}, u32[]{:S(2)}, u32[]{:S(2)}) collective-permute-start(bf16[64,1024]{1,0:T(8,128)(2,1)S(1)} %collective-permute-done.20.rest_4_), channel_id=1, source_target_pairs={{0,3},{1,0},{2,1},{3,2},{4,7},{5,4},{6,5},{7,6},{8,11},{9,8},{10,9... | collective-permute-start | bytes 393224 | tf_op jit(solution)/shard_map/ppermute | solution.py:45
  70.4 6.9 %collective-permute-start.23 = (bf16[64,1024]{1,0:T(8,128)(2,1)S(1)}, bf16[64,1024]{1,0:T(8,128)(2,1)S(1)}, u32[]{:S(2)}, u32[]{:S(2)}) collective-permute-start(bf16[64,1024]{1,0:T(8,128)(2,1)S(1)} %collective-permute-done.20.rest_4_), channel_id=1, source_target_pairs={{0,2},{1,3},{2,0},{3,1},{4,6},{5,7},{6,4},{7,5},{8,10},{9,11},{10,... | collective-permute-start | bytes 393224 | tf_op jit(solution)/shard_map/ppermute | solution.py:45
  84.4 4.4 %collective-permute-start.24 = (bf16[66,64,128]{2,1,0:T(8,128)(2,1)S(1)}, bf16[66,64,128]{2,1,0:T(8,128)(2,1)S(1)}, u32[]{:S(2)}, u32[]{:S(2)}) collective-permute-start(bf16[66,64,128]{2,1,0:T(8,128)(2,1)S(1)} %get-tuple-element.51), channel_id=1, source_target_pairs={{0,8},{8,0},{16,24},{24,16},{32,40},{40,32},{48,56},{56,48},{64,72... | collective-permute-start | bytes 3244040 | tf_op jit(solution)/shard_map/ppermute | solution.py:39
  85.3 15.7 %collective-permute-start.26 = (bf16[33,64,128]{2,1,0:T(8,128)(2,1)S(1)}, bf16[33,64,128]{2,1,0:T(8,128)(2,1)S(1)}, u32[]{:S(2)}, u32[]{:S(2)}) collective-permute-start(bf16[33,64,128]{2,1,0:T(8,128)(2,1)S(1)} %get-tuple-element.53._), channel_id=1, source_target_pairs={{0,64},{8,72},{16,80},{24,88},{32,96},{40,104},{48,112},{56,120},{... | collective-permute-start | bytes 1622024 | tf_op jit(solution)/shard_map/ppermute | solution.py:39
  86.8 14.2 %collective-permute-start.27 = (bf16[33,64,128]{2,1,0:T(8,128)(2,1)S(1)}, bf16[33,64,128]{2,1,0:T(8,128)(2,1)S(1)}, u32[]{:S(2)}, u32[]{:S(2)}) collective-permute-start(bf16[33,64,128]{2,1,0:T(8,128)(2,1)S(1)} %get-tuple-element.55), channel_id=1, source_target_pairs={{0,192},{8,200},{16,208},{24,216},{32,224},{40,232},{48,240},{56,2... | collective-permute-start | bytes 1622024 | tf_op jit(solution)/shard_map/ppermute | solution.py:39
  89.1 16.0 %collective-permute-start.31 = (bf16[9,64,128]{2,1,0:T(8,128)(2,1)S(1)}, bf16[9,64,128]{2,1,0:T(8,128)(2,1)S(1)}, u32[]{:S(2)}, u32[]{:S(2)}) collective-permute-start(bf16[9,64,128]{2,1,0:T(8,128)(2,1)S(1)} %get-tuple-element.61), channel_id=1, source_target_pairs={{0,16},{8,24},{16,32},{24,40},{32,48},{40,56},{48,0},{56,8},{64,80... | collective-permute-start | bytes 442376 | tf_op jit(solution)/shard_map/ppermute | solution.py:39
  89.1 16.0 %collective-permute-start.32 = (bf16[9,64,128]{2,1,0:T(8,128)(2,1)S(1)}, bf16[9,64,128]{2,1,0:T(8,128)(2,1)S(1)}, u32[]{:S(2)}, u32[]{:S(2)}) collective-permute-start(bf16[9,64,128]{2,1,0:T(8,128)(2,1)S(1)} %get-tuple-element.62), channel_id=1, source_target_pairs={{0,48},{8,56},{16,0},{24,8},{32,16},{40,24},{48,32},{56,40},{64,11... | collective-permute-start | bytes 442376 | tf_op jit(solution)/shard_map/ppermute | solution.py:39
  93.0 12.1 %collective-permute-start.33 = (bf16[9,64,128]{2,1,0:T(8,128)(2,1)S(1)}, bf16[9,64,128]{2,1,0:T(8,128)(2,1)S(1)}, u32[]{:S(2)}, u32[]{:S(2)}) collective-permute-start(bf16[9,64,128]{2,1,0:T(8,128)(2,1)S(1)} %get-tuple-element.63), channel_id=1, source_target_pairs={{0,32},{8,40},{16,48},{24,56},{32,0},{40,8},{48,16},{56,24},{64,96... | collective-permute-start | bytes 442376 | tf_op jit(solution)/shard_map/ppermute | solution.py:39
  101.2 8.7 %collective-permute-start.28 = (bf16[9,64,128]{2,1,0:T(8,128)(2,1)S(1)}, bf16[9,64,128]{2,1,0:T(8,128)(2,1)S(1)}, u32[]{:S(2)}, u32[]{:S(2)}) collective-permute-start(bf16[9,64,128]{2,1,0:T(8,128)(2,1)S(1)} %get-tuple-element.57), channel_id=1, source_target_pairs={{0,16},{8,24},{16,32},{24,40},{32,48},{40,56},{48,0},{56,8},{64,80... | collective-permute-start | bytes 442376 | tf_op jit(solution)/shard_map/ppermute | solution.py:39
  101.3 11.0 %collective-permute-start.29 = (bf16[9,64,128]{2,1,0:T(8,128)(2,1)S(1)}, bf16[9,64,128]{2,1,0:T(8,128)(2,1)S(1)}, u32[]{:S(2)}, u32[]{:S(2)}) collective-permute-start(bf16[9,64,128]{2,1,0:T(8,128)(2,1)S(1)} %get-tuple-element.58), channel_id=1, source_target_pairs={{0,48},{8,56},{16,0},{24,8},{32,16},{40,24},{48,32},{56,40},{64,11... | collective-permute-start | bytes 442376 | tf_op jit(solution)/shard_map/ppermute | solution.py:39
  105.1 10.8 %collective-permute-start.30 = (bf16[9,64,128]{2,1,0:T(8,128)(2,1)S(1)}, bf16[9,64,128]{2,1,0:T(8,128)(2,1)S(1)}, u32[]{:S(2)}, u32[]{:S(2)}) collective-permute-start(bf16[9,64,128]{2,1,0:T(8,128)(2,1)S(1)} %get-tuple-element.59), channel_id=1, source_target_pairs={{0,32},{8,40},{16,48},{24,56},{32,0},{40,8},{48,16},{56,24},{64,96... | collective-permute-start | bytes 442376 | tf_op jit(solution)/shard_map/ppermute | solution.py:39
  109.9 6.7 %collective-permute-start.34 = (bf16[9,64,128]{2,1,0:T(8,128)(2,1)S(1)}, bf16[9,64,128]{2,1,0:T(8,128)(2,1)S(1)}, u32[]{:S(2)}, u32[]{:S(2)}) collective-permute-start(bf16[9,64,128]{2,1,0:T(8,128)(2,1)S(1)} %sum_far.1), channel_id=1, source_target_pairs={{0,128},{8,136},{16,144},{24,152},{32,160},{40,168},{48,176},{56,1... | collective-permute-start | bytes 442376 | tf_op jit(solution)/shard_map/ppermute | solution.py:39
  (12 other events, 159.3 us)
